TPU v7x, 32 devices: a whole 2x2x4 slice. The times are simulated.
32 devices in a mesh: dp: 16 (over z, y, core), tensor: 2 (over x).
Axes of the slice: x: 2, y: 2, z: 4, core: 2. Of those that a mesh axis runs over, the one named last changes fastest.
Arguments:
- hidden: bfloat16 [16384, 1536], P(('dp', 'tensor')), may hold values from -6 to 6
- pre_gain: float32 [2, 1536], replicated, may hold values from 0.25 to 1.75
- w_zx: bfloat16 [2, 1536, 2, 3072], P(None, 'dp', None, 'tensor'), may hold values from -0.15625 to 0.15625
- w_bc: bfloat16 [2, 1536, 256], P(None, 'dp'), may hold values from -0.15625 to 0.15625
- w_dt: bfloat16 [2, 1536, 48], P(None, 'dp', 'tensor'), may hold values from -0.15625 to 0.15625
- conv_x: float32 [2, 4, 3072], P(None, None, 'tensor'), may hold values from -3 to 3
- conv_x_bias: float32 [2, 3072], P(None, 'tensor'), may hold values from -3 to 3
- conv_bc: float32 [2, 4, 256], replicated, may hold values from -3 to 3
- conv_bc_bias: float32 [2, 256], replicated, may hold values from -3 to 3
- dt_bias: float32 [2, 48], P(None, 'tensor'), may hold values from -6 to -2
- a_log: float32 [2, 48], P(None, 'tensor'), may hold values from -1 to 2.77
- d_skip: float32 [2, 48], P(None, 'tensor'), may hold values from 0.5 to 2
- norm_gain: float32 [2, 3072], P(None, 'tensor'), may hold values from 0.25 to 1.75
- w_out: bfloat16 [2, 3072, 1536], P(None, 'tensor', 'dp'), may hold values from -0.109375 to 0.109375
- cotangent: bfloat16 [16384, 1536], P(('dp', 'tensor')), may hold values from -6 to 6
Outputs:
- hidden_out: float32 [16384, 1536], P(('dp', 'tensor'))
- grad_hidden: float32 [16384, 1536], P(('dp', 'tensor'))
- grad_pre_gain: float32 [2, 1536], replicated
- grad_w_zx: float32 [2, 1536, 2, 3072], P(None, 'dp', None, 'tensor')
- grad_w_bc: float32 [2, 1536, 256], P(None, 'dp')
- grad_w_dt: float32 [2, 1536, 48], P(None, 'dp', 'tensor')
- grad_conv_x: float32 [2, 4, 3072], P(None, None, 'tensor')
- grad_conv_x_bias: float32 [2, 3072], P(None, 'tensor')
- grad_conv_bc: float32 [2, 4, 256], replicated
- grad_conv_bc_bias: float32 [2, 256], replicated
- grad_dt_bias: float32 [2, 48], P(None, 'tensor')
- grad_a_log: float32 [2, 48], P(None, 'tensor')
- grad_d_skip: float32 [2, 48], P(None, 'tensor')
- grad_norm_gain: float32 [2, 3072], P(None, 'tensor')
- grad_w_out: float32 [2, 3072, 1536], P(None, 'tensor', 'dp')
All inputs are finite; a program needn't handle non-finite values.
Results may differ from a plain program's by a relative error of at most 0.009.
Values may be sent and summed in bfloat16 or wider, within the bound.
No kernel may reach another device: no remote copies, remote signals or barrier semaphores. Data moves between devices by JAX's collectives and lax.ppermute only.
A program may use at most 320 MiB of HBM per device.

v0:
```python
import jax
import jax.numpy as jnp
from jax import lax
from jax.sharding import PartitionSpec as P

HEADDIM = 64
BLOCK = 256
LAYERS = 2
INNER = 3072


epsilon = 1e-05
highest = lax.Precision.HIGHEST


def causal_conv(values, taps, offset):
    tap_count = taps.shape[0]
    padded = jnp.pad(values, ((tap_count - 1, 0), (0, 0)))
    result = jnp.zeros_like(values) + offset[None, :]
    for position in range(tap_count):
        result = result + taps[position][None, :] * padded[position : position + values.shape[0]]
    return result


def ssd_block(carried_state, block_inputs):
    x_heads, step_sizes, decay_rates, b_part, c_part = block_inputs
    rows_here = x_heads.shape[0]
    cumulative = jnp.cumsum(decay_rates, axis=0)
    causal_mask = (jnp.arange(rows_here)[:, None] >= jnp.arange(rows_here)[None, :]).astype(
        cumulative.dtype
    )
    across = jnp.transpose(cumulative)
    spread = across[:, :, None] - across[:, None, :]
    kernel = jnp.exp(jnp.where(causal_mask[None] > 0.5, spread, 0.0)) * causal_mask[None]
    matches = jnp.dot(c_part, jnp.transpose(b_part), precision=highest)
    driven = x_heads * step_sizes[:, :, None]
    within = jnp.einsum("hij,jhp->ihp", kernel * matches[None], driven, precision=highest)
    carried_out = (
        jnp.einsum("is,hps->ihp", c_part, carried_state, precision=highest)
        * jnp.exp(cumulative)[:, :, None]
    )
    remaining = jnp.exp(cumulative[-1][None, :] - cumulative)
    next_state = carried_state * jnp.exp(cumulative[-1])[:, None, None] + jnp.einsum(
        "jhp,js->hps", driven * remaining[:, :, None], b_part, precision=highest
    )
    return (next_state, within + carried_out)


def ssd_scan(x_heads, step_sizes, decay_rates, b_part, c_part):
    blocks = x_heads.shape[0] // BLOCK

    def split_rows(array):
        return array.reshape((blocks, BLOCK) + array.shape[1:])

    initial = jnp.zeros((x_heads.shape[1], x_heads.shape[2], b_part.shape[1]), x_heads.dtype)
    final_state, outputs = lax.scan(
        jax.checkpoint(ssd_block),
        initial,
        (
            split_rows(x_heads),
            split_rows(step_sizes),
            split_rows(decay_rates),
            split_rows(b_part),
            split_rows(c_part),
        ),
    )
    return outputs.reshape(x_heads.shape)


def local_scan(x_pre, dt_pre, b_part, c_part, conv_taps, conv_offset, dt_offset, log_rate):
    x_conv = jax.nn.silu(causal_conv(x_pre, conv_taps, conv_offset))
    step_sizes = jax.nn.softplus(dt_pre + dt_offset[None, :])
    decay_rates = -step_sizes * jnp.exp(log_rate)[None, :]
    x_heads = x_conv.reshape(x_conv.shape[0], -1, HEADDIM)
    within = ssd_scan(x_heads, step_sizes, decay_rates, b_part, c_part)
    return (x_heads, within)


def finish(within, x_heads, gate_pre, skip_gain):
    mixed = within + skip_gain[None, :, None] * x_heads
    return mixed.reshape(gate_pre.shape) * jax.nn.silu(gate_pre)


def state_inputs(bc_pre, taps, offset):
    both_parts = jax.nn.silu(causal_conv(bc_pre, taps, offset))
    state_width = both_parts.shape[1] // 2
    return (both_parts[:, :state_width], both_parts[:, state_width:])


def prenorm(current, gain_row):
    return (
        current
        * lax.rsqrt(jnp.mean(current * current, axis=-1, keepdims=True) + epsilon)
        * gain_row[None, :]
    )


def right_product(left, right_matrix):
    return lax.dot_general(
        left, right_matrix, (((1,), (1,)), ((), ())), preferred_element_type=jnp.float32
    )


def row_product(left, right_matrix):
    return lax.dot_general(
        left, right_matrix, (((0,), (0,)), ((), ())), preferred_element_type=jnp.float32
    )


def stack_member(layer_terms, member):
    return jnp.stack([entry_terms[member] for entry_terms in layer_terms])


def fetch_weights(w_zx, w_bc, w_dt, w_out, layer_index):
    return (
        lax.all_gather(w_zx[layer_index], "dp", axis=0, tiled=True),
        lax.all_gather(w_bc[layer_index], "dp", axis=0, tiled=True),
        lax.all_gather(w_dt[layer_index], "dp", axis=0, tiled=True),
        lax.all_gather(w_out[layer_index], "dp", axis=1, tiled=True),
    )


def local(
    hidden,
    pre_gain,
    w_zx,
    w_bc,
    w_dt,
    conv_x,
    conv_x_bias,
    conv_bc,
    conv_bc_bias,
    dt_bias,
    a_log,
    d_skip,
    norm_gain,
    w_out,
    cotangent,
):
    rows_local = hidden.shape[0]
    tensor_index = lax.axis_index("tensor")
    tensor_count = lax.axis_size("tensor")
    current = hidden.astype(jnp.float32)
    saved = []
    for layer_index in range(LAYERS):
        gathered = fetch_weights(w_zx, w_bc, w_dt, w_out, layer_index)
        zx_full, bc_full, dt_full, out_full = gathered
        normed_float, norm_pull = jax.vjp(prenorm, current, pre_gain[layer_index])
        normed = lax.all_gather(normed_float.astype(jnp.bfloat16), "tensor", axis=0, tiled=True)
        inner_local = zx_full.shape[2]
        gate_x = jnp.dot(
            normed, zx_full.reshape(zx_full.shape[0], -1), preferred_element_type=jnp.float32
        )
        bc_pre = jnp.dot(normed, bc_full, preferred_element_type=jnp.float32)
        dt_pre = jnp.dot(normed, dt_full, preferred_element_type=jnp.float32)
        gate_pre = gate_x[:, :inner_local]
        x_pre = gate_x[:, inner_local:]
        (b_part, c_part), state_pull = jax.vjp(
            state_inputs, bc_pre, conv_bc[layer_index], conv_bc_bias[layer_index]
        )
        (x_heads, within), scan_pull = jax.vjp(
            local_scan,
            x_pre,
            dt_pre,
            b_part,
            c_part,
            conv_x[layer_index],
            conv_x_bias[layer_index],
            dt_bias[layer_index],
            a_log[layer_index],
        )
        gated, finish_pull = jax.vjp(finish, within, x_heads, gate_pre, d_skip[layer_index])
        square_sum = lax.psum(jnp.sum(gated * gated, axis=1), "tensor")
        inv_rms = lax.rsqrt(square_sum[:, None] / INNER + epsilon)
        shaped = (gated * inv_rms * norm_gain[layer_index][None, :]).astype(jnp.bfloat16)
        out_terms = jnp.dot(shaped, out_full, preferred_element_type=jnp.float32)
        saved.append(
            (normed, shaped, gated, inv_rms, finish_pull, scan_pull, state_pull, norm_pull)
        )
        current = current + lax.psum_scatter(out_terms, "tensor", scatter_dimension=0, tiled=True)
    grad_rows = cotangent.astype(jnp.float32)
    big_grads = [None] * LAYERS
    small_terms = [None] * LAYERS
    for layer_index in reversed(range(LAYERS)):
        normed, shaped, gated, inv_rms, finish_pull, scan_pull, state_pull, norm_pull = saved[
            layer_index
        ]
        zx_full, bc_full, dt_full, out_full = fetch_weights(w_zx, w_bc, w_dt, w_out, layer_index)
        zx_flat = zx_full.reshape(zx_full.shape[0], -1)
        out_grad = lax.all_gather(grad_rows.astype(jnp.bfloat16), "tensor", axis=0, tiled=True)
        grad_out_weight = row_product(shaped, out_grad)
        shaped_grad = right_product(out_grad, out_full)
        grad_norm_gain = jnp.sum(shaped_grad * gated * inv_rms, axis=0)
        weighted = shaped_grad * norm_gain[layer_index][None, :]
        row_dot = lax.psum(jnp.sum(weighted * gated, axis=1), "tensor")
        grad_gated = weighted * inv_rms - gated * (inv_rms * inv_rms * inv_rms) * (
            row_dot[:, None] / INNER
        )
        grad_within, grad_heads, grad_gate, grad_skip = finish_pull(grad_gated)
        grad_x, grad_dt, grad_b, grad_c, grad_taps, grad_offset, grad_dt_bias, grad_log_rate = (
            scan_pull((grad_heads, grad_within))
        )
        grad_b, grad_c = lax.psum((grad_b, grad_c), "tensor")
        grad_bc_pre, grad_bc_taps, grad_bc_offset = state_pull((grad_b, grad_c))
        low_gate_x = jnp.concatenate([grad_gate, grad_x], axis=1).astype(jnp.bfloat16)
        low_dt = grad_dt.astype(jnp.bfloat16)
        low_bc = grad_bc_pre.astype(jnp.bfloat16)
        back_terms = right_product(low_gate_x, zx_flat) + right_product(low_dt, dt_full)
        own_rows = lax.dynamic_slice_in_dim(low_bc, tensor_index * rows_local, rows_local, 0)
        normed_grad = lax.psum_scatter(
            back_terms, "tensor", scatter_dimension=0, tiled=True
        ) + right_product(own_rows, bc_full)
        grad_zx_weight = row_product(normed, low_gate_x).reshape(zx_full.shape)
        grad_bc_weight = row_product(normed, low_bc)
        grad_dt_weight = row_product(normed, low_dt)
        big_grads[layer_index] = (
            lax.psum_scatter(grad_zx_weight, "dp", scatter_dimension=0, tiled=True),
            lax.psum_scatter(grad_bc_weight, "dp", scatter_dimension=0, tiled=True),
            lax.psum_scatter(grad_dt_weight, "dp", scatter_dimension=0, tiled=True),
            lax.psum_scatter(grad_out_weight, "dp", scatter_dimension=1, tiled=True),
        )
        grad_norm_in, grad_pre = norm_pull(normed_grad)
        grad_rows = grad_rows + grad_norm_in
        small_terms[layer_index] = (
            grad_pre,
            grad_taps,
            grad_offset,
            grad_bc_taps,
            grad_bc_offset,
            grad_dt_bias,
            grad_log_rate,
            grad_skip,
            grad_norm_gain,
        )
    first_tensor = (tensor_index == 0).astype(jnp.float32)

    def place_share(local_grad):
        width_here = local_grad.shape[-1]
        full_grad = jnp.zeros(local_grad.shape[:-1] + (width_here * tensor_count,), jnp.float32)
        return lax.dynamic_update_slice_in_dim(
            full_grad, local_grad, tensor_index * width_here, full_grad.ndim - 1
        )

    def own_share(summed_grad, width_here):
        return lax.dynamic_slice_in_dim(
            summed_grad, tensor_index * width_here, width_here, summed_grad.ndim - 1
        )

    local_taps = stack_member(small_terms, 1)
    local_offset = stack_member(small_terms, 2)
    local_dt = stack_member(small_terms, 5)
    local_rate = stack_member(small_terms, 6)
    local_skip = stack_member(small_terms, 7)
    local_gain = stack_member(small_terms, 8)
    summed = lax.psum(
        (
            stack_member(small_terms, 0),
            place_share(local_taps),
            place_share(local_offset),
            stack_member(small_terms, 3) * first_tensor,
            stack_member(small_terms, 4) * first_tensor,
            place_share(local_dt),
            place_share(local_rate),
            place_share(local_skip),
            place_share(local_gain),
        ),
        ("dp", "tensor"),
    )
    grad_pre_gain = summed[0]
    grad_conv_x = own_share(summed[1], local_taps.shape[-1])
    grad_conv_x_bias = own_share(summed[2], local_offset.shape[-1])
    grad_conv_bc = summed[3]
    grad_conv_bc_bias = summed[4]
    grad_dt_bias = own_share(summed[5], local_dt.shape[-1])
    grad_a_log = own_share(summed[6], local_rate.shape[-1])
    grad_d_skip = own_share(summed[7], local_skip.shape[-1])
    grad_norm_gain = own_share(summed[8], local_gain.shape[-1])
    grad_w_zx = stack_member(big_grads, 0)
    grad_w_bc = stack_member(big_grads, 1)
    grad_w_dt = stack_member(big_grads, 2)
    grad_w_out = stack_member(big_grads, 3)
    return (
        current,
        grad_rows,
        grad_pre_gain,
        grad_w_zx,
        grad_w_bc,
        grad_w_dt,
        grad_conv_x,
        grad_conv_x_bias,
        grad_conv_bc,
        grad_conv_bc_bias,
        grad_dt_bias,
        grad_a_log,
        grad_d_skip,
        grad_norm_gain,
        grad_w_out,
    )


def solution(mesh):
    return jax.shard_map(
        local,
        mesh=mesh,
        in_specs=(
            P(("dp", "tensor"), None),
            P(),
            P(None, "dp", None, "tensor"),
            P(None, "dp", None),
            P(None, "dp", "tensor"),
            P(None, None, "tensor"),
            P(None, "tensor"),
            P(),
            P(),
            P(None, "tensor"),
            P(None, "tensor"),
            P(None, "tensor"),
            P(None, "tensor"),
            P(None, "tensor", "dp"),
            P(("dp", "tensor"), None),
        ),
        out_specs=(
            P(("dp", "tensor"), None),
            P(("dp", "tensor"), None),
            P(),
            P(None, "dp", None, "tensor"),
            P(None, "dp", None),
            P(None, "dp", "tensor"),
            P(None, None, "tensor"),
            P(None, "tensor"),
            P(),
            P(),
            P(None, "tensor"),
            P(None, "tensor"),
            P(None, "tensor"),
            P(None, "tensor"),
            P(None, "tensor", "dp"),
        ),
        check_vma=False,
    )
```

profile of v0, /device:TPU:0, one launch (start us, length us, event | category | flops | bytes accessed | tf_op | source)
XLA Modules:
  0.0 3110.5 jit_solution(16658787345059235335)
XLA Ops:
  16.3 25.5 all-gather.2
  42.1 19.9 all-gather
  71.8 73.5 %all-gather.25.cloned.1.call-done = bf16[1,1536,2,1536]{3,2,0,1:T(2,128)(2,1)} async-done(((bf16[1,96,2,1536]{3,2,0,1:T(2,128)(2,1)}), bf16[1,1536,2,1536]{3,2,0,1:T(2,128)(2,1)}) %all-gather.25.cloned.1.call-update) | async-done | bytes 9437200 | tf_op jit(solution)/shard_map/all_gather | solution.py:116
  155.1 16.1 fusion.306
  181.2 10.0 reshape.958
  191.3 9.9 copy.285
  206.5 80.9 %while.82 = (s32[]{:T(128)}, f32[24,64,128]{2,1,0:T(8,128)S(1)}, f32[4,256,24,64]{1,3,2,0:T(8,128)}, f32[4,24,64,128]{3,2,1,0:T(8,128)}, f32[4,256,24]{1,2,0:T(8...) while((s32[]{:T(128)}, f32[24,64,128]{2,1,0:T(8,128)S(1)}, ...), condition=%wide.region_4.6_spmd.clone, body=%wide.region_1.5_spmd.clone.sunk | while | flops 2526752768 | bytes 13884213 | solution.py:56
  297.2 11.1 reshape.946
  308.3 9.8 multiply_reduce_fusion.27
  323.7 10.7 fusion.222
  335.2 74.7 %reduce-scatter.15.cloned.1.call-done = f32[512,1536]{1,0:T(8,128)} async-done(((f32[1024,1536]{1,0:T(8,128)}), f32[512,1536]{1,0:T(8,128)}) %reduce-scatter.15.cloned.1.call-update) | async-done | bytes 3145744 | tf_op jit(solution)/shard_map/reduce_scatter | solution.py:180
  417.0 28.0 all-gather.6
  445.1 21.9 all-gather.4
  467.6 32.6 %all-gather.29.cloned.1.call-done = bf16[1,1536,2,1536]{3,2,0,1:T(2,128)(2,1)} async-done(((bf16[1,96,2,1536]{3,2,0,1:T(2,128)(2,1)}), bf16[1,1536,2,1536]{3,2,0,1:T(2,128)(2,1)}) %all-gather.29.cloned.1.call-update) | async-done | bytes 9437200 | tf_op jit(solution)/shard_map/all_gather | solution.py:116
  500.1 10.4 copy.445
  510.5 35.7 %all-gather.19.cloned.1.call-done = bf16[1024,1536]{1,0:T(8,128)(2,1)} async-done(((bf16[512,1536]{1,0:T(8,128)(2,1)}), bf16[1024,1536]{1,0:T(8,128)(2,1)}) %all-gather.19.cloned.1.call-update) | async-done | bytes 3145744 | tf_op jit(solution)/shard_map/all_gather | solution.py:149
  546.2 16.0 fusion.307
  572.2 10.0 reshape.959
  606.1 80.7 %while.83 = (s32[]{:T(128)}, f32[24,64,128]{2,1,0:T(8,128)S(1)}, f32[4,256,24,64]{1,3,2,0:T(8,128)}, f32[4,24,64,128]{3,2,1,0:T(8,128)}, f32[4,256,24]{1,2,0:T(8...) while((s32[]{:T(128)}, f32[24,64,128]{2,1,0:T(8,128)S(1)}, ...), condition=%wide.region_12.14_spmd.clone, body=%wide.region_9.13_spmd.clone.sunk | while | flops 2526752768 | bytes 13884213 | solution.py:56
  686.9 9.8 copy.317
  696.7 11.1 reshape.947
  707.9 10.0 multiply_reduce_fusion.26
  722.9 11.6 multiply_reduce_fusion.12
  739.9 17.2 multiply_reduce_fusion.14
  757.0 10.0 reshape.948
  783.3 205.2 %while.84 = (s32[]{:T(128)}, f32[24,64,128]{2,1,0:T(8,128)}, f32[4,256,24,64]{1,3,2,0:T(8,128)}, f32[4,256,24]{1,0,2:T(4,128)}, f32[4,256,24]{1,0,2:T(4,128)}, /...) while((s32[]{:T(128)}, f32[24,64,128]{2,1,0:T(8,128)}, ...), condition=%wide.region_31.33_spmd.clone, body=%wide.region_18.32_spmd.clone.sunk | while | flops 5770125312 | bytes 51068740 | solution.py:56
  803.4 10.9 fusion.471
  854.9 10.9 fusion.471
  906.3 10.9 fusion.471
  957.8 10.9 fusion.471
  990.8 9.9 copy.320
  1000.7 11.1 reshape.949
  1011.9 17.2 multiply_reduce_fusion.18
  1041.8 13.6 fusion.227
  1067.4 71.0 %reduce-scatter.19.cloned.1.call-done = f32[512,1536]{1,0:T(8,128)} async-done(((f32[1024,1536]{1,0:T(8,128)}), f32[512,1536]{1,0:T(8,128)}) %reduce-scatter.19.cloned.1.call-update) | async-done | bytes 3145744 | tf_op jit(solution)/shard_map/reduce_scatter | solution.py:210
  1146.3 45.0 %all-gather.23.cloned.1.call-done = bf16[1024,1536]{1,0:T(8,128)(2,1)} async-done(((bf16[512,1536]{1,0:T(8,128)(2,1)}), bf16[1024,1536]{1,0:T(8,128)(2,1)}) %all-gather.23.cloned.1.call-update) | async-done | bytes 3145744 | tf_op jit(solution)/shard_map/all_gather | solution.py:190
  1191.3 11.5 multiply_reduce_fusion.13
  1207.7 17.2 multiply_reduce_fusion.15
  1224.9 10.0 reshape.950
  1251.1 205.3 %while.85 = (s32[]{:T(128)}, f32[24,64,128]{2,1,0:T(8,128)}, f32[4,256,24,64]{1,3,2,0:T(8,128)}, f32[4,256,24]{1,0,2:T(4,128)}, f32[4,256,24]{1,0,2:T(4,128)}, /...) while((s32[]{:T(128)}, f32[24,64,128]{2,1,0:T(8,128)}, ...), condition=%wide.region_51.53_spmd.clone, body=%wide.region_38.52_spmd.clone.sunk | while | flops 5770125312 | bytes 51068740 | solution.py:56
  1271.5 10.9 fusion.498
  1322.9 10.9 fusion.498
  1374.4 10.9 fusion.498
  1425.9 10.9 fusion.498
  1466.2 11.1 reshape.951
  1477.4 18.9 multiply_reduce_fusion.22
  1507.3 14.5 fusion.225
  1529.8 16.3 fusion.226
  1546.0 25.0 reshape.885
  1587.4 16.3 fusion.224
  1603.7 24.5 reshape.884
  1628.9 10.7 fusion.218
  1648.1 11.1 fusion.283
  1661.1 10.8 fusion.282
  1678.3 331.0 %all-reduce.62.cloned.1.call-done = f32[1536,2,1536]{2,1,0:T(2,128)} async-done(((f32[1536,2,1536]{2,1,0:T(2,128)}), f32[1536,2,1536]{2,1,0:T(2,128)}) %all-reduce.62.cloned.1.call-update) | async-done | bytes 18874384
  2011.6 125.3 %all-reduce.54.cloned.1.call-done = f32[2,4,3072]{2,1,0:T(4,128)} async-done(((f32[2,4,3072]{2,1,0:T(4,128)}), f32[2,4,3072]{2,1,0:T(4,128)}) %all-reduce.54.cloned.1.call-update) | async-done | bytes 98320 | tf_op jit(solution)/shard_map/psum | solution.py:255
  2138.3 59.8 %reduce-scatter.31.cloned.1.call-done = f32[96,24]{1,0:T(8,128)} async-done(((f32[1536,24]{1,0:T(8,128)}), f32[96,24]{1,0:T(8,128)}) %reduce-scatter.31.cloned.1.call-update) | async-done | bytes 9232
  2199.7 61.1 %reduce-scatter.25.cloned.1.call-done = f32[96,256]{1,0:T(8,128)} async-done(((f32[1536,256]{1,0:T(8,128)}), f32[96,256]{1,0:T(8,128)}) %reduce-scatter.25.cloned.1.call-update) | async-done | bytes 98320 | tf_op jit(solution)/shard_map/reduce_scatter | solution.py:218
  2260.7 62.6 %reduce-scatter.23.cloned.1.call-done = f32[96,256]{1,0:T(8,128)} async-done(((f32[1536,256]{1,0:T(8,128)}), f32[96,256]{1,0:T(8,128)}) %reduce-scatter.23.cloned.1.call-update) | async-done | bytes 98320 | tf_op jit(solution)/shard_map/reduce_scatter | solution.py:218
  2325.0 330.2 %all-reduce.60.cloned.1.call-done = f32[1536,2,1536]{2,1,0:T(2,128)} async-done(((f32[1536,2,1536]{2,1,0:T(2,128)}), f32[1536,2,1536]{2,1,0:T(2,128)}) %all-reduce.60.cloned.1.call-update) | async-done | bytes 18874384
  2660.3 74.4 %reduce-scatter.17.cloned.1.call-done = f32[512,1536]{1,0:T(8,128)} async-done(((f32[1024,1536]{1,0:T(8,128)}), f32[512,1536]{1,0:T(8,128)}) %reduce-scatter.17.cloned.1.call-update) | async-done | bytes 3145744 | tf_op jit(solution)/shard_map/reduce_scatter | solution.py:180
  2742.0 122.2 %all-reduce.64.cloned.1.call-done = (f32[2,1536]{1,0:T(2,128)}, f32[2,3072]{1,0:T(2,128)}, f32[2,4,256]{2,1,0:T(4,128)}, f32[2,256]{1,0:T(2,128)}, f32[2,48]{1,0...) async-done(((f32[2,1536]{1,0:T(2,128)}, f32[2,3072]{1,0:T(2,128)}, f32[2,4,256]{2,1,0:T(4,128)}, f32[2,256]{1,0:T(2,128)}, f32[2,48]{1,0:T(2,128)}, ...) | async-done | bytes 72848 | tf_op jit(solution)/shard_map/psum | solution.py:255
  2870.6 111.6 %reduce-scatter.29.cloned.1.call-done = f32[1536,96]{0,1:T(8,128)} async-done(((f32[1536,1536]{0,1:T(8,128)}), f32[1536,96]{0,1:T(8,128)}) %reduce-scatter.29.cloned.1.call-update) | async-done | bytes 589840 | tf_op jit(solution)/shard_map/reduce_scatter | solution.py:220
  2982.2 115.1 %reduce-scatter.27.cloned.1.call-done = f32[1536,96]{0,1:T(8,128)} async-done(((f32[1536,1536]{0,1:T(8,128)}), f32[1536,96]{0,1:T(8,128)}) %reduce-scatter.27.cloned.1.call-update) | async-done | bytes 589840 | tf_op jit(solution)/shard_map/reduce_scatter | solution.py:220
  (1110 shorter events, 757.9 us)
Async XLA Ops:
  7.3 34.6 %copy-start.120 = (bf16[2,96,24]{1,2,0:T(8,128)(2,1)S(1)}, bf16[2,96,24]{1,2,0:T(8,128)(2,1)}, u32[]{:S(2)}) copy-start(bf16[2,96,24]{1,2,0:T(8,128)(2,1)} %param.28) | copy-start | bytes 27652
  7.3 55.9 %all-gather.17.cloned.1.call-start = ((), (), s32[]{:S(2)}) async-start(), calls=%async_computation.10 | async-start | bytes 4718592 | tf_op jit(solution)/shard_map/all_gather | solution.py:149
  8.2 404.2 %copy-start.58 = (f32[1536]{0:T(1024)}, f32[1536]{0:T(1024)S(1)}, u32[]{:S(2)}) copy-start(f32[1536]{0:T(1024)S(1)} %get-tuple-element.1321) | copy-start | bytes 18436
  10.0 52.4 %copy-start.157 = (f32[2,24]{1,0:T(2,128)S(1)}, f32[2,24]{1,0:T(2,128)}, u32[]{:S(2)}) copy-start(f32[2,24]{1,0:T(2,128)} %param.35) | copy-start | bytes 580
  10.0 52.5 %copy-start.119 = (f32[2,1536]{1,0:T(2,128)S(1)}, f32[2,1536]{1,0:T(2,128)}, u32[]{:S(2)}) copy-start(f32[2,1536]{1,0:T(2,128)} %param.36) | copy-start | bytes 36868
  10.0 53.1 %copy-start.144 = (f32[2,24]{1,0:T(2,128)S(1)}, f32[2,24]{1,0:T(2,128)}, u32[]{:S(2)}) copy-start(f32[2,24]{1,0:T(2,128)} %param.34) | copy-start | bytes 580
  10.0 53.1 %copy-start.158 = (f32[2,24]{1,0:T(2,128)S(1)}, f32[2,24]{1,0:T(2,128)}, u32[]{:S(2)}) copy-start(f32[2,24]{1,0:T(2,128)} %param.33) | copy-start | bytes 580
  13.1 132.2 %all-gather.25.cloned.1.call-start = ((), (), s32[]{:S(2)}) async-start(), calls=%async_computation.23 | async-start | bytes 10027008 | tf_op jit(solution)/shard_map/all_gather | solution.py:116
  15.0 308.7 %all-gather.27.cloned.1.call-start = ((), (), s32[]{:S(2)}) async-start(), calls=%async_computation.24 | async-start | bytes 5013504 | tf_op jit(solution)/shard_map/all_gather | solution.py:119
  15.9 394.0 %reduce-scatter.15.cloned.1.call-start = ((), (), s32[]{:S(2)}) async-start(), calls=%async_computation.11 | async-start | bytes 9437184 | tf_op jit(solution)/shard_map/reduce_scatter | solution.py:180
  16.2 158.3 %copy-start.71 = (f32[1536]{0:T(1024)}, f32[1536]{0:T(1024)S(1)}, u32[]{:S(2)}) copy-start(f32[1536]{0:T(1024)S(1)} %get-tuple-element.1311) | copy-start | bytes 18436
  16.2 158.3 %copy-start.73 = (f32[1536]{0:T(1024)}, f32[1536]{0:T(1024)S(1)}, u32[]{:S(2)}) copy-start(f32[1536]{0:T(1024)S(1)} %get-tuple-element.1312) | copy-start | bytes 18436
  16.2 158.3 %copy-start.75 = (f32[1536]{0:T(1024)}, f32[1536]{0:T(1024)S(1)}, u32[]{:S(2)}) copy-start(f32[1536]{0:T(1024)S(1)} %get-tuple-element.1313) | copy-start | bytes 18436
  16.2 158.3 %copy-start.77 = (f32[1536]{0:T(1024)}, f32[1536]{0:T(1024)S(1)}, u32[]{:S(2)}) copy-start(f32[1536]{0:T(1024)S(1)} %get-tuple-element.1314) | copy-start | bytes 18436
  16.2 549.3 %copy-start.79 = (f32[1536]{0:T(1024)}, f32[1536]{0:T(1024)S(1)}, u32[]{:S(2)}) copy-start(f32[1536]{0:T(1024)S(1)} %get-tuple-element.1309) | copy-start | bytes 18436
  16.2 549.3 %copy-start.81 = (f32[1536]{0:T(1024)}, f32[1536]{0:T(1024)S(1)}, u32[]{:S(2)}) copy-start(f32[1536]{0:T(1024)S(1)} %get-tuple-element.1310) | copy-start | bytes 18436
  16.2 549.3 %copy-start.83 = (f32[1536]{0:T(1024)}, f32[1536]{0:T(1024)S(1)}, u32[]{:S(2)}) copy-start(f32[1536]{0:T(1024)S(1)} %get-tuple-element.1315) | copy-start | bytes 18436
  16.2 549.3 %copy-start.85 = (f32[1536]{0:T(1024)}, f32[1536]{0:T(1024)S(1)}, u32[]{:S(2)}) copy-start(f32[1536]{0:T(1024)S(1)} %get-tuple-element.1316) | copy-start | bytes 18436
  41.8 553.1 %copy-start.129 = (f32[1,1,256]{2,1,0:T(1,128)}, f32[1,1,256]{2,1,0:T(1,128)S(1)}, u32[]{:S(2)}) copy-start(f32[1,1,256]{2,1,0:T(1,128)S(1)} %get-tuple-element.1529) | copy-start | bytes 3076
  41.9 553.1 %copy-start.131 = (f32[1,1,256]{2,1,0:T(1,128)}, f32[1,1,256]{2,1,0:T(1,128)S(1)}, u32[]{:S(2)}) copy-start(f32[1,1,256]{2,1,0:T(1,128)S(1)} %get-tuple-element.1530) | copy-start | bytes 3076
  41.9 553.1 %copy-start.133 = (f32[1,1,256]{2,1,0:T(1,128)}, f32[1,1,256]{2,1,0:T(1,128)S(1)}, u32[]{:S(2)}) copy-start(f32[1,1,256]{2,1,0:T(1,128)S(1)} %get-tuple-element.1535) | copy-start | bytes 3076
  41.9 553.1 %copy-start.135 = (f32[1,1,256]{2,1,0:T(1,128)}, f32[1,1,256]{2,1,0:T(1,128)S(1)}, u32[]{:S(2)}) copy-start(f32[1,1,256]{2,1,0:T(1,128)S(1)} %get-tuple-element.1536) | copy-start | bytes 3076
  62.5 245.8 %copy-start.61 = (f32[1536]{0:T(1024)}, f32[1536]{0:T(1024)S(1)}, u32[]{:S(2)}) copy-start(f32[1536]{0:T(1024)S(1)} %mul.1532) | copy-start | bytes 18436
  63.1 260.5 %copy-start.91 = (f32[1536]{0:T(1024)}, f32[1536]{0:T(1024)S(1)}, u32[]{:S(2)}) copy-start(f32[1536]{0:T(1024)S(1)} %get-tuple-element.1318) | copy-start | bytes 18436
  63.2 534.6 %copy-start.139 = (f32[24]{0:T(128)}, f32[24]{0:T(128)S(1)}, u32[]{:S(2)}) copy-start(f32[24]{0:T(128)S(1)} %get-tuple-element.1558) | copy-start | bytes 292
  334.4 75.6 %copy-start.7 = (bf16[512,1536]{1,0:T(8,128)(2,1)S(1)}, bf16[512,1536]{1,0:T(8,128)(2,1)}, u32[]{:S(2)}) copy-start(bf16[512,1536]{1,0:T(8,128)(2,1)} %param.24) | copy-start | bytes 4718596
  334.4 165.7 %all-gather.29.cloned.1.call-start = ((), (), s32[]{:S(2)}) async-start(), calls=%async_computation.25 | async-start | bytes 10027008 | tf_op jit(solution)/shard_map/all_gather | solution.py:116
  335.0 211.2 %all-gather.19.cloned.1.call-start = ((), (), s32[]{:S(2)}) async-start(), calls=%async_computation.12 | async-start | bytes 4718592 | tf_op jit(solution)/shard_map/all_gather | solution.py:149
  412.3 98.2 %copy-start.110 = (f32[512]{0:T(512)}, f32[512]{0:T(512)S(1)}, u32[]{:S(2)}) copy-start(f32[512]{0:T(512)S(1)} %get-tuple-element.1445) | copy-start | bytes 6148
  412.4 98.2 %copy-start.87 = (f32[512]{0:T(512)}, f32[512]{0:T(512)S(1)}, u32[]{:S(2)}) copy-start(f32[512]{0:T(512)S(1)} %fusion.275) | copy-start | bytes 6148
  415.5 307.3 %all-gather.21.cloned.1.call-start = ((), (), s32[]{:S(2)}) async-start(), calls=%async_computation.14 | async-start | bytes 4718592 | tf_op jit(solution)/shard_map/all_gather | solution.py:190
  416.2 306.6 %all-gather.31.cloned.1.call-start = ((), (), s32[]{:S(2)}) async-start(), calls=%async_computation.26 | async-start | bytes 5013504 | tf_op jit(solution)/shard_map/all_gather | solution.py:119
  417.0 643.9 %all-reduce.56.cloned.1.call-start = ((), (), s32[]{:S(2)}) async-start(), calls=%async_computation.27 | async-start | bytes 2097152 | tf_op jit(solution)/shard_map/psum | solution.py:203
  445.0 146.9 %copy-start.24 = (bf16[1,1536,256]{2,1,0:T(8,128)(2,1)}, bf16[1,1536,256]{2,1,0:T(8,128)(2,1)S(1)}, u32[]{:S(2)}) copy-start(bf16[1,1536,256]{2,1,0:T(8,128)(2,1)S(1)} %all-gather.6) | copy-start | bytes 2359300
  467.4 130.4 %copy-start.34 = (bf16[1,1536,24]{1,2,0:T(8,128)(2,1)}, bf16[1,1536,24]{1,2,0:T(8,128)(2,1)S(1)}, u32[]{:S(2)}) copy-start(bf16[1,1536,24]{1,2,0:T(8,128)(2,1)S(1)} %copy.290) | copy-start | bytes 221188
  467.6 272.3 %copy-start.64 = (f32[1536]{0:T(1024)}, f32[1536]{0:T(1024)S(1)}, u32[]{:S(2)}) copy-start(f32[1536]{0:T(1024)S(1)} %mul.1580) | copy-start | bytes 18436
  990.8 147.6 %reduce-scatter.19.cloned.1.call-start = ((), (), s32[]{:S(2)}) async-start(), calls=%async_computation.15 | async-start | bytes 9437184 | tf_op jit(solution)/shard_map/reduce_scatter | solution.py:210
  1060.6 130.7 %all-gather.23.cloned.1.call-start = ((), (), s32[]{:S(2)}) async-start(), calls=%async_computation.16 | async-start | bytes 4718592 | tf_op jit(solution)/shard_map/all_gather | solution.py:190
  1060.9 77.5 %copy-start.3 = (f32[512,1536]{1,0:T(8,128)S(1)}, f32[512,1536]{1,0:T(8,128)}, u32[]{:S(2)}) copy-start(f32[512,1536]{1,0:T(8,128)} %copy-done.2) | copy-start | bytes 9437188
  1060.9 77.5 %copy-start.59 = (f32[1536]{0:T(1024)S(1)}, f32[1536]{0:T(1024)}, u32[]{:S(2)}) copy-start(f32[1536]{0:T(1024)} %copy-done.58) | copy-start | bytes 18436
  1060.9 77.5 %copy-start.88 = (f32[512]{0:T(512)S(1)}, f32[512]{0:T(512)}, u32[]{:S(2)}) copy-start(f32[512]{0:T(512)} %copy-done.87) | copy-start | bytes 6148
  1067.4 75.1 %copy-start.111 = (f32[512]{0:T(512)S(1)}, f32[512]{0:T(512)}, u32[]{:S(2)}) copy-start(f32[512]{0:T(512)} %copy-done.110) | copy-start | bytes 6148
  1142.4 48.9 %copy-start.92 = (f32[1536]{0:T(1024)S(1)}, f32[1536]{0:T(1024)}, u32[]{:S(2)}) copy-start(f32[1536]{0:T(1024)} %copy-done.91) | copy-start | bytes 18436
  1142.4 48.9 %copy-start.113 = (f32[1024]{0:T(1024)S(1)}, f32[1024]{0:T(1024)}, u32[]{:S(2)}) copy-start(f32[1024]{0:T(1024)} %copy-done.112) | copy-start | bytes 12292
  1146.2 433.2 %all-reduce.58.cloned.1.call-start = ((), (), s32[]{:S(2)}) async-start(), calls=%async_computation.28 | async-start | bytes 2097152 | tf_op jit(solution)/shard_map/psum | solution.py:203
  1146.3 61.4 %copy-start.62 = (f32[1536]{0:T(1024)S(1)}, f32[1536]{0:T(1024)}, u32[]{:S(2)}) copy-start(f32[1536]{0:T(1024)} %copy-done.61) | copy-start | bytes 18436
  1146.3 61.4 %copy-start.117 = (f32[1024]{0:T(1024)S(1)}, f32[1024]{0:T(1024)}, u32[]{:S(2)}) copy-start(f32[1024]{0:T(1024)} %get-tuple-element.1537) | copy-start | bytes 12292
  1497.4 145.4 %reduce-scatter.21.cloned.1.call-start = ((), (), s32[]{:S(2)}) async-start(), calls=%async_computation.17 | async-start | bytes 9437184 | tf_op jit(solution)/shard_map/reduce_scatter | solution.py:210
  1525.9 151.5 %reduce-scatter.33.cloned.1.call-start = ((), (), s32[]{:S(2)}) async-start(), calls=%async_computation.30 | async-start | bytes 835584
  1529.7 479.5 %all-reduce.62.cloned.1.call-start = ((), (), s32[]{:S(2)}) async-start(), calls=%async_computation.32 | async-start | bytes 37748736
  1571.1 565.8 %all-reduce.54.cloned.1.call-start = ((), (), s32[]{:S(2)}) async-start(), calls=%async_computation.20 | async-start | bytes 196608 | tf_op jit(solution)/shard_map/psum | solution.py:255
  1572.7 625.5 %reduce-scatter.31.cloned.1.call-start = ((), (), s32[]{:S(2)}) async-start(), calls=%async_computation.29 | async-start | bytes 835584
  1575.1 685.7 %reduce-scatter.25.cloned.1.call-start = ((), (), s32[]{:S(2)}) async-start(), calls=%async_computation.19 | async-start | bytes 1671168 | tf_op jit(solution)/shard_map/reduce_scatter | solution.py:218
  1579.4 744.0 %reduce-scatter.23.cloned.1.call-start = ((), (), s32[]{:S(2)}) async-start(), calls=%async_computation.18 | async-start | bytes 1671168 | tf_op jit(solution)/shard_map/reduce_scatter | solution.py:218
  1587.3 1067.9 %all-reduce.60.cloned.1.call-start = ((), (), s32[]{:S(2)}) async-start(), calls=%async_computation.31 | async-start | bytes 37748736
  1628.2 1106.6 %reduce-scatter.17.cloned.1.call-start = ((), (), s32[]{:S(2)}) async-start(), calls=%async_computation.13 | async-start | bytes 9437184 | tf_op jit(solution)/shard_map/reduce_scatter | solution.py:180
  1639.8 1224.4 %all-reduce.64.cloned.1.call-start = ((), (), s32[]{:S(2)}) async-start(), calls=%async_computation.33 | async-start | bytes 149504 | tf_op jit(solution)/shard_map/psum | solution.py:255
  1648.1 1334.2 %reduce-scatter.29.cloned.1.call-start = ((), (), s32[]{:S(2)}) async-start(), calls=%async_computation.22 | async-start | bytes 10027008 | tf_op jit(solution)/shard_map/reduce_scatter | solution.py:220
  1659.3 1438.1 %reduce-scatter.27.cloned.1.call-start = ((), (), s32[]{:S(2)}) async-start(), calls=%async_computation.21 | async-start | bytes 10027008 | tf_op jit(solution)/shard_map/reduce_scatter | solution.py:220
  1671.9 988.4 %copy-start.109 = (f32[512]{0:T(512)S(1)}, f32[512]{0:T(512)}, u32[]{:S(2)}) copy-start(f32[512]{0:T(512)} %copy-done.108) | copy-start | bytes 6148
  1671.9 1062.8 %copy-start.4 = (f32[512,1536]{1,0:T(8,128)S(1)}, f32[512,1536]{1,0:T(8,128)}, u32[]{:S(2)}) copy-start(f32[512,1536]{1,0:T(8,128)} %copy-done.2) | copy-start | bytes 9437188
  1672.0 1062.8 %copy-start.60 = (f32[1536]{0:T(1024)S(1)}, f32[1536]{0:T(1024)}, u32[]{:S(2)}) copy-start(f32[1536]{0:T(1024)} %copy-done.58) | copy-start | bytes 18436
  1672.0 1062.8 %copy-start.89 = (f32[512]{0:T(512)S(1)}, f32[512]{0:T(512)}, u32[]{:S(2)}) copy-start(f32[512]{0:T(512)} %copy-done.87) | copy-start | bytes 6148
  1672.0 1062.8 %copy-start.107 = (f32[512]{0:T(512)S(1)}, f32[512]{0:T(512)}, u32[]{:S(2)}) copy-start(f32[512]{0:T(512)} %copy-done.106) | copy-start | bytes 6148
  (181 other events, 1837.6 us)
Sparse Core Ops, SparseCore 0:
  13.2 47.6 all-gather.16
  63.7 81.5 all-gather.24
  148.2 51.5 all-gather.26
  334.5 75.3 reduce-scatter.14
  412.3 87.7 all-gather.28
  502.2 43.9 all-gather.18
  547.8 44.9 all-gather.20
  595.3 53.3 all-gather.30
  990.9 40.5 all-reduce.55
  1060.7 77.6 reduce-scatter.18
  1146.4 44.9 all-gather.22
  1497.5 40.0 all-reduce.57
  1539.9 77.0 reduce-scatter.20
  1620.8 56.5 reduce-scatter.32
  1681.1 328.1 all-reduce.61
  2016.2 120.6 all-reduce.53
  2140.7 57.4 reduce-scatter.30
  2202.3 58.4 reduce-scatter.24
  2264.9 58.4 reduce-scatter.22
  2327.0 328.1 all-reduce.59
  2657.6 77.1 reduce-scatter.16
  2741.8 122.3 all-reduce.63
  2868.8 113.3 reduce-scatter.28
  2986.2 111.0 reduce-scatter.26
where the time goes:
time: 3120 us; the launch traced here: 3110 us
  waiting for transfers between devices  1730 us (55%)
  matrix products  586 us (19%)
  local copies, waits for them, and re-layouts  404 us (13%)
  other arithmetic  251 us (8%)
  blocking collectives  115 us (4%)
    unnamed x28, waiting for transfers between devices  727 us
    psum x2, waiting for transfers between devices, local(): lax.psum((stack_member(small_terms, 0), place_share(local_taps), place_sh...  247 us
    reduce_scatter x2, waiting for transfers between devices, local(): lax.psum_scatter(grad_out_weight, 'dp', scatter_dimension=1, tiled=True)  227 us
    dot_general x24, matrix products, ssd_block(): jnp.einsum('hij,jhp->ihp', kernel * matches[None], driven, precision=high...  223 us
    reduce_scatter x2, waiting for transfers between devices, local(): lax.psum_scatter(out_terms, 'tensor', scatter_dimension=0, tiled=True)  149 us
    reduce_scatter x2, waiting for transfers between devices, local(): lax.psum_scatter(grad_bc_weight, 'dp', scatter_dimension=0, tiled=True)  124 us
    all_gather x2, waiting for transfers between devices, fetch_weights(): lax.all_gather(w_zx[layer_index], 'dp', axis=0, tiled=True)  106 us
    unnamed x301, local copies, waits for them, and re-layouts  79.8 us
  transfers between devices with their start and end apart: 24, of which 17 were waited for; matrix products, arithmetic and copies ran while one was open for 21% of the time, Pallas kernels for 0%

commit v1 on v0

v1 whole, which is shorter than its diff:
```python
import functools
import jax
import jax.numpy as jnp
from jax import lax
from jax.experimental import pallas as pl
from jax.experimental.pallas import tpu as pltpu
from jax.sharding import PartitionSpec as P

HEADDIM = 64
INNER = 3072
LANES = 128
Q = 128
GROUP = 256
LOG2E = 1.4426950408889634
epsilon = 1e-05
highest = lax.Precision.HIGHEST
bf16 = jnp.bfloat16
f32 = jnp.float32


def sigmoid(v):
    return 0.5 * jnp.tanh(0.5 * v) + 0.5


def mm(a, b, precision=None):
    return lax.dot_general(
        a, b, (((1,), (0,)), ((), ())), precision=precision, preferred_element_type=f32
    )


def mm_t(a, b):
    return lax.dot_general(a, b, (((1,), (1,)), ((), ())), preferred_element_type=f32)


def t_mm(a, b):
    return lax.dot_general(a, b, (((0,), (0,)), ((), ())), preferred_element_type=f32)


def iota2(shape, dim):
    return lax.broadcasted_iota(jnp.int32, shape, dim)


def split_lanes(v):
    high = v.astype(bf16).astype(f32)
    rest = v - high
    return (high + pltpu.roll(rest, 32, axis=1)).astype(bf16)


def taps_sum(ext_ref, taps_ref, bias_ref, columns):
    total = bias_ref[0:1, columns]
    for k in range(4):
        total = total + taps_ref[k : k + 1, columns] * ext_ref[5 + k : 5 + k + Q, columns]
    return total


def chunk_terms(bcdt_ref, bext_ref, bct_ref, bcb_ref, dtv_ref, head_count):
    bext_ref[8 : 8 + Q, :] = bcdt_ref[:, 0:256]
    z = taps_sum(bext_ref, bct_ref, bcb_ref, slice(0, 256))
    s = sigmoid(z)
    bc = z * s
    dsilu = s * (1.0 + z * (1.0 - s))
    b_part = bc[:, 0:128]
    c_part = bc[:, 128:256]
    pre = bcdt_ref[:, 256:384] + dtv_ref[0:1, :]
    live = iota2((Q, LANES), 1) < head_count
    step = jnp.where(live, jnp.maximum(pre, 0.0) + jnp.log1p(jnp.exp(-jnp.abs(pre))), 0.0)
    decay = step * dtv_ref[1:2, :]
    rows = iota2((Q, Q), 0)
    cols = iota2((Q, Q), 1)
    lower = rows >= cols
    cum = mm(lower.astype(f32), decay, highest)
    return b_part, c_part, dsilu, pre, live, step, decay, cum, lower


def fwd_kernel(
    zx_ref, bcdt_ref, taps_ref, chan_ref, bct_ref, bcb_ref, dtv_ref, spread_ref,
    sh_ref, mixed_ref, sin_ref, ssq_ref, ext_ref, bext_ref, state_ref, *, head_count,
):
    width = sh_ref.shape[1]

    @pl.when(pl.program_id(0) == 0)
    def _():
        ext_ref[0:8, :] = jnp.zeros((8, width), f32)
        bext_ref[0:8, :] = jnp.zeros((8, 256), f32)
        state_ref[...] = jnp.zeros_like(state_ref)

    @pl.when(pl.program_id(0) > 0)
    def _():
        ext_ref[0:8, :] = ext_ref[Q : Q + 8, :]
        bext_ref[0:8, :] = bext_ref[Q : Q + 8, :]

    b_part, c_part, _, _, live, step, decay, cum, lower = chunk_terms(
        bcdt_ref, bext_ref, bct_ref, bcb_ref, dtv_ref, head_count
    )
    cum2 = cum * LOG2E
    across = cum2.T
    last = cum2[Q - 1 : Q, :]
    bb = b_part.astype(bf16)
    cb = c_part.astype(bf16)
    bt = b_part.T.astype(bf16)
    c_both = jnp.concatenate([cb, (c_part - cb.astype(f32)).astype(bf16)], axis=1)
    scores = jnp.where(lower, mm(c_part, b_part.T, highest), 0.0)
    step_l = split_lanes(step)
    grow_l = split_lanes(jnp.where(live, jnp.exp2(cum2), 0.0))
    left_l = split_lanes(jnp.where(live, jnp.exp2(last - cum2), 0.0))
    all_l = split_lanes(jnp.where(live[0:8], jnp.exp2(jnp.broadcast_to(last, (8, LANES))), 0.0))
    half = iota2((Q, LANES), 1) < HEADDIM
    ssq = jnp.zeros((Q, LANES), f32)
    for g in range(width // GROUP):
        columns = slice(g * GROUP, (g + 1) * GROUP)
        spread = spread_ref[:, columns]
        step_e = mm(step_l, spread)
        grow_e = mm(grow_l, spread)
        left_e = mm(left_l, spread)
        all_e = mm(all_l, spread)[0:1, :]
        ext_ref[8 : 8 + Q, columns] = zx_ref[:, width + g * GROUP : width + (g + 1) * GROUP].astype(f32)
        z = taps_sum(ext_ref, taps_ref, chan_ref, columns)
        xc = z * sigmoid(z)
        v = xc * step_e
        vb = v.astype(bf16)
        vl = (v - vb.astype(f32)).astype(bf16)
        state = state_ref[:, columns]
        state_b = state.astype(bf16)
        sin_ref[0, :, columns] = state_b
        state_l = (state - state_b.astype(f32)).astype(bf16)
        y = mm(c_both, jnp.concatenate([state_b, state_b], axis=0)) + mm(cb, state_l)
        y = y * grow_e
        parts = []
        for pair in range(GROUP // LANES):
            head = (g * GROUP + pair * LANES) // HEADDIM
            lanes = slice(pair * LANES, (pair + 1) * LANES)
            vp, vq = vb[:, lanes], vl[:, lanes]
            highs, lows = [], []
            for h in (head, head + 1):
                d = cum2[:, h : h + 1] - across[h : h + 1, :]
                m = scores * jnp.exp2(-jnp.abs(d))
                mb = m.astype(bf16)
                highs.append(mb)
                lows.append((m - mb.astype(f32)).astype(bf16))
            block = [jnp.where(half, vp, 0), jnp.where(half, 0, vp)]
            block_l = [jnp.where(half, vq, 0), jnp.where(half, 0, vq)]
            parts.append(
                mm(
                    jnp.concatenate(highs + lows + highs, axis=1),
                    jnp.concatenate(block + block + block_l, axis=0),
                )
            )
        y = y + jnp.concatenate(parts, axis=1)
        state_ref[:, columns] = state * all_e + mm(bt, (v * left_e).astype(bf16))
        mixed = y + chan_ref[2:3, columns] * xc
        mixed_ref[:, columns] = mixed.astype(bf16)
        gate = zx_ref[:, columns].astype(f32)
        gated = mixed * (gate * sigmoid(gate))
        squares = gated * gated
        ssq = ssq + squares[:, 0:LANES] + squares[:, LANES : 2 * LANES]
        sh_ref[:, columns] = gated * chan_ref[1:2, columns]
    ssq_ref[...] = ssq


def bwd_kernel(
    sg_ref, zx_ref, xprev_ref, mixed_ref, sin_ref, bcdt_ref, bcprev_ref, coef_ref,
    taps_ref, chan_ref, bct_ref, bcb_ref, dtv_ref, spread_ref, gather_ref,
    low_ref, gchan_ref, gbc_ref, gdt_ref,
    ext_ref, bext_ref, dz_ref, dbz_ref, dstate_ref, colsum_ref, *, head_count,
):
    width = sg_ref.shape[1]
    step_id = pl.program_id(0)
    is_first = step_id == pl.num_programs(0) - 1

    @pl.when(step_id == 0)
    def _():
        dz_ref[Q : Q + 8, :] = jnp.zeros((8, width), f32)
        dbz_ref[Q : Q + 8, :] = jnp.zeros((8, 256), f32)
        dstate_ref[...] = jnp.zeros_like(dstate_ref)
        gchan_ref[...] = jnp.zeros_like(gchan_ref)
        gbc_ref[...] = jnp.zeros_like(gbc_ref)
        gdt_ref[...] = jnp.zeros_like(gdt_ref)
        colsum_ref[...] = jnp.zeros_like(colsum_ref)

    @pl.when(step_id > 0)
    def _():
        dz_ref[Q : Q + 8, :] = dz_ref[0:8, :]
        dbz_ref[Q : Q + 8, :] = dbz_ref[0:8, :]

    keep = jnp.where(is_first, 0.0, 1.0)
    ext_ref[0:8, :] = xprev_ref[8:16, :].astype(f32) * keep
    bext_ref[0:8, :] = bcprev_ref[:, 0:256] * keep
    b_part, c_part, bc_dsilu, dt_pre, live, step, decay, cum, lower = chunk_terms(
        bcdt_ref, bext_ref, bct_ref, bcb_ref, dtv_ref, head_count
    )
    cum2 = cum * LOG2E
    across = cum2.T
    last = cum2[Q - 1 : Q, :]
    bb = b_part.astype(bf16)
    cb = c_part.astype(bf16)
    bt = b_part.T.astype(bf16)
    ct = c_part.T.astype(bf16)
    upper = iota2((Q, Q), 0) <= iota2((Q, Q), 1)
    scores = jnp.where(lower, mm(c_part, b_part.T, highest), 0.0)
    scores_t = scores.T
    step_l = split_lanes(step)
    grow_l = split_lanes(jnp.where(live, jnp.exp2(cum2), 0.0))
    left_l = split_lanes(jnp.where(live, jnp.exp2(last - cum2), 0.0))
    all_l = split_lanes(jnp.where(live[0:8], jnp.exp2(jnp.broadcast_to(last, (8, LANES))), 0.0))
    half = iota2((Q, LANES), 1) < HEADDIM
    coef = coef_ref[:, 0:1]
    inv = coef_ref[:, 1:2]
    d_scores = jnp.zeros((Q, Q), f32)
    d_c = jnp.zeros((Q, LANES), f32)
    d_b = jnp.zeros((Q, LANES), f32)
    row_sums = jnp.zeros((Q, LANES), f32)
    red_step = jnp.zeros((Q, LANES), f32)
    red_in = jnp.zeros((Q, LANES), f32)
    red_out = jnp.zeros((Q, LANES), f32)
    red_all = jnp.zeros((8, LANES), f32)
    ones = jnp.ones((16, Q), bf16)
    pair_rows = iota2((2 * Q, LANES), 0) // Q
    pair_cols = iota2((2 * Q, LANES), 1)
    for g in range(width // GROUP):
        columns = slice(g * GROUP, (g + 1) * GROUP)
        spread = spread_ref[:, columns]
        gather = gather_ref[columns, :]
        step_e = mm(step_l, spread)
        grow_e = mm(grow_l, spread)
        left_e = mm(left_l, spread)
        all_e = mm(all_l, spread)[0:1, :]
        ext_ref[8 : 8 + Q, columns] = zx_ref[:, width + g * GROUP : width + (g + 1) * GROUP].astype(f32)
        z = taps_sum(ext_ref, taps_ref, chan_ref, columns)
        s = sigmoid(z)
        xc = z * s
        x_dsilu = s * (1.0 + z * (1.0 - s))
        gate = zx_ref[:, columns].astype(f32)
        gs = sigmoid(gate)
        act = gate * gs
        act_d = gs * (1.0 + gate * (1.0 - gs))
        mixed = mixed_ref[:, columns].astype(f32)
        gated = mixed * act
        sg = sg_ref[:, columns] * inv
        grad_gated = sg * chan_ref[1:2, columns] - gated * coef
        dy = grad_gated * act
        low_ref[:, columns] = (grad_gated * mixed * act_d).astype(bf16)
        gchan_ref[5:6, columns] += jnp.sum(sg * gated, axis=0, keepdims=True)
        gchan_ref[6:7, columns] += jnp.sum(dy * xc, axis=0, keepdims=True)
        dyb = dy.astype(bf16)
        v = xc * step_e
        vb = v.astype(bf16)
        sin = sin_ref[0, :, columns]
        ey = dy * grow_e
        eyb = ey.astype(bf16)
        inter = ey * mm(cb, sin)
        dstate = dstate_ref[:, columns]
        dstate_b = dstate.astype(bf16)
        dv_state = mm(bb, dstate_b) * left_e
        d_c = d_c + mm_t(eyb, sin)
        d_b = d_b + mm_t((v * left_e).astype(bf16), dstate_b)
        kept = jnp.sum(sin.astype(f32) * dstate, axis=0, keepdims=True) * all_e
        dstate_ref[:, columns] = dstate * all_e + mm(ct, eyb)
        parts = []
        for pair in range(GROUP // LANES):
            lanes = slice(pair * LANES, (pair + 1) * LANES)
            head = (g * GROUP + pair * LANES) // HEADDIM
            vp = vb[:, lanes]
            dp = dyb[:, lanes]
            v_block = jnp.concatenate([jnp.where(half, vp, 0), jnp.where(half, 0, vp)], axis=0)
            d_block = jnp.concatenate([jnp.where(half, dp, 0), jnp.where(half, 0, dp)], axis=0)
            dm = mm_t(dp, v_block)
            mts = []
            ws = []
            for i, h in enumerate((head, head + 1)):
                d = cum2[:, h : h + 1] - across[h : h + 1, :]
                e = jnp.exp2(-jnp.abs(d))
                dme = dm[:, i * Q : (i + 1) * Q] * e
                d_scores = d_scores + dme
                mts.append((scores_t * e).astype(bf16))
                ws.append((dme * scores).astype(bf16))
            parts.append(mm(jnp.concatenate(mts, axis=1), d_block))
            w = jnp.concatenate(ws, axis=1)
            picks = (pair_cols == head + pair_rows).astype(bf16)
            row_sums = row_sums + mm(w, picks)
            sums = mm(ones, w)
            colsum_ref[head : head + 1, :] = sums[0:1, 0:Q]
            colsum_ref[head + 1 : head + 2, :] = sums[0:1, Q : 2 * Q]
        dv = jnp.concatenate(parts, axis=1) + dv_state
        red_step = red_step + mm((dv * xc).astype(bf16), gather)
        red_in = red_in + mm(inter.astype(bf16), gather)
        red_out = red_out + mm((v * dv_state).astype(bf16), gather)
        red_all = red_all + mm(jnp.broadcast_to(kept, (8, GROUP)), gather.astype(f32), highest)
        dz = (dv * step_e + chan_ref[2:3, columns] * dy) * x_dsilu
        dz_ref[0:Q, columns] = dz
        dx = jnp.zeros((Q, GROUP), f32)
        for k in range(4):
            dx = dx + taps_ref[k : k + 1, columns] * dz_ref[3 - k : 3 - k + Q, columns]
            gchan_ref[k : k + 1, columns] += jnp.sum(
                dz * ext_ref[5 + k : 5 + k + Q, columns], axis=0, keepdims=True
            )
        gchan_ref[4:5, columns] += jnp.sum(dz, axis=0, keepdims=True)
        low_ref[:, width + g * GROUP : width + (g + 1) * GROUP] = dx.astype(bf16)
    through = row_sums - colsum_ref[...].T + red_in
    d_decay = mm(upper.astype(f32), through, highest) + mm(
        jnp.where(upper, 0.0, 1.0), red_out, highest
    ) + red_all[0:1, :]
    d_decay = jnp.where(live, d_decay, 0.0)
    d_pre = (red_step + d_decay * dtv_ref[1:2, :]) * sigmoid(dt_pre)
    d_pre = jnp.where(live, d_pre, 0.0)
    gdt_ref[0:1, :] += jnp.sum(d_pre, axis=0, keepdims=True)
    gdt_ref[1:2, :] += jnp.sum(d_decay * decay, axis=0, keepdims=True)
    low_ref[:, 2 * width + 256 : 2 * width + 384] = d_pre.astype(bf16)
    d_scores = jnp.where(lower, d_scores, 0.0)
    d_c = d_c + mm(d_scores, b_part, highest)
    d_b = d_b + mm(d_scores.T, c_part, highest)
    dbz = jnp.concatenate([d_b, d_c], axis=1) * bc_dsilu
    dbz_ref[0:Q, :] = dbz
    dbc = jnp.zeros((Q, 256), f32)
    for k in range(4):
        dbc = dbc + bct_ref[k : k + 1, :] * dbz_ref[3 - k : 3 - k + Q, :]
        gbc_ref[k : k + 1, :] += jnp.sum(
            dbz * bext_ref[5 + k : 5 + k + Q, :], axis=0, keepdims=True
        )
    gbc_ref[4:5, :] += jnp.sum(dbz, axis=0, keepdims=True)
    low_ref[:, 2 * width : 2 * width + 256] = dbc.astype(bf16)


def spread_matrix(width):
    heads = jnp.arange(width) // HEADDIM
    lanes = jnp.arange(LANES)
    return ((lanes[:, None] == heads[None, :]) | (lanes[:, None] == heads[None, :] + 32)).astype(bf16)


def gather_matrix(width):
    heads = jnp.arange(width) // HEADDIM
    return (heads[:, None] == jnp.arange(LANES)[None, :]).astype(bf16)


def whole(shape):
    return pl.BlockSpec(shape, lambda c: (0,) * len(shape))


VMEM_LIMIT = 48 * 1024 * 1024


def mixer_forward(zx, bcdt, taps, chan, bct, bcb, dtv):
    rows, width2 = zx.shape
    width = width2 // 2
    chunks = rows // Q
    return pl.pallas_call(
        functools.partial(fwd_kernel, head_count=width // HEADDIM),
        grid=(chunks,),
        in_specs=[
            pl.BlockSpec((Q, width2), lambda c: (c, 0)),
            pl.BlockSpec((Q, 384), lambda c: (c, 0)),
            whole((4, width)), whole((8, width)), whole((4, 256)), whole((1, 256)),
            whole((8, LANES)), whole((LANES, width)),
        ],
        out_specs=[
            pl.BlockSpec((Q, width), lambda c: (c, 0)),
            pl.BlockSpec((Q, width), lambda c: (c, 0)),
            pl.BlockSpec((1, LANES, width), lambda c: (c, 0, 0)),
            pl.BlockSpec((Q, LANES), lambda c: (c, 0)),
        ],
        out_shape=[
            jax.ShapeDtypeStruct((rows, width), f32),
            jax.ShapeDtypeStruct((rows, width), bf16),
            jax.ShapeDtypeStruct((chunks, LANES, width), bf16),
            jax.ShapeDtypeStruct((rows, LANES), f32),
        ],
        scratch_shapes=[
            pltpu.VMEM((Q + 8, width), f32),
            pltpu.VMEM((Q + 8, 256), f32),
            pltpu.VMEM((LANES, width), f32),
        ],
        compiler_params=pltpu.CompilerParams(
            dimension_semantics=("arbitrary",), vmem_limit_bytes=VMEM_LIMIT
        ),
        cost_estimate=pl.CostEstimate(
            flops=2 * rows * width * 3 * LANES, bytes_accessed=rows * width * 12, transcendentals=0
        ),
    )(zx, bcdt, taps, chan, bct, bcb, dtv, spread_matrix(width))


def mixer_backward(sg, zx, mixed, sin, bcdt, coef, taps, chan, bct, bcb, dtv):
    rows, width2 = zx.shape
    width = width2 // 2
    chunks = rows // Q
    last = chunks - 1
    return pl.pallas_call(
        functools.partial(bwd_kernel, head_count=width // HEADDIM),
        grid=(chunks,),
        in_specs=[
            pl.BlockSpec((Q, width), lambda c: (last - c, 0)),
            pl.BlockSpec((Q, width2), lambda c: (last - c, 0)),
            pl.BlockSpec((16, width), lambda c: (jnp.maximum((last - c) * (Q // 16) - 1, 0), 1)),
            pl.BlockSpec((Q, width), lambda c: (last - c, 0)),
            pl.BlockSpec((1, LANES, width), lambda c: (last - c, 0, 0)),
            pl.BlockSpec((Q, 384), lambda c: (last - c, 0)),
            pl.BlockSpec((8, 384), lambda c: (jnp.maximum((last - c) * (Q // 8) - 1, 0), 0)),
            pl.BlockSpec((Q, LANES), lambda c: (last - c, 0)),
            whole((4, width)), whole((8, width)), whole((4, 256)), whole((1, 256)),
            whole((8, LANES)), whole((LANES, width)), whole((width, LANES)),
        ],
        out_specs=[
            pl.BlockSpec((Q, width2 + 384), lambda c: (last - c, 0)),
            whole((8, width)), whole((8, 256)), whole((8, LANES)),
        ],
        out_shape=[
            jax.ShapeDtypeStruct((rows, width2 + 384), bf16),
            jax.ShapeDtypeStruct((8, width), f32),
            jax.ShapeDtypeStruct((8, 256), f32),
            jax.ShapeDtypeStruct((8, LANES), f32),
        ],
        scratch_shapes=[
            pltpu.VMEM((Q + 8, width), f32),
            pltpu.VMEM((Q + 8, 256), f32),
            pltpu.VMEM((Q + 8, width), f32),
            pltpu.VMEM((Q + 8, 256), f32),
            pltpu.VMEM((LANES, width), f32),
            pltpu.VMEM((LANES, LANES), f32),
        ],
        compiler_params=pltpu.CompilerParams(
            dimension_semantics=("arbitrary",), vmem_limit_bytes=VMEM_LIMIT
        ),
        cost_estimate=pl.CostEstimate(
            flops=2 * rows * width * 10 * LANES, bytes_accessed=rows * width * 20, transcendentals=0
        ),
    )(sg, zx, zx, mixed, sin, bcdt, bcdt, coef, taps, chan, bct, bcb, dtv,
      spread_matrix(width), gather_matrix(width))


def pair_swap(v):
    return lax.ppermute(v, "tensor", ((0, 1), (1, 0)))


def both_rows(own, other, first):
    return jnp.where(
        first, jnp.concatenate([own, other], axis=0), jnp.concatenate([other, own], axis=0)
    )


def sum_devices(v):
    span = 1
    size = lax.axis_size("dp")
    while span < size:
        v = v + lax.ppermute(v, "dp", [(i, i ^ span) for i in range(size)])
        span *= 2
    return v


def head_lanes(v):
    return jnp.pad(v, ((0, LANES - v.shape[0]),))


def local(
    hidden,
    pre_gain,
    w_zx,
    w_bc,
    w_dt,
    conv_x,
    conv_x_bias,
    conv_bc,
    conv_bc_bias,
    dt_bias,
    a_log,
    d_skip,
    norm_gain,
    w_out,
    cotangent,
):
    layers = pre_gain.shape[0]
    own_count, depth = hidden.shape
    rows = own_count * lax.axis_size("tensor")
    width = w_zx.shape[-1]
    heads = dt_bias.shape[-1]
    tensor_index = lax.axis_index("tensor")
    first = tensor_index == 0

    def own_half(v):
        return lax.dynamic_slice_in_dim(v, tensor_index * own_count, own_count, 0)

    def other_half(v):
        return lax.dynamic_slice_in_dim(v, (1 - tensor_index) * own_count, own_count, 0)

    def gather_pair(v):
        return both_rows(v, pair_swap(v), first)

    in_weights = []
    out_weights = []
    for l in range(layers):
        shard = jnp.concatenate(
            [
                w_zx[l].reshape(w_zx.shape[1], -1),
                w_bc[l],
                jnp.pad(w_dt[l], ((0, 0), (0, LANES - heads))),
            ],
            axis=1,
        )
        in_weights.append(lax.all_gather(shard, "dp", axis=0, tiled=True))
        out_weights.append(lax.all_gather(w_out[l].T, "dp", axis=0, tiled=True))
    params = []
    for l in range(layers):
        chan = jnp.zeros((8, width), f32)
        chan = chan.at[0].set(conv_x_bias[l]).at[1].set(norm_gain[l])
        chan = chan.at[2].set(jnp.repeat(d_skip[l], HEADDIM))
        dtv = jnp.zeros((8, LANES), f32)
        dtv = dtv.at[0].set(head_lanes(dt_bias[l])).at[1].set(head_lanes(-jnp.exp(a_log[l])))
        params.append((conv_x[l], chan, conv_bc[l], conv_bc_bias[l][None, :], dtv))

    current = hidden.astype(f32)
    cot = gather_pair(cotangent)
    saved = []
    for l in range(layers):
        w_in = in_weights[l]
        rms = lax.rsqrt(jnp.mean(current * current, axis=1, keepdims=True) + epsilon)
        normed = gather_pair((current * rms * pre_gain[l][None, :]).astype(bf16))
        zx = mm(normed, w_in[:, : 2 * width])
        bcdt = mm(normed, w_in[:, 2 * width :])
        scaled, mixed, states, squares = mixer_forward(zx, bcdt, *params[l])
        squares = jnp.sum(squares, axis=1).reshape(8, -1)
        squares = (squares + pair_swap(squares)).reshape(rows, 1)
        inv = lax.rsqrt(squares / INNER + epsilon)
        shaped = (scaled * inv).astype(bf16)
        other = mm_t(other_half(shaped), out_weights[l])
        arrived = pair_swap(other.astype(bf16))
        own = mm_t(own_half(shaped), out_weights[l])
        lifted = own + arrived.astype(f32)
        if l == layers - 1:
            own_dot = jnp.sum(own_half(cot).astype(f32) * own, axis=1, keepdims=True)
            other_dot = jnp.sum(other_half(cot).astype(f32) * other, axis=1, keepdims=True)
            dots = jnp.where(
                first,
                jnp.concatenate([own_dot, other_dot], axis=0),
                jnp.concatenate([other_dot, own_dot], axis=0),
            ).reshape(8, -1)
            last_dot = (dots + pair_swap(dots)).reshape(rows, 1)
        saved.append((current, rms, normed, zx, bcdt, shaped, mixed, states, inv, lifted))
        current = current + lifted
    hidden_out = current
    grad_rows = cotangent.astype(f32)
    outputs = [None] * layers
    packed = [None] * layers
    for l in reversed(range(layers)):
        current, rms, normed, zx, bcdt, shaped, mixed, states, inv, lifted = saved[l]
        w_in = in_weights[l]
        if l == layers - 1:
            out_grad = cot
            row_dot = last_dot
        else:
            own_grad = grad_rows.astype(bf16)
            out_grad = gather_pair(own_grad)
            own_dot = jnp.sum(own_grad.astype(f32) * lifted, axis=1).reshape(8, -1)
            row_dot = both_rows(own_dot.reshape(-1, 1), pair_swap(own_dot).reshape(-1, 1), first)
        coef = jnp.pad(
            jnp.concatenate([inv * inv * row_dot / INNER, inv], axis=1), ((0, 0), (0, LANES - 2))
        )
        shaped_grad = mm(out_grad, out_weights[l])
        grad_out = t_mm(out_grad, shaped).astype(bf16)
        low, gchan, gbc, gdt = mixer_backward(
            shaped_grad, zx, mixed, states, bcdt, coef, *params[l]
        )
        arrived = pair_swap(mm_t(other_half(low), w_in).astype(bf16))
        normed_grad = mm_t(own_half(low), w_in) + arrived.astype(f32)
        grad_in = t_mm(normed, low[:, : 2 * width]).astype(bf16)
        grad_side = t_mm(normed, low[:, 2 * width :])
        grad_out_own = lax.psum_scatter(grad_out, "dp", scatter_dimension=0, tiled=True)
        grad_in_own = lax.psum_scatter(grad_in, "dp", scatter_dimension=0, tiled=True)
        grad_side = lax.psum_scatter(grad_side, "dp", scatter_dimension=0, tiled=True)
        unit = current * rms
        weighted = normed_grad * pre_gain[l][None, :]
        grad_pre = jnp.sum(normed_grad * unit, axis=0)
        grad_rows = grad_rows + rms * (
            weighted - unit * jnp.mean(weighted * unit, axis=1, keepdims=True)
        )
        gchan = gchan.at[7].set(grad_pre)
        packed[l] = jnp.concatenate([gchan, gbc, gdt], axis=1)
        grad_in_own = grad_in_own.astype(f32)
        grad_bc = grad_side[:, :256]
        outputs[l] = (
            grad_in_own.reshape(-1, 2, width),
            grad_bc + pair_swap(grad_bc),
            grad_side[:, 256 : 256 + heads],
            grad_out_own.astype(f32).T,
        )
    small = jnp.stack(packed)
    row = lax.broadcasted_iota(jnp.int32, small.shape, 1)
    col = lax.broadcasted_iota(jnp.int32, small.shape, 2)
    shared = ((row == 7) & (col < width)) | ((col >= width) & (col < width + 256))
    small = sum_devices(small + jnp.where(shared, pair_swap(small), 0.0))
    grad_w_zx, grad_w_bc, grad_w_dt, grad_w_out = (
        jnp.stack([o[i] for o in outputs]) for i in range(4)
    )
    return (
        hidden_out,
        grad_rows,
        small[:, 7, :width],
        grad_w_zx,
        grad_w_bc,
        grad_w_dt,
        small[:, 0:4, :width],
        small[:, 4, :width],
        small[:, 0:4, width : width + 256],
        small[:, 4, width : width + 256],
        small[:, 0, width + 256 : width + 256 + heads],
        small[:, 1, width + 256 : width + 256 + heads],
        jnp.sum(small[:, 6, :width].reshape(layers, heads, HEADDIM), axis=2),
        small[:, 5, :width],
        grad_w_out,
    )


def solution(mesh):
    return jax.shard_map(
        local,
        mesh=mesh,
        in_specs=(
            P(("dp", "tensor"), None),
            P(),
            P(None, "dp", None, "tensor"),
            P(None, "dp", None),
            P(None, "dp", "tensor"),
            P(None, None, "tensor"),
            P(None, "tensor"),
            P(),
            P(),
            P(None, "tensor"),
            P(None, "tensor"),
            P(None, "tensor"),
            P(None, "tensor"),
            P(None, "tensor", "dp"),
            P(("dp", "tensor"), None),
        ),
        out_specs=(
            P(("dp", "tensor"), None),
            P(("dp", "tensor"), None),
            P(),
            P(None, "dp", None, "tensor"),
            P(None, "dp", None),
            P(None, "dp", "tensor"),
            P(None, None, "tensor"),
            P(None, "tensor"),
            P(),
            P(),
            P(None, "tensor"),
            P(None, "tensor"),
            P(None, "tensor"),
            P(None, "tensor"),
            P(None, "tensor", "dp"),
        ),
        check_vma=False,
    )
```

time: 3120 us -> 1070 us (0.34)
  waiting for transfers between devices: 1730 us -> 594 us
  matrix products: 586 us -> 197 us
  local copies, waits for them, and re-layouts: 404 us -> 38.9 us
  other arithmetic: 251 us -> 41.6 us
  Pallas kernels: 0 us -> 160 us
  blocking collectives: 115 us -> 0 us
    unnamed x28 -> x10, waiting for transfers between devices: 727 us -> 0.16 us
    dot_general x134 -> x20, matrix products: 582 us -> 197 us  [the longest x6 68 us: t_mm(): lax.dot_general(a, b, (((0,), (0,)), ((), ())), preferred_element_type=f32)]
    reduce_scatter x8 -> x6, waiting for transfers between devices: 571 us -> 292 us  [the longest x2 226 us: local(): lax.psum_scatter(grad_in, 'dp', scatter_dimension=0, tiled=True)]
    ppermute x0 -> x19, waiting for transfers between devices: none -> 252 us  [the longest x15 239 us: pair_swap(): return lax.ppermute(v, 'tensor', ((0, 1), (1, 0)))]
    psum x4 -> x0, waiting for transfers between devices: 248 us -> none  [the longest x2 247 us: local(): lax.psum((stack_member(small_terms, 0), place_share(local_taps), place_sh...]
    reshape x38 -> x1, local copies, waits for them, and re-layouts: 177 us -> 0.08 us  [local(): own_dot = jnp.sum(own_grad.astype(f32) * lifted, axis=1).reshape(8, -1)]
    pallas_call x0 -> x4, Pallas kernels: none -> 160 us  [the longest x2 103 us: mixer_backward(): pl.pallas_call(functools.partial(bwd_kernel, head_count=width // HEADDIM)...]
    all_gather x8 -> x4, waiting for transfers between devices: 187 us -> 49 us  [the longest x2 49 us: local(): in_weights.append(lax.all_gather(shard, 'dp', axis=0, tiled=True))]
  transfers between devices with their start and end apart: 24 -> 29, of which waited for: 17 -> 19; matrix products, arithmetic and copies ran while one was open for 21% -> 21% of each run, Pallas kernels for 0% -> 10%
where the time goes in v1:
time: 1070 us; the launch traced here: 1060 us
  waiting for transfers between devices  594 us (56%)
  matrix products  197 us (18%)
  Pallas kernels  160 us (15%)
  other arithmetic  41.6 us (4%)
  local copies, waits for them, and re-layouts  38.9 us (4%)
  starting transfers between devices  17.9 us (2%)
  between operations  15.3 us (1%)
    ppermute x15, waiting for transfers between devices, pair_swap(): return lax.ppermute(v, 'tensor', ((0, 1), (1, 0)))  239 us
    reduce_scatter x2, waiting for transfers between devices, local(): lax.psum_scatter(grad_in, 'dp', scatter_dimension=0, tiled=True)  226 us
    pallas_call x2, Pallas kernels, mixer_backward(): pl.pallas_call(functools.partial(bwd_kernel, head_count=width // HEADDIM)...  103 us
    dot_general x6, matrix products, t_mm(): lax.dot_general(a, b, (((0,), (0,)), ((), ())), preferred_element_type=f32)  68 us
    reduce_scatter x2, waiting for transfers between devices, local(): lax.psum_scatter(grad_out, 'dp', scatter_dimension=0, tiled=True)  66.6 us
    dot_general x8, matrix products, mm_t(): lax.dot_general(a, b, (((1,), (1,)), ((), ())), preferred_element_type=f32)  64.8 us
    dot_general x6, matrix products, mm(): lax.dot_general(a, b, (((1,), (0,)), ((), ())), precision=precision, pref...  64.5 us
    pallas_call x2, Pallas kernels, mixer_forward(): pl.pallas_call(functools.partial(fwd_kernel, head_count=width // HEADDIM)...  57.1 us
  transfers between devices with their start and end apart: 29, of which 19 were waited for; matrix products, arithmetic and copies ran while one was open for 21% of the time, Pallas kernels for 10%

profile of v1, /device:TPU:0, one launch (start us, length us, event | category | flops | bytes accessed | tf_op | source)
XLA Modules:
  0.0 1064.8 jit_solution(572124062028972727)
XLA Ops:
  8.9 2.1 fusion.70
  15.3 1.6 fusion.18
  16.9 2.9 collective-permute-start
  24.1 30.5 %collective-permute-done = bf16[512,1536]{1,0:T(8,128)(2,1)} collective-permute-done((bf16[512,1536]{1,0:T(8,128)(2,1)}, bf16[512,1536]{1,0:T(8,128)(2,1)}, u32[]{:S(2)}, u32[]{:S(2)}) %collective-permute-start) | collective-permute-done | bytes 1572896 | tf_op jit(solution)/shard_map/ppermute | solution.py:429
  54.5 49.0 %all-gather.5.cloned.1.call-done = bf16[1536,3456]{1,0:T(8,128)(2,1)} async-done(((bf16[96,3456]{1,0:T(8,128)(2,1)}), bf16[1536,3456]{1,0:T(8,128)(2,1)}) %all-gather.5.cloned.1.call-update) | async-done | bytes 10616848 | tf_op jit(solution)/shard_map/all_gather | solution.py:496
  103.6 5.3 fusion.42.bcdt_ref.bcprev_ref
  109.8 15.9 %fusion.2.zx_ref.xprev_ref = f32[1024,3072]{1,0:T(8,128)} fusion(bf16[1536,3456]{1,0:T(8,128)(2,1)S(1)} %copy-done.65, bf16[512,1536]{1,0:T(8,128)(2,1)} %collective-permute-done, bf16[512,1536]{1,0:T(8,128)(2,1)} %fusion.18, pred[]{:T(512)S(6)} %eq.59), kind=kOutput, calls=%fused_computation.4 | convolution fusion | flops 9677832192 | bytes 25165824 | tf_op jit(solution)/shard_map/dot_general | solution.py:26
  125.7 28.6 %shard_map.262 = (f32[1024,1536]{1,0:T(8,128)}, bf16[1024,1536]{1,0:T(8,128)(2,1)S(1)}, bf16[8,128,1536]{2,1,0:T(8,128)(2,1)}, f32[1024,128]{1,0:T(8,128)S(1)}) custom-call(f32[1024,3072]{1,0:T(8,128)} %fusion.2.zx_ref.xprev_ref, f32[1024,384]{1,0:T(8,128)S(1)} %fusion.42.bcdt_ref.bcprev_ref, f32[4,1536]{1,0:T(4,128)S(1)} %get-tuple-element.249.taps_ref, ...), custom_call_target="tpu_custom_call" | custom-call | flops 1207959552 | bytes 18874368 | tf_op jit(solution)/shard_map/pallas_call | solution.py:345
  154.3 1.7 copy-done.2
  156.2 1.5 collective-permute-start.1
  158.1 1.7 collective-permute-done.1
  160.5 4.9 multiply_convert_fusion.1
  165.4 7.2 convolution_convert_fusion.4
  172.6 1.4 collective-permute-start.2
  174.6 35.6 %collective-permute-done.2 = bf16[512,1536]{1,0:T(8,128)(2,1)} collective-permute-done((bf16[512,1536]{1,0:T(8,128)(2,1)}, bf16[512,1536]{1,0:T(8,128)(2,1)}, u32[]{:S(2)}, u32[]{:S(2)}) %collective-permute-start.2) | collective-permute-done | bytes 1572896 | tf_op jit(solution)/shard_map/ppermute | solution.py:429
  210.3 7.8 multiply_reduce_fusion.5
  218.1 1.6 multiply_convert_fusion.2
  222.7 21.2 %collective-permute-done.6 = bf16[512,1536]{1,0:T(8,128)(2,1)} collective-permute-done((bf16[512,1536]{1,0:T(8,128)(2,1)}, bf16[512,1536]{1,0:T(8,128)(2,1)}, u32[]{:S(2)}, u32[]{:S(2)}) %collective-permute-start.6) | collective-permute-done | bytes 1572896 | tf_op jit(solution)/shard_map/ppermute | solution.py:429
  244.0 4.5 maximum_select_fusion.2
  248.4 27.2 %collective-permute-done.3 = bf16[512,1536]{1,0:T(8,128)(2,1)} collective-permute-done((bf16[512,1536]{1,0:T(8,128)(2,1)}, bf16[512,1536]{1,0:T(8,128)(2,1)}, u32[]{:S(2)}, u32[]{:S(2)}) %collective-permute-start.3) | collective-permute-done | bytes 1572896 | tf_op jit(solution)/shard_map/ppermute | solution.py:429
  275.6 5.3 fusion.40.bcdt_ref.bcprev_ref
  281.0 15.9 %fusion.zx_ref.xprev_ref = f32[1024,3072]{1,0:T(8,128)} fusion(bf16[1536,3456]{1,0:T(8,128)(2,1)S(1)} %copy-done.66, bf16[512,1536]{1,0:T(8,128)(2,1)} %collective-permute-done.3, bf16[512,1536]{1,0:T(8,128)(2,1)} %multiply_convert_fusion.2, pred[]{:T(512)S(6)} %eq.59), kind=kOutput, calls=%fused_computation.2 | convolution fusion | flops 9677832192 | bytes 25165824 | tf_op jit(solution)/shard_map/dot_general | solution.py:26
  296.9 28.5 %shard_map.263 = (f32[1024,1536]{1,0:T(8,128)}, bf16[1024,1536]{1,0:T(8,128)(2,1)S(1)}, bf16[8,128,1536]{2,1,0:T(8,128)(2,1)}, f32[1024,128]{1,0:T(8,128)S(1)}) custom-call(f32[1024,3072]{1,0:T(8,128)} %fusion.zx_ref.xprev_ref, f32[1024,384]{1,0:T(8,128)S(1)} %fusion.40.bcdt_ref.bcprev_ref, f32[4,1536]{1,0:T(4,128)S(1)} %copy-done.14, ...), custom_call_target="tpu_custom_call" | custom-call | flops 1207959552 | bytes 18874368 | tf_op jit(solution)/shard_map/pallas_call | solution.py:345
  325.4 1.7 copy-done.4
  327.9 1.8 reduce_sum.111
  331.1 10.0 fusion.76.sg_ref
  342.2 1.9 copy-done.67
  344.2 2.6 fusion.31
  347.2 4.6 multiply_reduce_fusion.4
  353.2 2.3 collective-permute-done.7
  356.1 1.7 copy.53
  359.9 1.9 copy-done.5
  364.0 51.4 %shard_map.264 = (bf16[1024,3456]{1,0:T(8,128)(2,1)}, f32[8,1536]{1,0:T(8,128)S(1)}, f32[8,256]{1,0:T(8,128)S(1)}, f32[8,128]{1,0:T(8,128)S(1)}) custom-call(f32[1024,1536]{1,0:T(8,128)} %fusion.76.sg_ref, f32[1024,3072]{1,0:T(8,128)} %fusion.zx_ref.xprev_ref, f32[1024,3072]{1,0:T(8,128)} %fusion.zx_ref.xprev_ref, bf16[1024,1536]{1,0:T(8,128)(2,1)S(1)} %copy-done.5, ...), custom_call_target="tpu_custom_call" | custom-call | flops 4026531840 | bytes 31457280 | tf_op jit(solution)/shard_map/pallas_call | solution.py:385
  415.4 9.8 fusion.25
  427.4 35.3 %collective-permute-done.8 = bf16[512,1536]{1,0:T(8,128)(2,1)S(1)} collective-permute-done((bf16[512,1536]{1,0:T(8,128)(2,1)S(1)}, bf16[512,1536]{1,0:T(8,128)(2,1)S(1)}, u32[]{:S(2)}, u32[]{:S(2)}) %collective-permute-start.8) | collective-permute-done | bytes 1572896 | tf_op jit(solution)/shard_map/ppermute | solution.py:429
  462.7 10.4 multiply_reduce_fusion
  473.2 19.0 %collective-permute-done.5 = bf16[512,1536]{1,0:T(8,128)(2,1)S(1)} collective-permute-done((bf16[512,1536]{1,0:T(8,128)(2,1)}, bf16[512,1536]{1,0:T(8,128)(2,1)S(1)}, u32[]{:S(2)}, u32[]{:S(2)}) %collective-permute-start.5) | collective-permute-done | bytes 1572896 | tf_op jit(solution)/shard_map/ppermute | solution.py:429
  492.2 5.6 multiply_reduce_fusion.1
  498.5 6.7 fusion.44
  505.3 1.4 collective-permute-start.10
  506.7 23.7 %collective-permute-done.10 = f32[8,64]{1,0:T(8,128)S(1)} collective-permute-done((f32[8,64]{1,0:T(8,128)S(1)}, f32[8,64]{1,0:T(8,128)S(1)}, u32[]{:S(2)}, u32[]{:S(2)}) %collective-permute-start.10) | collective-permute-done | bytes 2080 | tf_op jit(solution)/shard_map/ppermute | solution.py:429
  530.8 12.1 %fusion.53.sg_ref = f32[1024,1536]{1,0:T(8,128)} fusion(bf16[1536,1536]{1,0:T(8,128)(2,1)} %all-gather.7.cloned.1.call-done, bf16[512,1536]{1,0:T(8,128)(2,1)} %collective-permute-done.9, bf16[512,1536]{1,0:T(8,128)(2,1)} %get-tuple-element.230, pred[]{:T(512)S(6)} %eq.59), kind=kOutput, calls=%fused_computation.81 | convolution fusion | flops 4845993984 | bytes 14155777 | tf_op jit(solution)/shard_map/dot_general | solution.py:26
  542.9 51.6 %shard_map.265 = (bf16[1024,3456]{1,0:T(8,128)(2,1)}, f32[8,1536]{1,0:T(8,128)S(1)}, f32[8,256]{1,0:T(8,128)S(1)}, f32[8,128]{1,0:T(8,128)S(1)}) custom-call(f32[1024,1536]{1,0:T(8,128)} %fusion.53.sg_ref, f32[1024,3072]{1,0:T(8,128)} %fusion.2.zx_ref.xprev_ref, f32[1024,3072]{1,0:T(8,128)} %fusion.2.zx_ref.xprev_ref, bf16[1024,1536]{1,0:T(8,128)(2,1)S(1)} %copy-done.3, ...), custom_call_target="tpu_custom_call" | custom-call | flops 4026531840 | bytes 31457280 | tf_op jit(solution)/shard_map/pallas_call | solution.py:385
  594.5 6.5 fusion.46
  601.1 9.2 convolution_convert_fusion.2
  610.3 10.0 convolution_convert_fusion.3
  620.4 17.8 %convolution_convert_fusion = bf16[1536,3072]{1,0:T(8,128)(2,1)} fusion(bf16[1024,3456]{1,0:T(8,128)(2,1)} %get-tuple-element.181, bf16[512,1536]{1,0:T(8,128)(2,1)} %collective-permute-done.3, bf16[512,1536]{1,0:T(8,128)(2,1)} %multiply_convert_fusion.2, pred[]{:T(512)S(6)} %eq.59), kind=kOutput, calls=%fused_computation | convolution fusion | flops 9682550784 | bytes 18874368 | tf_op jit(solution)/shard_map/dot_general | solution.py:36
  638.3 17.7 %convolution_convert_fusion.1 = bf16[1536,3072]{1,0:T(8,128)(2,1)} fusion(bf16[1024,3456]{1,0:T(8,128)(2,1)} %get-tuple-element.184, bf16[512,1536]{1,0:T(8,128)(2,1)} %collective-permute-done, bf16[512,1536]{1,0:T(8,128)(2,1)} %fusion.18, pred[]{:T(512)S(6)} %eq.59), kind=kOutput, calls=%fused_computation.1 | convolution fusion | flops 9682550784 | bytes 18874368 | tf_op jit(solution)/shard_map/dot_general | solution.py:36
  656.1 10.7 %fusion.28 = bf16[512,1536]{1,0:T(8,128)(2,1)} fusion(bf16[1536,3456]{1,0:T(8,128)(2,1)} %all-gather.5.cloned.1.call-done, bf16[1024,3456]{1,0:T(8,128)(2,1)} %get-tuple-element.184, s32[]{:T(128)S(6)} %select_n.99), kind=kOutput, calls=%fused_computation.51 | convolution fusion | flops 5436604416 | bytes 15728644 | tf_op jit(solution)/shard_map/dot_general | solution.py:32
  667.9 30.5 %collective-permute-done.11 = bf16[512,1536]{1,0:T(8,128)(2,1)} collective-permute-done((bf16[512,1536]{1,0:T(8,128)(2,1)}, bf16[512,1536]{1,0:T(8,128)(2,1)}, u32[]{:S(2)}, u32[]{:S(2)}) %collective-permute-start.11) | collective-permute-done | bytes 1572896 | tf_op jit(solution)/shard_map/ppermute | solution.py:429
  698.5 11.6 %fusion.23 = (f32[1536]{0:T(1024)S(1)}, f32[512]{0:T(512)S(1)}, f32[512,1536]{1,0:T(8,128)}) fusion(bf16[512,1536]{1,0:T(8,128)(2,1)S(1)} %copy-done.28, f32[512]{0:T(512)S(1)} %copy-done.52, bf16[512,1536]{1,0:T(8,128)(2,1)} %collective-permute-done.11, f32[1536]{0:T(1024)S(1)} %copy-done.38, bf16[1536,3456]{1,0:T(8,128)(2,1)} %all-gather.5.cloned.1.call-done, ...), kind=kOutput, calls=%fused_computation.32 | convolution fusion | flops 5442893824 | bytes 20463620 | tf_op jit(solution)/shard_map/dot_general | solution.py:32
  710.9 4.3 collective-permute-done.12
  717.9 4.5 collective-permute-done.18
  723.4 9.3 collective-permute-done.15
  732.8 5.9 fusion.22
  738.7 4.0 collective-permute-done.16
  751.0 3.2 collective-permute-done.17
  755.8 66.6 %reduce-scatter.15.cloned.1.call-done = bf16[96,1536]{1,0:T(8,128)(2,1)} async-done(((bf16[1536,1536]{1,0:T(8,128)(2,1)}), bf16[96,1536]{1,0:T(8,128)(2,1)}) %reduce-scatter.15.cloned.1.call-update) | async-done | bytes 294928 | tf_op jit(solution)/shard_map/reduce_scatter | solution.py:563
  822.4 2.1 maximum_convert_fusion.1
  824.6 112.4 %reduce-scatter.9.cloned.1.call-done = bf16[96,3072]{1,0:T(8,128)(2,1)} async-done(((bf16[1536,3072]{1,0:T(8,128)(2,1)}), bf16[96,3072]{1,0:T(8,128)(2,1)}) %reduce-scatter.9.cloned.1.call-update) | async-done | bytes 589840 | tf_op jit(solution)/shard_map/reduce_scatter | solution.py:564
  936.9 2.4 stack_reshape.9
  939.4 113.2 %reduce-scatter.7.cloned.1.call-done = bf16[96,3072]{1,0:T(8,128)(2,1)} async-done(((bf16[1536,3072]{1,0:T(8,128)(2,1)}), bf16[96,3072]{1,0:T(8,128)(2,1)}) %reduce-scatter.7.cloned.1.call-update) | async-done | bytes 589840 | tf_op jit(solution)/shard_map/reduce_scatter | solution.py:564
  1052.6 2.2 stack_reshape.8
  1054.8 2.9 maximum_convert_fusion
  (272 shorter events, 44.8 us)
Async XLA Ops:
  7.2 96.4 %all-gather.5.cloned.1.call-start = ((), (), s32[]{:S(2)}) async-start(), calls=%async_computation.6 | async-start | bytes 11280384 | tf_op jit(solution)/shard_map/all_gather | solution.py:496
  12.0 153.4 %all-gather.7.cloned.1.call-start = ((), (), s32[]{:S(2)}) async-start(), calls=%async_computation.7 | async-start | bytes 5013504 | tf_op jit(solution)/shard_map/all_gather | solution.py:497
  12.9 235.5 %all-gather.9.cloned.1.call-start = ((), (), s32[]{:S(2)}) async-start(), calls=%async_computation.8 | async-start | bytes 11280384 | tf_op jit(solution)/shard_map/all_gather | solution.py:496
  14.1 9.1 copy-start.58
  14.1 9.1 copy-start.43
  14.2 316.9 %all-gather.11.cloned.1.call-start = ((), (), s32[]{:S(2)}) async-start(), calls=%async_computation.9 | async-start | bytes 5013504 | tf_op jit(solution)/shard_map/all_gather | solution.py:497
  16.9 37.6 %collective-permute-start = (bf16[512,1536]{1,0:T(8,128)(2,1)}, bf16[512,1536]{1,0:T(8,128)(2,1)}, u32[]{:S(2)}, u32[]{:S(2)}) collective-permute-start(bf16[512,1536]{1,0:T(8,128)(2,1)} %fusion.18), channel_id=1, source_target_pairs={{0,1},{1,0},{2,3},{3,2},{4,5},{5,4},{6,7},{7,6},{8,9},{9,8},{10,11... | collective-permute-start | bytes 4718600 | tf_op jit(solution)/shard_map/ppermute | solution.py:429
  22.7 103.0 %copy-start.7 = (f32[8,1536]{1,0:T(8,128)}, f32[8,1536]{1,0:T(8,128)S(1)}, u32[]{:S(2)}) copy-start(f32[8,1536]{1,0:T(8,128)S(1)} %scatter.44.chan_ref) | copy-start | bytes 147460
  22.7 31.8 %copy-start.41 = (s32[1536]{0:T(1024)}, s32[1536]{0:T(1024)S(1)}, u32[]{:S(2)}) copy-start(s32[1536]{0:T(1024)S(1)} %get-tuple-element.272) | copy-start | bytes 18436
  23.3 102.4 %copy-start.18 = (f32[1,256]{1,0:T(1,128)}, f32[1,256]{1,0:T(1,128)S(1)}, u32[]{:S(2)}) copy-start(f32[1,256]{1,0:T(1,128)S(1)} %get-tuple-element.259.bcb_ref) | copy-start | bytes 3076
  23.9 101.8 %copy-start.12 = (f32[4,1536]{1,0:T(4,128)}, f32[4,1536]{1,0:T(4,128)S(1)}, u32[]{:S(2)}) copy-start(f32[4,1536]{1,0:T(4,128)S(1)} %get-tuple-element.249.taps_ref) | copy-start | bytes 73732
  156.2 3.7 collective-permute-start.1
  157.7 557.7 %reduce-scatter.13.cloned.1.call-start = ((), (), s32[]{:S(2)}) async-start(), calls=%async_computation.13 | async-start | bytes 2506752 | tf_op jit(solution)/shard_map/reduce_scatter | solution.py:565
  165.4 44.9 %copy-start.27 = (bf16[512,1536]{1,0:T(8,128)(2,1)S(1)}, bf16[512,1536]{1,0:T(8,128)(2,1)}, u32[]{:S(2)}) copy-start(bf16[512,1536]{1,0:T(8,128)(2,1)} %param.39) | copy-start | bytes 4718596
  172.6 37.6 %collective-permute-start.2 = (bf16[512,1536]{1,0:T(8,128)(2,1)}, bf16[512,1536]{1,0:T(8,128)(2,1)}, u32[]{:S(2)}, u32[]{:S(2)}) collective-permute-start(bf16[512,1536]{1,0:T(8,128)(2,1)} %convolution_convert_fusion.4), channel_id=1, source_target_pairs={{0,1},{1,0},{2,3},{3,2},{4,5},{5,4},{6,7},{7,6},{8,9},{9,8},{10,11... | collective-permute-start | bytes 4718600 | tf_op jit(solution)/shard_map/ppermute | solution.py:429
  174.0 70.0 %collective-permute-start.6 = (bf16[512,1536]{1,0:T(8,128)(2,1)}, bf16[512,1536]{1,0:T(8,128)(2,1)}, u32[]{:S(2)}, u32[]{:S(2)}) collective-permute-start(bf16[512,1536]{1,0:T(8,128)(2,1)} %param.53), channel_id=1, source_target_pairs={{0,1},{1,0},{2,3},{3,2},{4,5},{5,4},{6,7},{7,6},{8,9},{9,8},{10,11... | collective-permute-start | bytes 4718600 | tf_op jit(solution)/shard_map/ppermute | solution.py:429
  174.6 43.5 %copy-start.39 = (f32[1536]{0:T(1024)S(1)}, f32[1536]{0:T(1024)}, u32[]{:S(2)}) copy-start(f32[1536]{0:T(1024)} %get-tuple-element.227) | copy-start | bytes 18436
  219.7 55.9 %collective-permute-start.3 = (bf16[512,1536]{1,0:T(8,128)(2,1)}, bf16[512,1536]{1,0:T(8,128)(2,1)}, u32[]{:S(2)}, u32[]{:S(2)}) collective-permute-start(bf16[512,1536]{1,0:T(8,128)(2,1)} %multiply_convert_fusion.2), channel_id=1, source_target_pairs={{0,1},{1,0},{2,3},{3,2},{4,5},{5,4},{6,7},{7,6},{8,9},{9,8},{10,11... | collective-permute-start | bytes 4718600 | tf_op jit(solution)/shard_map/ppermute | solution.py:429
  221.7 26.8 %copy-start.9 = (f32[8,1536]{1,0:T(8,128)}, f32[8,1536]{1,0:T(8,128)S(1)}, u32[]{:S(2)}) copy-start(f32[8,1536]{1,0:T(8,128)S(1)} %scatter.51.chan_ref) | copy-start | bytes 147460
  248.4 32.5 %copy-start.66 = (bf16[1536,3456]{1,0:T(8,128)(2,1)S(1)}, bf16[1536,3456]{1,0:T(8,128)(2,1)}, u32[]{:S(2)}) copy-start(bf16[1536,3456]{1,0:T(8,128)(2,1)} %all-gather.9.cloned.1.call-done) | copy-start | bytes 31850500
  281.0 15.9 %copy-start.10 = (f32[8,1536]{1,0:T(8,128)S(1)}, f32[8,1536]{1,0:T(8,128)}, u32[]{:S(2)}) copy-start(f32[8,1536]{1,0:T(8,128)} %copy-done.9) | copy-start | bytes 147460
  281.0 15.9 %copy-start.14 = (f32[4,1536]{1,0:T(4,128)S(1)}, f32[4,1536]{1,0:T(4,128)}, u32[]{:S(2)}) copy-start(f32[4,1536]{1,0:T(4,128)} %get-tuple-element.248.taps_ref) | copy-start | bytes 73732
  281.0 15.9 %copy-start.20 = (f32[1,256]{1,0:T(1,128)S(1)}, f32[1,256]{1,0:T(1,128)}, u32[]{:S(2)}) copy-start(f32[1,256]{1,0:T(1,128)} %get-tuple-element.258.bcb_ref) | copy-start | bytes 3076
  329.7 11.4 %collective-permute-start.4 = (f32[8,128]{1,0:T(8,128)}, f32[8,128]{1,0:T(8,128)}, u32[]{:S(2)}, u32[]{:S(2)}) collective-permute-start(f32[8,128]{1,0:T(8,128)} %bitcast.122), channel_id=1, source_target_pairs={{0,1},{1,0},{2,3},{3,2},{4,5},{5,4},{6,7},{7,6},{8,9},{9,8},{10,11... | collective-permute-start | bytes 12296 | tf_op jit(solution)/shard_map/ppermute | solution.py:429
  331.1 10.0 copy-start.46
  331.1 10.7 %copy-start.31 = (f32[1024,1536]{1,0:T(8,128)S(1)}, f32[1024,1536]{1,0:T(8,128)}, u32[]{:S(2)}) copy-start(f32[1024,1536]{1,0:T(8,128)} %get-tuple-element.177) | copy-start | bytes 18874372
  351.8 3.7 collective-permute-start.7
  415.4 9.9 copy-start.16
  415.4 9.9 copy-start.22
  415.4 9.9 copy-start.24
  415.4 47.3 %copy-start.30 = (f32[512,1536]{1,0:T(8,128)S(1)}, f32[512,1536]{1,0:T(8,128)}, u32[]{:S(2)}) copy-start(f32[512,1536]{1,0:T(8,128)} %copy-done.29) | copy-start | bytes 9437188
  415.4 47.3 %copy-start.40 = (f32[1536]{0:T(1024)S(1)}, f32[1536]{0:T(1024)}, u32[]{:S(2)}) copy-start(f32[1536]{0:T(1024)} %get-tuple-element.227) | copy-start | bytes 18436
  415.4 47.3 %copy-start.50 = (f32[512]{0:T(512)S(1)}, f32[512]{0:T(512)}, u32[]{:S(2)}) copy-start(f32[512]{0:T(512)} %copy-done.49) | copy-start | bytes 6148
  425.3 37.4 %collective-permute-start.8 = (bf16[512,1536]{1,0:T(8,128)(2,1)S(1)}, bf16[512,1536]{1,0:T(8,128)(2,1)S(1)}, u32[]{:S(2)}, u32[]{:S(2)}) collective-permute-start(bf16[512,1536]{1,0:T(8,128)(2,1)S(1)} %fusion.25), channel_id=1, source_target_pairs={{0,1},{1,0},{2,3},{3,2},{4,5},{5,4},{6,7},{7,6},{8,9},{9,8},{10,11... | collective-permute-start | bytes 4718600 | tf_op jit(solution)/shard_map/ppermute | solution.py:429
  426.1 66.1 %copy-start.34 = (f32[512,1536]{1,0:T(8,128)S(1)}, f32[512,1536]{1,0:T(8,128)}, u32[]{:S(2)}) copy-start(f32[512,1536]{1,0:T(8,128)} %get-tuple-element.266) | copy-start | bytes 9437188
  426.1 66.1 %copy-start.35 = (f32[512,1536]{1,0:T(8,128)S(1)}, f32[512,1536]{1,0:T(8,128)}, u32[]{:S(2)}) copy-start(f32[512,1536]{1,0:T(8,128)} %get-tuple-element.267) | copy-start | bytes 9437188
  426.1 66.1 %collective-permute-start.5 = (bf16[512,1536]{1,0:T(8,128)(2,1)}, bf16[512,1536]{1,0:T(8,128)(2,1)S(1)}, u32[]{:S(2)}, u32[]{:S(2)}) collective-permute-start(bf16[512,1536]{1,0:T(8,128)(2,1)} %get-tuple-element.235), channel_id=1, source_target_pairs={{0,1},{1,0},{2,3},{3,2},{4,5},{5,4},{6,7},{7,6},{8,9},{9,8},{10,11... | collective-permute-start | bytes 4718600 | tf_op jit(solution)/shard_map/ppermute | solution.py:429
  497.8 8.9 copy-start.54
  497.8 33.0 %collective-permute-start.9 = (bf16[512,1536]{1,0:T(8,128)(2,1)}, bf16[512,1536]{1,0:T(8,128)(2,1)}, u32[]{:S(2)}, u32[]{:S(2)}) collective-permute-start(bf16[512,1536]{1,0:T(8,128)(2,1)} %get-tuple-element.230), channel_id=1, source_target_pairs={{0,1},{1,0},{2,3},{3,2},{4,5},{5,4},{6,7},{7,6},{8,9},{9,8},{10,11... | collective-permute-start | bytes 4718600 | tf_op jit(solution)/shard_map/ppermute | solution.py:429
  505.2 242.6 %reduce-scatter.11.cloned.1.call-start = ((), (), s32[]{:S(2)}) async-start(), calls=%async_computation.12 | async-start | bytes 2506752 | tf_op jit(solution)/shard_map/reduce_scatter | solution.py:565
  505.3 25.1 %collective-permute-start.10 = (f32[8,64]{1,0:T(8,128)S(1)}, f32[8,64]{1,0:T(8,128)S(1)}, u32[]{:S(2)}, u32[]{:S(2)}) collective-permute-start(f32[8,64]{1,0:T(8,128)S(1)} %reshape.595), channel_id=1, source_target_pairs={{0,1},{1,0},{2,3},{3,2},{4,5},{5,4},{6,7},{7,6},{8,9},{9,8},{10,11... | collective-permute-start | bytes 6152 | tf_op jit(solution)/shard_map/ppermute | solution.py:429
  530.8 12.1 %copy-start.1 = (bf16[1536,128]{1,0:T(8,128)(2,1)S(1)}, bf16[1536,128]{1,0:T(8,128)(2,1)}, u32[]{:S(2)}) copy-start(bf16[1536,128]{1,0:T(8,128)(2,1)} %fusion.48.gather_ref) | copy-start | bytes 1179652
  530.8 12.1 %copy-start.3 = (bf16[1024,1536]{1,0:T(8,128)(2,1)S(1)}, bf16[1024,1536]{1,0:T(8,128)(2,1)}, u32[]{:S(2)}) copy-start(bf16[1024,1536]{1,0:T(8,128)(2,1)} %copy-done.2) | copy-start | bytes 9437188
  530.8 12.1 %copy-start.8 = (f32[8,1536]{1,0:T(8,128)S(1)}, f32[8,1536]{1,0:T(8,128)}, u32[]{:S(2)}) copy-start(f32[8,1536]{1,0:T(8,128)} %copy-done.7) | copy-start | bytes 147460
  530.8 12.1 %copy-start.13 = (f32[4,1536]{1,0:T(4,128)S(1)}, f32[4,1536]{1,0:T(4,128)}, u32[]{:S(2)}) copy-start(f32[4,1536]{1,0:T(4,128)} %copy-done.12) | copy-start | bytes 73732
  530.8 12.1 %copy-start.19 = (f32[1,256]{1,0:T(1,128)S(1)}, f32[1,256]{1,0:T(1,128)}, u32[]{:S(2)}) copy-start(f32[1,256]{1,0:T(1,128)} %copy-done.18) | copy-start | bytes 3076
  601.0 154.8 %reduce-scatter.17.cloned.1.call-start = ((), (), s32[]{:S(2)}) async-start(), calls=%async_computation.15 | async-start | bytes 5013504 | tf_op jit(solution)/shard_map/reduce_scatter | solution.py:563
  610.3 212.2 %reduce-scatter.15.cloned.1.call-start = ((), (), s32[]{:S(2)}) async-start(), calls=%async_computation.14 | async-start | bytes 5013504 | tf_op jit(solution)/shard_map/reduce_scatter | solution.py:563
  620.4 316.6 %reduce-scatter.9.cloned.1.call-start = ((), (), s32[]{:S(2)}) async-start(), calls=%async_computation.11 | async-start | bytes 10027008 | tf_op jit(solution)/shard_map/reduce_scatter | solution.py:564
  638.3 414.3 %reduce-scatter.7.cloned.1.call-start = ((), (), s32[]{:S(2)}) async-start(), calls=%async_computation.10 | async-start | bytes 10027008 | tf_op jit(solution)/shard_map/reduce_scatter | solution.py:564
  656.1 11.6 %copy-start.17 = (f32[8,1536]{1,0:T(8,128)S(1)}, f32[8,1536]{1,0:T(8,128)}, u32[]{:S(2)}) copy-start(f32[8,1536]{1,0:T(8,128)} %copy-done.16) | copy-start | bytes 147460
  656.1 11.8 %copy-start.23 = (f32[8,256]{1,0:T(8,128)S(1)}, f32[8,256]{1,0:T(8,128)}, u32[]{:S(2)}) copy-start(f32[8,256]{1,0:T(8,128)} %copy-done.22) | copy-start | bytes 24580
  656.1 11.8 %copy-start.25 = (f32[8,128]{1,0:T(8,128)S(1)}, f32[8,128]{1,0:T(8,128)}, u32[]{:S(2)}) copy-start(f32[8,128]{1,0:T(8,128)} %copy-done.24) | copy-start | bytes 12292
  656.1 42.4 %copy-start.28 = (bf16[512,1536]{1,0:T(8,128)(2,1)S(1)}, bf16[512,1536]{1,0:T(8,128)(2,1)}, u32[]{:S(2)}) copy-start(bf16[512,1536]{1,0:T(8,128)(2,1)} %param.39) | copy-start | bytes 4718596
  656.1 42.3 %copy-start.38 = (f32[1536]{0:T(1024)S(1)}, f32[1536]{0:T(1024)}, u32[]{:S(2)}) copy-start(f32[1536]{0:T(1024)} %copy-done.37) | copy-start | bytes 18436
  656.1 42.3 %copy-start.52 = (f32[512]{0:T(512)S(1)}, f32[512]{0:T(512)}, u32[]{:S(2)}) copy-start(f32[512]{0:T(512)} %copy-done.51) | copy-start | bytes 6148
  666.9 31.6 %collective-permute-start.11 = (bf16[512,1536]{1,0:T(8,128)(2,1)}, bf16[512,1536]{1,0:T(8,128)(2,1)}, u32[]{:S(2)}, u32[]{:S(2)}) collective-permute-start(bf16[512,1536]{1,0:T(8,128)(2,1)} %fusion.28), channel_id=1, source_target_pairs={{0,1},{1,0},{2,3},{3,2},{4,5},{5,4},{6,7},{7,6},{8,9},{9,8},{10,11... | collective-permute-start | bytes 4718600 | tf_op jit(solution)/shard_map/ppermute | solution.py:429
  710.3 4.9 collective-permute-start.12
  715.3 2.4 collective-permute-start.13
  717.2 5.2 collective-permute-start.18
  717.8 5.5 collective-permute-start.14
  723.3 9.4 collective-permute-start.15
  732.7 10.0 collective-permute-start.16
  749.6 4.6 collective-permute-start.17
  (33 other events, 123.2 us)
Sparse Core Ops, SparseCore 0:
  12.1 91.3 all-gather.4
  106.4 51.3 all-gather.6
  160.1 87.2 all-gather.8
  249.5 51.5 all-gather.10
  505.3 60.5 reduce-scatter.12
  601.1 59.9 reduce-scatter.10
  665.0 78.3 reduce-scatter.16
  747.7 74.6 reduce-scatter.14
  826.5 110.3 reduce-scatter.8
  941.4 111.0 reduce-scatter.6

commit v2 on v1

--- a/solution.py
+++ b/solution.py
@@ -435,13 +435,59 @@
     )
 
 
+def dp_factors():
+    size = lax.axis_size("dp")
+    known = {16: (2, 2, 4), 64: (2, 4, 2, 4)}
+    return known.get(size, (size,))
+
+
+def after(v, other):
+    return lax.optimization_barrier((v, other))[0]
+
+
+def ring_scatter(arrays, marks=()):
+    size = lax.axis_size("dp")
+    index = lax.axis_index("dp")
+    stride = 1
+    state = [v.reshape((size, v.shape[0] // size) + v.shape[1:]) for v in arrays]
+    for factor in dp_factors():
+        place = (index // stride) % factor
+        hops = []
+        for i in range(size):
+            here = (i // stride) % factor
+            hops.append((i, i + ((here + 1) % factor - here) * stride))
+        previous = None
+        for n, blocks in enumerate(state):
+            outer = blocks.shape[0] // factor
+            parts = blocks.reshape((outer, factor) + blocks.shape[1:])
+
+            def pick(step):
+                return lax.dynamic_index_in_dim(parts, (place + step) % factor, 1, keepdims=False)
+
+            moving = pick(factor - 1)
+            if previous is not None and factor == 2 and stride > 1:
+                moving = after(moving, previous)
+            for step in range(factor - 1):
+                if n == len(state) - 1 and stride * factor == size and step < len(marks):
+                    moving = after(moving, marks[step])
+                arrived = lax.ppermute(moving, "dp", hops)
+                previous = arrived
+                moving = arrived.astype(f32) + pick(2 * factor - 2 - step).astype(f32)
+                moving = moving.astype(blocks.dtype)
+            state[n] = moving
+        stride *= factor
+    return [b.reshape((v.shape[0] // size,) + v.shape[1:]) for b, v in zip(state, arrays)]
+
+
 def sum_devices(v):
     span = 1
     size = lax.axis_size("dp")
+    sums = []
     while span < size:
         v = v + lax.ppermute(v, "dp", [(i, i ^ span) for i in range(size)])
+        sums.append(v)
         span *= 2
-    return v
+    return sums
 
 
 def head_lanes(v):
@@ -505,12 +551,17 @@
         params.append((conv_x[l], chan, conv_bc[l], conv_bc_bias[l][None, :], dtv))
 
     current = hidden.astype(f32)
-    cot = gather_pair(cotangent)
     saved = []
     for l in range(layers):
         w_in = in_weights[l]
         rms = lax.rsqrt(jnp.mean(current * current, axis=1, keepdims=True) + epsilon)
-        normed = gather_pair((current * rms * pre_gain[l][None, :]).astype(bf16))
+        own_normed = (current * rms * pre_gain[l][None, :]).astype(bf16)
+        if l == 0:
+            arrived = pair_swap(jnp.concatenate([own_normed, cotangent], axis=0))
+            normed = both_rows(own_normed, arrived[:own_count], first)
+            cot = both_rows(cotangent, arrived[own_count:], first)
+        else:
+            normed = gather_pair(own_normed)
         zx = mm(normed, w_in[:, : 2 * width])
         bcdt = mm(normed, w_in[:, 2 * width :])
         scaled, mixed, states, squares = mixer_forward(zx, bcdt, *params[l])
@@ -536,6 +587,7 @@
     hidden_out = current
     grad_rows = cotangent.astype(f32)
     outputs = [None] * layers
+    out_parts = [None] * layers
     packed = [None] * layers
     for l in reversed(range(layers)):
         current, rms, normed, zx, bcdt, shaped, mixed, states, inv, lifted = saved[l]
@@ -556,13 +608,34 @@
         low, gchan, gbc, gdt = mixer_backward(
             shaped_grad, zx, mixed, states, bcdt, coef, *params[l]
         )
+        if l == 0 and layers > 1:
+            low, done_in = lax.optimization_barrier((low, done_in))
         arrived = pair_swap(mm_t(other_half(low), w_in).astype(bf16))
-        normed_grad = mm_t(own_half(low), w_in) + arrived.astype(f32)
-        grad_in = t_mm(normed, low[:, : 2 * width]).astype(bf16)
-        grad_side = t_mm(normed, low[:, 2 * width :])
-        grad_out_own = lax.psum_scatter(grad_out, "dp", scatter_dimension=0, tiled=True)
-        grad_in_own = lax.psum_scatter(grad_in, "dp", scatter_dimension=0, tiled=True)
-        grad_side = lax.psum_scatter(grad_side, "dp", scatter_dimension=0, tiled=True)
+        if l > 0:
+            own = mm_t(own_half(low), w_in)
+            grad_in = t_mm(normed, low[:, : 2 * width]).astype(bf16)
+            grad_side = t_mm(normed, low[:, 2 * width :])
+            done_out = lax.psum_scatter(grad_out, "dp", scatter_dimension=0, tiled=True)
+            arrived, own, grad_in, grad_side, done_out = lax.optimization_barrier(
+                (arrived, own, grad_in, grad_side, done_out)
+            )
+            grad_out_own = done_out
+            done_in = lax.psum_scatter(grad_in, "dp", scatter_dimension=0, tiled=True)
+            grad_side_last = grad_side
+        else:
+            side_done = lax.psum_scatter(
+                after(grad_side_last, done_in), "dp", scatter_dimension=0, tiled=True
+            )
+            grad_parts = [
+                t_mm(normed, low[:, i * width : (i + 1) * width]).astype(bf16) for i in range(2)
+            ]
+            grad_side = t_mm(normed, low[:, 2 * width :])
+            own = mm_t(own_half(low), w_in)
+            arrived, own, grad_parts, grad_side = lax.optimization_barrier(
+                (arrived, own, grad_parts, grad_side)
+            )
+            grad_out_own = None
+        normed_grad = own + arrived.astype(f32)
         unit = current * rms
         weighted = normed_grad * pre_gain[l][None, :]
         grad_pre = jnp.sum(normed_grad * unit, axis=0)
@@ -571,19 +644,25 @@
         )
         gchan = gchan.at[7].set(grad_pre)
         packed[l] = jnp.concatenate([gchan, gbc, gdt], axis=1)
-        grad_in_own = grad_in_own.astype(f32)
-        grad_bc = grad_side[:, :256]
-        outputs[l] = (
-            grad_in_own.reshape(-1, 2, width),
-            grad_bc + pair_swap(grad_bc),
-            grad_side[:, 256 : 256 + heads],
-            grad_out_own.astype(f32).T,
-        )
+        out_parts[l] = grad_out_own
     small = jnp.stack(packed)
     row = lax.broadcasted_iota(jnp.int32, small.shape, 1)
     col = lax.broadcasted_iota(jnp.int32, small.shape, 2)
     shared = ((row == 7) & (col < width)) | ((col >= width) & (col < width + 256))
-    small = sum_devices(small + jnp.where(shared, pair_swap(small), 0.0))
+    sums = sum_devices(small + jnp.where(shared, pair_swap(small), 0.0))
+    small = sums[-1]
+    scattered = ring_scatter([grad_out] + grad_parts + [grad_side], sums[:-1])
+    out_parts[0] = scattered[0]
+    in_parts = [jnp.concatenate(scattered[1:3], axis=1), done_in]
+    side_parts = [scattered[3], side_done]
+    for l in range(layers):
+        grad_bc = side_parts[l][:, :256]
+        outputs[l] = (
+            in_parts[l].astype(f32).reshape(-1, 2, width),
+            grad_bc + pair_swap(grad_bc),
+            side_parts[l][:, 256 : 256 + heads],
+            out_parts[l].astype(f32).T,
+        )
     grad_w_zx, grad_w_bc, grad_w_dt, grad_w_out = (
         jnp.stack([o[i] for o in outputs]) for i in range(4)
     )

time: 1070 us -> 869 us (0.81)
  waiting for transfers between devices: 594 us -> 346 us
  starting transfers between devices: 17.9 us -> 33.8 us
  other arithmetic: 41.6 us -> 57.4 us
  local copies, waits for them, and re-layouts: 38.9 us -> 49.6 us
    reduce_scatter x6 -> x3, waiting for transfers between devices: 292 us -> 0.01 us  [the longest x1 0.01 us: local(): done_out = lax.psum_scatter(grad_out, 'dp', scatter_dimension=0, tiled=True)]
    ppermute x0 -> x20, waiting for transfers between devices: none -> 106 us  [ring_scatter(): arrived = lax.ppermute(moving, 'dp', hops)]
    ppermute x15 -> x14, waiting for transfers between devices: 239 us -> 195 us  [pair_swap(): return lax.ppermute(v, 'tensor', ((0, 1), (1, 0)))]
    all_gather x2, waiting for transfers between devices: 49 us -> 34 us  [local(): in_weights.append(lax.all_gather(shard, 'dp', axis=0, tiled=True))]
    convert_element_type x2 -> x14, other arithmetic: 3.21 us -> 18.2 us  [the longest x12 16.3 us: ring_scatter(): moving = moving.astype(blocks.dtype)]
    squeeze x0 -> x12, local copies, waits for them, and re-layouts: none -> 12.7 us  [pick(): lax.dynamic_index_in_dim(parts, (place + step) % factor, 1, keepdims=False)]
    unnamed x144 -> x159, local copies, waits for them, and re-layouts: 16.2 us -> 22.1 us
    dot_general x6 -> x7, matrix products: 68 us -> 67.5 us  [t_mm(): lax.dot_general(a, b, (((0,), (0,)), ((), ())), preferred_element_type=f32)]
  transfers between devices with their start and end apart: 29 -> 45, of which waited for: 19 -> 30; matrix products, arithmetic and copies ran while one was open for 21% -> 28% of each run, Pallas kernels for 10% -> 19%
where the time goes in v2:
time: 869 us; the launch traced here: 860 us
  waiting for transfers between devices  346 us (40%)
  matrix products  197 us (23%)
  Pallas kernels  160 us (18%)
  other arithmetic  57.4 us (7%)
  local copies, waits for them, and re-layouts  49.6 us (6%)
  starting transfers between devices  33.8 us (4%)
  between operations  16 us (2%)
    ppermute x14, waiting for transfers between devices, pair_swap(): return lax.ppermute(v, 'tensor', ((0, 1), (1, 0)))  195 us
    ppermute x20, waiting for transfers between devices, ring_scatter(): arrived = lax.ppermute(moving, 'dp', hops)  106 us
    pallas_call x2, Pallas kernels, mixer_backward(): pl.pallas_call(functools.partial(bwd_kernel, head_count=width // HEADDIM)...  103 us
    dot_general x7, matrix products, t_mm(): lax.dot_general(a, b, (((0,), (0,)), ((), ())), preferred_element_type=f32)  67.5 us
    dot_general x8, matrix products, mm_t(): lax.dot_general(a, b, (((1,), (1,)), ((), ())), preferred_element_type=f32)  65.6 us
    dot_general x6, matrix products, mm(): lax.dot_general(a, b, (((1,), (0,)), ((), ())), precision=precision, pref...  64.1 us
    pallas_call x2, Pallas kernels, mixer_forward(): pl.pallas_call(functools.partial(fwd_kernel, head_count=width // HEADDIM)...  57.3 us
    all_gather x2, waiting for transfers between devices, local(): in_weights.append(lax.all_gather(shard, 'dp', axis=0, tiled=True))  34 us
  transfers between devices with their start and end apart: 45, of which 30 were waited for; matrix products, arithmetic and copies ran while one was open for 28% of the time, Pallas kernels for 19%

profile of v2, /device:TPU:0, one launch (start us, length us, event | category | flops | bytes accessed | tf_op | source)
XLA Modules:
  0.0 860.4 jit_solution(11562242397834392509)
XLA Ops:
  17.3 3.3 pad_maximum_fusion.1
  20.6 2.9 collective-permute-start
  24.6 67.4 %collective-permute-done = bf16[1024,1536]{1,0:T(8,128)(2,1)} collective-permute-done((bf16[1024,1536]{1,0:T(8,128)(2,1)}, bf16[1024,1536]{1,0:T(8,128)(2,1)}, u32[]{:S(2)}, u32[]{:S(2)}) %collective-permute-start) | collective-permute-done | bytes 3145760 | tf_op jit(solution)/shard_map/ppermute | solution.py:429
  92.0 3.9 fusion.87
  95.9 7.6 all-gather.5.cloned.1.call-done
  103.5 5.1 fusion.51.bcdt_ref.bcprev_ref
  108.6 15.7 %fusion.2.zx_ref.xprev_ref = f32[1024,3072]{1,0:T(8,128)} fusion(bf16[1536,3456]{1,0:T(8,128)(2,1)} %all-gather.5.cloned.1.call-done, bf16[512,1536]{1,0:T(8,128)(2,1)S(1)} %copy-done.30, bf16[512,1536]{1,0:T(8,128)(2,1)S(1)} %copy-done.45, pred[]{:T(512)S(6)} %eq.168), kind=kOutput, calls=%fused_computation.3 | convolution fusion | flops 9677832192 | bytes 25165824 | tf_op jit(solution)/shard_map/dot_general | solution.py:26
  124.4 28.7 %shard_map.262 = (f32[1024,1536]{1,0:T(8,128)}, bf16[1024,1536]{1,0:T(8,128)(2,1)S(1)}, bf16[8,128,1536]{2,1,0:T(8,128)(2,1)}, f32[1024,128]{1,0:T(8,128)S(1)}) custom-call(f32[1024,3072]{1,0:T(8,128)} %fusion.2.zx_ref.xprev_ref, f32[1024,384]{1,0:T(8,128)S(1)} %fusion.51.bcdt_ref.bcprev_ref, f32[4,1536]{1,0:T(4,128)S(1)} %get-tuple-element.304.taps_ref, ...), custom_call_target="tpu_custom_call" | custom-call | flops 1207959552 | bytes 18874368 | tf_op jit(solution)/shard_map/pallas_call | solution.py:345
  158.6 5.0 multiply_convert_fusion.1
  163.6 6.8 convolution_convert_fusion.5
  171.7 34.2 %collective-permute-done.2 = bf16[512,1536]{1,0:T(8,128)(2,1)} collective-permute-done((bf16[512,1536]{1,0:T(8,128)(2,1)}, bf16[512,1536]{1,0:T(8,128)(2,1)}, u32[]{:S(2)}, u32[]{:S(2)}) %collective-permute-start.2) | collective-permute-done | bytes 1572896 | tf_op jit(solution)/shard_map/ppermute | solution.py:429
  205.9 7.9 multiply_reduce_fusion.5
  217.6 3.6 fusion.21
  221.1 26.4 %all-gather.9.cloned.1.call-done = bf16[1536,3456]{1,0:T(8,128)(2,1)} async-done(((bf16[96,3456]{1,0:T(8,128)(2,1)}), bf16[1536,3456]{1,0:T(8,128)(2,1)}) %all-gather.9.cloned.1.call-update) | async-done | bytes 10616848 | tf_op jit(solution)/shard_map/all_gather | solution.py:542
  249.9 5.6 fusion.49.bcdt_ref.bcprev_ref
  255.5 15.9 %fusion.zx_ref.xprev_ref = f32[1024,3072]{1,0:T(8,128)} fusion(bf16[1536,3456]{1,0:T(8,128)(2,1)S(1)} %copy-done.67, bf16[512,1536]{1,0:T(8,128)(2,1)} %collective-permute-done.3, bf16[512,1536]{1,0:T(8,128)(2,1)} %multiply_convert_fusion.2, pred[]{:T(512)S(6)} %eq.168), kind=kOutput, calls=%fused_computation.1 | convolution fusion | flops 9677832192 | bytes 25165824 | tf_op jit(solution)/shard_map/dot_general | solution.py:26
  271.4 28.6 %shard_map.263 = (f32[1024,1536]{1,0:T(8,128)}, bf16[1024,1536]{1,0:T(8,128)(2,1)S(1)}, bf16[8,128,1536]{2,1,0:T(8,128)(2,1)}, f32[1024,128]{1,0:T(8,128)S(1)}) custom-call(f32[1024,3072]{1,0:T(8,128)} %fusion.zx_ref.xprev_ref, f32[1024,384]{1,0:T(8,128)S(1)} %fusion.49.bcdt_ref.bcprev_ref, f32[4,1536]{1,0:T(4,128)S(1)} %get-tuple-element.303.taps_ref, ...), custom_call_target="tpu_custom_call" | custom-call | flops 1207959552 | bytes 18874368 | tf_op jit(solution)/shard_map/pallas_call | solution.py:345
  303.5 9.8 %fusion.94.sg_ref = f32[1024,1536]{1,0:T(8,128)} fusion(bf16[1024,1536]{1,0:T(8,128)(2,1)} %fusion.21, bf16[1536,1536]{1,0:T(8,128)(2,1)} %all-gather.11.cloned.1.call-done), kind=kOutput, calls=%fused_computation.208 | convolution fusion | flops 4831838208 | bytes 14155776 | tf_op jit(solution)/shard_map/dot_general | solution.py:26
  316.4 15.9 %convolution_convert_fusion.4 = bf16[1536,1536]{1,0:T(8,128)(2,1)} fusion(bf16[1024,1536]{1,0:T(8,128)(2,1)S(1)} %copy-done.39, bf16[1024,1536]{1,0:T(8,128)(2,1)S(1)} %multiply_convert_fusion), kind=kOutput, calls=%fused_computation.8 | convolution fusion | flops 4834197504 | bytes 11010048 | tf_op jit(solution)/shard_map/dot_general | solution.py:36
  332.3 5.1 fusion.40
  337.5 7.1 multiply_reduce_fusion.4
  345.3 3.0 collective-permute-done.6
  350.6 51.2 %shard_map.264 = (bf16[1024,3456]{1,0:T(8,128)(2,1)}, f32[8,1536]{1,0:T(8,128)S(1)}, f32[8,256]{1,0:T(8,128)S(1)}, f32[8,128]{1,0:T(8,128)S(1)}) custom-call(f32[1024,1536]{1,0:T(8,128)} %fusion.94.sg_ref, f32[1024,3072]{1,0:T(8,128)} %fusion.zx_ref.xprev_ref, f32[1024,3072]{1,0:T(8,128)} %fusion.zx_ref.xprev_ref, bf16[1024,1536]{1,0:T(8,128)(2,1)S(1)} %copy-done.5, ...), custom_call_target="tpu_custom_call" | custom-call | flops 4026531840 | bytes 31457280 | tf_op jit(solution)/shard_map/pallas_call | solution.py:385
  401.8 10.8 %fusion.31 = bf16[512,1536]{1,0:T(8,128)(2,1)} fusion(bf16[1536,3456]{1,0:T(8,128)(2,1)} %all-gather.9.cloned.1.call-done, bf16[1024,3456]{1,0:T(8,128)(2,1)} %get-tuple-element.200, s32[]{:T(128)S(6)} %select_n.256), kind=kOutput, calls=%fused_computation.61 | convolution fusion | flops 5436604416 | bytes 15728644 | tf_op jit(solution)/shard_map/dot_general | solution.py:32
  413.3 15.6 %convolution_convert_fusion = bf16[1536,3072]{1,0:T(8,128)(2,1)} fusion(bf16[1024,3456]{1,0:T(8,128)(2,1)S(1)} %copy-done.68, bf16[512,1536]{1,0:T(8,128)(2,1)} %collective-permute-done.3, bf16[512,1536]{1,0:T(8,128)(2,1)} %multiply_convert_fusion.2, pred[]{:T(512)S(6)} %eq.168), kind=kOutput, calls=%fused_computation | convolution fusion | flops 9682550784 | bytes 18874368 | tf_op jit(solution)/shard_map/dot_general | solution.py:36
  428.9 6.4 fusion.55
  435.3 10.9 %fusion.16 = f32[512,1536]{1,0:T(8,128)} fusion(bf16[1536,3456]{1,0:T(8,128)(2,1)} %all-gather.9.cloned.1.call-done, bf16[1024,3456]{1,0:T(8,128)(2,1)} %get-tuple-element.200, s32[]{:T(128)S(6)} %select_n.255), kind=kOutput, calls=%fused_computation.32 | convolution fusion | flops 5435817984 | bytes 17301508 | tf_op jit(solution)/shard_map/dot_general | solution.py:32
  447.8 4.9 multiply_reduce_fusion
  452.6 27.6 %collective-permute-done.5 = bf16[512,1536]{1,0:T(8,128)(2,1)S(1)} collective-permute-done((bf16[512,1536]{1,0:T(8,128)(2,1)}, bf16[512,1536]{1,0:T(8,128)(2,1)S(1)}, u32[]{:S(2)}, u32[]{:S(2)}) %collective-permute-start.5) | collective-permute-done | bytes 1572896 | tf_op jit(solution)/shard_map/ppermute | solution.py:429
  480.3 6.9 multiply_reduce_fusion.1
  488.1 32.2 %collective-permute-done.8 = bf16[512,1536]{1,0:T(8,128)(2,1)S(1)} collective-permute-done((bf16[512,1536]{1,0:T(8,128)(2,1)}, bf16[512,1536]{1,0:T(8,128)(2,1)S(1)}, u32[]{:S(2)}, u32[]{:S(2)}) %collective-permute-start.8) | collective-permute-done | bytes 1572896 | tf_op jit(solution)/shard_map/ppermute | solution.py:429
  520.3 8.3 convolution_convert_fusion.1
  531.1 4.6 collective-permute-done.17
  535.7 3.0 fusion.10
  541.6 3.1 collective-permute-done.9
  544.8 23.3 %collective-permute-done.18 = bf16[4,96,1536]{2,1,0:T(8,128)(2,1)} collective-permute-done((bf16[4,96,1536]{2,1,0:T(8,128)(2,1)}, bf16[4,96,1536]{2,1,0:T(8,128)(2,1)}, u32[]{:S(2)}, u32[]{:S(2)}) %collective-permute-start.18) | collective-permute-done | bytes 1179680 | tf_op jit(solution)/shard_map/ppermute | solution.py:473
  572.9 8.0 collective-permute-done.35
  582.0 12.0 %fusion.62.sg_ref = f32[1024,1536]{1,0:T(8,128)} fusion(bf16[1536,1536]{1,0:T(8,128)(2,1)} %all-gather.7.cloned.1.call-done, bf16[512,1536]{1,0:T(8,128)(2,1)} %copy-done.69, bf16[512,1536]{1,0:T(8,128)(2,1)} %get-tuple-element.283, pred[]{:T(512)S(6)} %eq.168), kind=kOutput, calls=%fused_computation.117 | convolution fusion | flops 4845993984 | bytes 14155777 | tf_op jit(solution)/shard_map/dot_general | solution.py:26
  595.7 51.3 %shard_map.265 = (bf16[1024,3456]{1,0:T(8,128)(2,1)}, f32[8,1536]{1,0:T(8,128)S(1)}, f32[8,256]{1,0:T(8,128)S(1)}, f32[8,128]{1,0:T(8,128)S(1)}) custom-call(f32[1024,1536]{1,0:T(8,128)} %fusion.62.sg_ref, f32[1024,3072]{1,0:T(8,128)} %fusion.2.zx_ref.xprev_ref, f32[1024,3072]{1,0:T(8,128)} %fusion.2.zx_ref.xprev_ref, bf16[1024,1536]{1,0:T(8,128)(2,1)S(1)} %copy-done.3, ...), custom_call_target="tpu_custom_call" | custom-call | flops 4026531840 | bytes 31457280 | tf_op jit(solution)/shard_map/pallas_call | solution.py:385
  648.2 9.3 %convolution_convert_fusion.2 = bf16[1536,1536]{1,0:T(8,128)(2,1)} fusion(bf16[1024,3456]{1,0:T(8,128)(2,1)} %get-tuple-element.207, bf16[512,1536]{1,0:T(8,128)(2,1)S(1)} %copy-done.31, bf16[512,1536]{1,0:T(8,128)(2,1)} %get-tuple-element.290, pred[]{:T(512)S(6)} %eq.168), kind=kOutput, calls=%fused_computation.6 | convolution fusion | flops 4848353280 | bytes 11010049 | tf_op jit(solution)/shard_map/dot_general | solution.py:36
  657.5 8.9 %convolution_convert_fusion.3 = bf16[1536,1536]{1,0:T(8,128)(2,1)} fusion(bf16[1024,3456]{1,0:T(8,128)(2,1)} %get-tuple-element.207, bf16[512,1536]{1,0:T(8,128)(2,1)S(1)} %copy-done.31, bf16[512,1536]{1,0:T(8,128)(2,1)S(1)} %copy-done.46, pred[]{:T(512)S(6)} %eq.168), kind=kOutput, calls=%fused_computation.7 | convolution fusion | flops 4848353280 | bytes 11010049 | tf_op jit(solution)/shard_map/dot_general | solution.py:36
  666.4 7.2 fusion.34
  674.7 3.1 fusion.53
  678.4 9.8 %fusion.12 = f32[512,1536]{1,0:T(8,128)S(1)} fusion(bf16[1536,3456]{1,0:T(8,128)(2,1)} %all-gather.5.cloned.1.call-done, bf16[1024,3456]{1,0:T(8,128)(2,1)} %get-tuple-element.207, s32[]{:T(128)S(6)} %select_n.255), kind=kOutput, calls=%fused_computation.28 | convolution fusion | flops 5435817984 | bytes 17301508 | tf_op jit(solution)/shard_map/dot_general | solution.py:32
  688.2 20.1 %collective-permute-done.10 = bf16[512,1536]{1,0:T(8,128)(2,1)} collective-permute-done((bf16[512,1536]{1,0:T(8,128)(2,1)}, bf16[512,1536]{1,0:T(8,128)(2,1)}, u32[]{:S(2)}, u32[]{:S(2)}) %collective-permute-start.10) | collective-permute-done | bytes 1572896 | tf_op jit(solution)/shard_map/ppermute | solution.py:429
  712.2 3.2 dynamic-slice_bitcast_fusion.2
  717.8 2.5 collective-permute-done.12
  721.2 3.2 dynamic-slice_bitcast_fusion
  727.5 4.9 collective-permute-done.14
  732.4 3.0 collective-permute-start.15
  735.5 4.2 fusion.26
  739.7 2.5 collective-permute-done.15
  747.2 3.2 fusion.11
  759.2 3.0 fusion.9
  763.3 15.5 %collective-permute-done.19 = bf16[4,96,1536]{2,1,0:T(8,128)(2,1)} collective-permute-done((bf16[4,96,1536]{2,1,0:T(8,128)(2,1)}, bf16[4,96,1536]{2,1,0:T(8,128)(2,1)}, u32[]{:S(2)}, u32[]{:S(2)}) %collective-permute-start.19) | collective-permute-done | bytes 1179680 | tf_op jit(solution)/shard_map/ppermute | solution.py:473
  784.0 8.7 %collective-permute-done.20 = bf16[1,96,1536]{2,1,0:T(8,128)(2,1)} collective-permute-done((bf16[1,96,1536]{2,1,0:T(8,128)(2,1)}, bf16[1,96,1536]{2,1,0:T(8,128)(2,1)}, u32[]{:S(2)}, u32[]{:S(2)}) %collective-permute-start.20) | collective-permute-done | bytes 294944 | tf_op jit(solution)/shard_map/ppermute | solution.py:473
  793.9 10.6 %collective-permute-done.24 = bf16[4,96,1536]{2,1,0:T(8,128)(2,1)} collective-permute-done((bf16[4,96,1536]{2,1,0:T(8,128)(2,1)}, bf16[4,96,1536]{2,1,0:T(8,128)(2,1)}, u32[]{:S(2)}, u32[]{:S(2)}) %collective-permute-start.24) | collective-permute-done | bytes 1179680 | tf_op jit(solution)/shard_map/ppermute | solution.py:473
  808.1 9.8 %collective-permute-done.25 = bf16[1,96,1536]{2,1,0:T(8,128)(2,1)S(1)} collective-permute-done((bf16[1,96,1536]{2,1,0:T(8,128)(2,1)S(1)}, bf16[1,96,1536]{2,1,0:T(8,128)(2,1)S(1)}, u32[]{:S(2)}, u32[]{:S(2)}) %collective-permute-start.25) | collective-permute-done | bytes 294944 | tf_op jit(solution)/shard_map/ppermute | solution.py:473
  818.4 10.6 %collective-permute-done.26 = bf16[1,96,1536]{2,1,0:T(8,128)(2,1)S(1)} collective-permute-done((bf16[1,96,1536]{2,1,0:T(8,128)(2,1)S(1)}, bf16[1,96,1536]{2,1,0:T(8,128)(2,1)S(1)}, u32[]{:S(2)}, u32[]{:S(2)}) %collective-permute-start.26) | collective-permute-done | bytes 294944 | tf_op jit(solution)/shard_map/ppermute | solution.py:473
  829.1 3.0 collective-permute-done.30
  832.6 8.1 collective-permute-done.31
  841.0 3.2 copy.68
  844.3 3.4 collective-permute-done.32
  849.9 2.6 collective-permute-done.33
  (355 shorter events, 91.0 us)
Async XLA Ops:
  7.2 96.3 %all-gather.5.cloned.1.call-start = ((), (), s32[]{:S(2)}) async-start(), calls=%async_computation.3 | async-start | bytes 11280384 | tf_op jit(solution)/shard_map/all_gather | solution.py:542
  11.9 151.7 %all-gather.7.cloned.1.call-start = ((), (), s32[]{:S(2)}) async-start(), calls=%async_computation.4 | async-start | bytes 5013504 | tf_op jit(solution)/shard_map/all_gather | solution.py:543
  13.9 233.6 %all-gather.9.cloned.1.call-start = ((), (), s32[]{:S(2)}) async-start(), calls=%async_computation.5 | async-start | bytes 11280384 | tf_op jit(solution)/shard_map/all_gather | solution.py:542
  15.1 288.3 %all-gather.11.cloned.1.call-start = ((), (), s32[]{:S(2)}) async-start(), calls=%async_computation.6 | async-start | bytes 5013504 | tf_op jit(solution)/shard_map/all_gather | solution.py:543
  20.6 71.4 %collective-permute-start = (bf16[1024,1536]{1,0:T(8,128)(2,1)}, bf16[1024,1536]{1,0:T(8,128)(2,1)}, u32[]{:S(2)}, u32[]{:S(2)}) collective-permute-start(bf16[1024,1536]{1,0:T(8,128)(2,1)} %pad_maximum_fusion.1), channel_id=1, source_target_pairs={{0,1},{1,0},{2,3},{3,2},{4,5},{5,4},{6,7},{7,6},{8,9},{9,8},{10,11... | collective-permute-start | bytes 9437192 | tf_op jit(solution)/shard_map/ppermute | solution.py:429
  23.9 100.4 %copy-start.10 = (f32[8,128]{1,0:T(8,128)}, f32[8,128]{1,0:T(8,128)S(1)}, u32[]{:S(2)}) copy-start(f32[8,128]{1,0:T(8,128)S(1)} %scatter.46.dtv_ref) | copy-start | bytes 12292
  24.3 100.1 %copy-start.6 = (f32[8,1536]{1,0:T(8,128)}, f32[8,1536]{1,0:T(8,128)S(1)}, u32[]{:S(2)}) copy-start(f32[8,1536]{1,0:T(8,128)S(1)} %scatter.44.chan_ref) | copy-start | bytes 147460
  24.3 100.0 %copy-start.14 = (f32[1,256]{1,0:T(1,128)}, f32[1,256]{1,0:T(1,128)S(1)}, u32[]{:S(2)}) copy-start(f32[1,256]{1,0:T(1,128)S(1)} %get-tuple-element.314.bcb_ref) | copy-start | bytes 3076
  24.4 100.0 %copy-start.12 = (f32[4,256]{1,0:T(4,128)}, f32[4,256]{1,0:T(4,128)S(1)}, u32[]{:S(2)}) copy-start(f32[4,256]{1,0:T(4,128)S(1)} %get-tuple-element.312.bct_ref) | copy-start | bytes 12292
  24.4 100.0 %copy-start.8 = (f32[4,1536]{1,0:T(4,128)}, f32[4,1536]{1,0:T(4,128)S(1)}, u32[]{:S(2)}) copy-start(f32[4,1536]{1,0:T(4,128)S(1)} %get-tuple-element.304.taps_ref) | copy-start | bytes 73732
  154.9 3.7 collective-permute-start.1
  156.5 289.9 %reduce-scatter.4.cloned.1.call-start = ((), (), s32[]{:S(2)}) async-start(), calls=%async_computation.7 | async-start | bytes 5013504 | tf_op jit(solution)/shard_map/reduce_scatter | solution.py:618
  170.4 35.6 %collective-permute-start.2 = (bf16[512,1536]{1,0:T(8,128)(2,1)}, bf16[512,1536]{1,0:T(8,128)(2,1)}, u32[]{:S(2)}, u32[]{:S(2)}) collective-permute-start(bf16[512,1536]{1,0:T(8,128)(2,1)} %convolution_convert_fusion.5), channel_id=1, source_target_pairs={{0,1},{1,0},{2,3},{3,2},{4,5},{5,4},{6,7},{7,6},{8,9},{9,8},{10,11... | collective-permute-start | bytes 4718600 | tf_op jit(solution)/shard_map/ppermute | solution.py:429
  215.3 34.6 %collective-permute-start.3 = (bf16[512,1536]{1,0:T(8,128)(2,1)}, bf16[512,1536]{1,0:T(8,128)(2,1)}, u32[]{:S(2)}, u32[]{:S(2)}) collective-permute-start(bf16[512,1536]{1,0:T(8,128)(2,1)} %multiply_convert_fusion.2), channel_id=1, source_target_pairs={{0,1},{1,0},{2,3},{3,2},{4,5},{5,4},{6,7},{7,6},{8,9},{9,8},{10,11... | collective-permute-start | bytes 4718600 | tf_op jit(solution)/shard_map/ppermute | solution.py:429
  301.9 11.4 %collective-permute-start.4 = (f32[8,128]{1,0:T(8,128)S(1)}, f32[8,128]{1,0:T(8,128)S(1)}, u32[]{:S(2)}, u32[]{:S(2)}) collective-permute-start(f32[8,128]{1,0:T(8,128)S(1)} %bitcast.200), channel_id=1, source_target_pairs={{0,1},{1,0},{2,3},{3,2},{4,5},{5,4},{6,7},{7,6},{8,9},{9,8},{10,11... | collective-permute-start | bytes 12296 | tf_op jit(solution)/shard_map/ppermute | solution.py:429
  332.3 315.9 %reduce-scatter.6.cloned.1.call-start = ((), (), s32[]{:S(2)}) async-start(), calls=%async_computation.8 | async-start | bytes 10027008 | tf_op jit(solution)/shard_map/reduce_scatter | solution.py:623
  344.6 3.7 collective-permute-start.6
  412.6 33.7 %collective-permute-start.7 = (bf16[512,1536]{1,0:T(8,128)(2,1)}, bf16[512,1536]{1,0:T(8,128)(2,1)S(1)}, u32[]{:S(2)}, u32[]{:S(2)}) collective-permute-start(bf16[512,1536]{1,0:T(8,128)(2,1)} %fusion.31), channel_id=1, source_target_pairs={{0,1},{1,0},{2,3},{3,2},{4,5},{5,4},{6,7},{7,6},{8,9},{9,8},{10,11... | collective-permute-start | bytes 4718600 | tf_op jit(solution)/shard_map/ppermute | solution.py:429
  446.4 310.9 %reduce-scatter.8.cloned.1.call-start = ((), (), s32[]{:S(2)}) async-start(), calls=%async_computation.9 | async-start | bytes 2506752 | tf_op jit(solution)/shard_map/reduce_scatter | solution.py:626
  446.4 33.8 %copy-start.17 = (f32[512,1536]{1,0:T(8,128)S(1)}, f32[512,1536]{1,0:T(8,128)}, u32[]{:S(2)}) copy-start(f32[512,1536]{1,0:T(8,128)} %copy-done.16) | copy-start | bytes 9437188
  446.4 33.8 %copy-start.21 = (bf16[512,1536]{1,0:T(8,128)(2,1)S(1)}, bf16[512,1536]{1,0:T(8,128)(2,1)}, u32[]{:S(2)}) copy-start(bf16[512,1536]{1,0:T(8,128)(2,1)} %param.53) | copy-start | bytes 4718596
  446.5 33.8 %copy-start.24 = (f32[512,1536]{1,0:T(8,128)S(1)}, f32[512,1536]{1,0:T(8,128)}, u32[]{:S(2)}) copy-start(f32[512,1536]{1,0:T(8,128)} %fusion.16) | copy-start | bytes 9437188
  446.5 33.8 %collective-permute-start.5 = (bf16[512,1536]{1,0:T(8,128)(2,1)}, bf16[512,1536]{1,0:T(8,128)(2,1)S(1)}, u32[]{:S(2)}, u32[]{:S(2)}) collective-permute-start(bf16[512,1536]{1,0:T(8,128)(2,1)} %get-tuple-element.288), channel_id=1, source_target_pairs={{0,1},{1,0},{2,3},{3,2},{4,5},{5,4},{6,7},{7,6},{8,9},{9,8},{10,11... | collective-permute-start | bytes 4718600 | tf_op jit(solution)/shard_map/ppermute | solution.py:429
  487.2 33.2 %collective-permute-start.8 = (bf16[512,1536]{1,0:T(8,128)(2,1)}, bf16[512,1536]{1,0:T(8,128)(2,1)S(1)}, u32[]{:S(2)}, u32[]{:S(2)}) collective-permute-start(bf16[512,1536]{1,0:T(8,128)(2,1)} %get-tuple-element.283), channel_id=1, source_target_pairs={{0,1},{1,0},{2,3},{3,2},{4,5},{5,4},{6,7},{7,6},{8,9},{9,8},{10,11... | collective-permute-start | bytes 4718600 | tf_op jit(solution)/shard_map/ppermute | solution.py:429
  531.0 4.7 collective-permute-start.17
  539.8 28.3 %collective-permute-start.18 = (bf16[4,96,1536]{2,1,0:T(8,128)(2,1)}, bf16[4,96,1536]{2,1,0:T(8,128)(2,1)}, u32[]{:S(2)}, u32[]{:S(2)}) collective-permute-start(bf16[4,96,1536]{2,1,0:T(8,128)(2,1)} %dynamic-slice_bitcast_fusion.5), channel_id=1, source_target_pairs={{0,4},{2,6},{4,0},{6,2},{8,12},{10,14},{12,8},{14,10},{16,20},{18,... | collective-permute-start | bytes 3538952 | tf_op jit(solution)/shard_map/ppermute | solution.py:473
  541.1 3.6 collective-permute-start.9
  570.7 10.1 %collective-permute-start.35 = (bf16[1,96,1536]{2,1,0:T(8,128)(2,1)S(1)}, bf16[1,96,1536]{2,1,0:T(8,128)(2,1)S(1)}, u32[]{:S(2)}, u32[]{:S(2)}) collective-permute-start(bf16[1,96,1536]{2,1,0:T(8,128)(2,1)S(1)} %constant_dynamic-slice_fusion), channel_id=1, source_target_pairs={{0,8},{2,10},{4,12},{6,14},{8,16},{10,18},{12,20},{14,22},{16,24},... | collective-permute-start | bytes 884744 | tf_op jit(solution)/shard_map/ppermute | solution.py:473
  581.9 12.1 %collective-permute-start.36 = (bf16[1,96,1536]{2,1,0:T(8,128)(2,1)S(1)}, bf16[1,96,1536]{2,1,0:T(8,128)(2,1)S(1)}, u32[]{:S(2)}, u32[]{:S(2)}) collective-permute-start(bf16[1,96,1536]{2,1,0:T(8,128)(2,1)S(1)} %add_convert_fusion.2), channel_id=1, source_target_pairs={{0,8},{2,10},{4,12},{6,14},{8,16},{10,18},{12,20},{14,22},{16,24},... | collective-permute-start | bytes 884744 | tf_op jit(solution)/shard_map/ppermute | solution.py:473
  594.1 52.9 %collective-permute-start.37 = (bf16[1,96,1536]{2,1,0:T(8,128)(2,1)S(1)}, bf16[1,96,1536]{2,1,0:T(8,128)(2,1)S(1)}, u32[]{:S(2)}, u32[]{:S(2)}) collective-permute-start(bf16[1,96,1536]{2,1,0:T(8,128)(2,1)S(1)} %add_convert_fusion.1), channel_id=1, source_target_pairs={{0,8},{2,10},{4,12},{6,14},{8,16},{10,18},{12,20},{14,22},{16,24},... | collective-permute-start | bytes 884744 | tf_op jit(solution)/shard_map/ppermute | solution.py:473
  595.7 51.4 %copy-start.49 = (bf16[96,1536]{1,0:T(8,128)(2,1)S(1)}, bf16[96,1536]{1,0:T(8,128)(2,1)}, u32[]{:S(2)}) copy-start(bf16[96,1536]{1,0:T(8,128)(2,1)} %reduce-scatter.4.cloned.1.call-done) | copy-start | bytes 884740
  595.7 52.5 %copy-start.31 = (bf16[512,1536]{1,0:T(8,128)(2,1)S(1)}, bf16[512,1536]{1,0:T(8,128)(2,1)}, u32[]{:S(2)}) copy-start(bf16[512,1536]{1,0:T(8,128)(2,1)} %copy-done.29) | copy-start | bytes 4718596
  673.6 34.7 %collective-permute-start.10 = (bf16[512,1536]{1,0:T(8,128)(2,1)}, bf16[512,1536]{1,0:T(8,128)(2,1)}, u32[]{:S(2)}, u32[]{:S(2)}) collective-permute-start(bf16[512,1536]{1,0:T(8,128)(2,1)} %fusion.34), channel_id=1, source_target_pairs={{0,1},{1,0},{2,3},{3,2},{4,5},{5,4},{6,7},{7,6},{8,9},{9,8},{10,11... | collective-permute-start | bytes 4718600 | tf_op jit(solution)/shard_map/ppermute | solution.py:429
  678.4 30.0 %copy-start.19 = (bf16[512,1536]{1,0:T(8,128)(2,1)S(1)}, bf16[512,1536]{1,0:T(8,128)(2,1)}, u32[]{:S(2)}) copy-start(bf16[512,1536]{1,0:T(8,128)(2,1)} %param.39) | copy-start | bytes 4718596
  678.4 29.9 %copy-start.51 = (f32[1536]{0:T(1024)S(1)}, f32[1536]{0:T(1024)}, u32[]{:S(2)}) copy-start(f32[1536]{0:T(1024)} %copy-done.50) | copy-start | bytes 18436
  678.4 29.9 %copy-start.56 = (f32[512]{0:T(512)S(1)}, f32[512]{0:T(512)}, u32[]{:S(2)}) copy-start(f32[512]{0:T(512)} %copy-done.55) | copy-start | bytes 6148
  688.2 22.7 %copy-start.22 = (f32[512,1536]{1,0:T(8,128)}, f32[512,1536]{1,0:T(8,128)S(1)}, u32[]{:S(2)}) copy-start(f32[512,1536]{1,0:T(8,128)S(1)} %fusion.12) | copy-start | bytes 9437188
  711.1 4.9 collective-permute-start.11
  715.5 31.8 %collective-permute-start.16 = (bf16[8,96,1536]{2,1,0:T(8,128)(2,1)}, bf16[8,96,1536]{2,1,0:T(8,128)(2,1)}, u32[]{:S(2)}, u32[]{:S(2)}) collective-permute-start(bf16[8,96,1536]{2,1,0:T(8,128)(2,1)} %dynamic-slice_bitcast_fusion.2), channel_id=1, source_target_pairs={{0,2},{2,0},{4,6},{6,4},{8,10},{10,8},{12,14},{14,12},{16,18},{18,... | collective-permute-start | bytes 7077896 | tf_op jit(solution)/shard_map/ppermute | solution.py:473
  716.2 4.2 collective-permute-start.12
  716.2 19.2 %copy-start.25 = (f32[512,1536]{1,0:T(8,128)S(1)}, f32[512,1536]{1,0:T(8,128)}, u32[]{:S(2)}) copy-start(f32[512,1536]{1,0:T(8,128)} %get-tuple-element.284) | copy-start | bytes 9437188
  717.3 36.6 %collective-permute-start.28 = (f32[8,96,384]{2,1,0:T(8,128)}, f32[8,96,384]{2,1,0:T(8,128)}, u32[]{:S(2)}, u32[]{:S(2)}) collective-permute-start(f32[8,96,384]{2,1,0:T(8,128)} %dynamic-slice_bitcast_fusion.3), channel_id=1, source_target_pairs={{0,2},{2,0},{4,6},{6,4},{8,10},{10,8},{12,14},{14,12},{16,18},{18,... | collective-permute-start | bytes 3538952 | tf_op jit(solution)/shard_map/ppermute | solution.py:473
  720.5 5.4 collective-permute-start.13
  724.4 34.7 %collective-permute-start.23 = (bf16[8,96,1536]{2,1,0:T(8,128)(2,1)}, bf16[8,96,1536]{2,1,0:T(8,128)(2,1)}, u32[]{:S(2)}, u32[]{:S(2)}) collective-permute-start(bf16[8,96,1536]{2,1,0:T(8,128)(2,1)} %dynamic-slice_bitcast_fusion), channel_id=1, source_target_pairs={{0,2},{2,0},{4,6},{6,4},{8,10},{10,8},{12,14},{14,12},{16,18},{18,... | collective-permute-start | bytes 7077896 | tf_op jit(solution)/shard_map/ppermute | solution.py:473
  725.9 6.5 collective-permute-start.14
  732.4 9.7 %collective-permute-start.15 = (f32[2,8,1920]{2,1,0:T(8,128)S(1)}, f32[2,8,1920]{2,1,0:T(8,128)S(1)}, u32[]{:S(2)}, u32[]{:S(2)}) collective-permute-start(f32[2,8,1920]{2,1,0:T(8,128)S(1)} %add.447), channel_id=1, source_target_pairs={{0,16},{2,18},{4,20},{6,22},{8,24},{10,26},{12,28},{14,30},{16,0},... | collective-permute-start | bytes 368648 | tf_op jit(solution)/shard_map/ppermute | solution.py:487
  753.0 25.8 %collective-permute-start.19 = (bf16[4,96,1536]{2,1,0:T(8,128)(2,1)}, bf16[4,96,1536]{2,1,0:T(8,128)(2,1)}, u32[]{:S(2)}, u32[]{:S(2)}) collective-permute-start(bf16[4,96,1536]{2,1,0:T(8,128)(2,1)} %dynamic-slice_bitcast_fusion.6), channel_id=1, source_target_pairs={{0,4},{2,6},{4,0},{6,2},{8,12},{10,14},{12,8},{14,10},{16,20},{18,... | collective-permute-start | bytes 3538952 | tf_op jit(solution)/shard_map/ppermute | solution.py:473
  758.2 22.4 %copy-start.27 = (bf16[8,96,1536]{2,1,0:T(8,128)(2,1)S(1)}, bf16[8,96,1536]{2,1,0:T(8,128)(2,1)}, u32[]{:S(2)}) copy-start(bf16[8,96,1536]{2,1,0:T(8,128)(2,1)} %copy-done.26) | copy-start | bytes 7077892
  758.2 25.8 %collective-permute-start.34 = (f32[96,256]{1,0:T(8,128)S(1)}, f32[96,256]{1,0:T(8,128)S(1)}, u32[]{:S(2)}, u32[]{:S(2)}) collective-permute-start(f32[96,256]{1,0:T(8,128)S(1)} %slice.386), channel_id=1, source_target_pairs={{0,1},{1,0},{2,3},{3,2},{4,5},{5,4},{6,7},{7,6},{8,9},{9,8},{10,11... | collective-permute-start | bytes 294920 | tf_op jit(solution)/shard_map/ppermute | solution.py:429
  762.2 21.7 %copy-start.48 = (f32[96,384]{1,0:T(8,128)S(1)}, f32[96,384]{1,0:T(8,128)}, u32[]{:S(2)}) copy-start(f32[96,384]{1,0:T(8,128)} %reduce-scatter.8.cloned.1.call-done) | copy-start | bytes 442372
  778.8 25.7 %collective-permute-start.24 = (bf16[4,96,1536]{2,1,0:T(8,128)(2,1)}, bf16[4,96,1536]{2,1,0:T(8,128)(2,1)}, u32[]{:S(2)}, u32[]{:S(2)}) collective-permute-start(bf16[4,96,1536]{2,1,0:T(8,128)(2,1)} %dynamic-slice_bitcast_fusion.4), channel_id=1, source_target_pairs={{0,4},{2,6},{4,0},{6,2},{8,12},{10,14},{12,8},{14,10},{16,20},{18,... | collective-permute-start | bytes 3538952 | tf_op jit(solution)/shard_map/ppermute | solution.py:473
  783.9 8.8 %collective-permute-start.20 = (bf16[1,96,1536]{2,1,0:T(8,128)(2,1)}, bf16[1,96,1536]{2,1,0:T(8,128)(2,1)}, u32[]{:S(2)}, u32[]{:S(2)}) collective-permute-start(bf16[1,96,1536]{2,1,0:T(8,128)(2,1)} %constant_dynamic-slice_fusion.3), channel_id=1, source_target_pairs={{0,8},{2,10},{4,12},{6,14},{8,16},{10,18},{12,20},{14,22},{16,24},... | collective-permute-start | bytes 884744 | tf_op jit(solution)/shard_map/ppermute | solution.py:473
  784.0 24.0 %copy-start.34 = (bf16[4,96,1536]{2,1,0:T(8,128)(2,1)S(1)}, bf16[4,96,1536]{2,1,0:T(8,128)(2,1)}, u32[]{:S(2)}) copy-start(bf16[4,96,1536]{2,1,0:T(8,128)(2,1)} %copy-done.33) | copy-start | bytes 3538948
  793.8 24.4 %copy-start.38 = (f32[8,96,384]{2,1,0:T(8,128)S(1)}, f32[8,96,384]{2,1,0:T(8,128)}, u32[]{:S(2)}) copy-start(f32[8,96,384]{2,1,0:T(8,128)} %copy-done.37) | copy-start | bytes 3538948
  793.9 14.1 %collective-permute-start.21 = (bf16[1,96,1536]{2,1,0:T(8,128)(2,1)S(1)}, bf16[1,96,1536]{2,1,0:T(8,128)(2,1)S(1)}, u32[]{:S(2)}, u32[]{:S(2)}) collective-permute-start(bf16[1,96,1536]{2,1,0:T(8,128)(2,1)S(1)} %add_convert_fusion.8), channel_id=1, source_target_pairs={{0,8},{2,10},{4,12},{6,14},{8,16},{10,18},{12,20},{14,22},{16,24},... | collective-permute-start | bytes 884744 | tf_op jit(solution)/shard_map/ppermute | solution.py:473
  806.1 11.8 %collective-permute-start.25 = (bf16[1,96,1536]{2,1,0:T(8,128)(2,1)S(1)}, bf16[1,96,1536]{2,1,0:T(8,128)(2,1)S(1)}, u32[]{:S(2)}, u32[]{:S(2)}) collective-permute-start(bf16[1,96,1536]{2,1,0:T(8,128)(2,1)S(1)} %constant_dynamic-slice_fusion.2), channel_id=1, source_target_pairs={{0,8},{2,10},{4,12},{6,14},{8,16},{10,18},{12,20},{14,22},{16,24},... | collective-permute-start | bytes 884744 | tf_op jit(solution)/shard_map/ppermute | solution.py:473
  806.1 12.1 %collective-permute-start.29 = (f32[4,96,384]{2,1,0:T(8,128)}, f32[4,96,384]{2,1,0:T(8,128)S(1)}, u32[]{:S(2)}, u32[]{:S(2)}) collective-permute-start(f32[4,96,384]{2,1,0:T(8,128)} %dynamic-slice_bitcast_fusion.7), channel_id=1, source_target_pairs={{0,4},{2,6},{4,0},{6,2},{8,12},{10,14},{12,8},{14,10},{16,20},{18,... | collective-permute-start | bytes 1769480 | tf_op jit(solution)/shard_map/ppermute | solution.py:473
  808.0 24.4 %collective-permute-start.22 = (bf16[1,96,1536]{2,1,0:T(8,128)(2,1)S(1)}, bf16[1,96,1536]{2,1,0:T(8,128)(2,1)S(1)}, u32[]{:S(2)}, u32[]{:S(2)}) collective-permute-start(bf16[1,96,1536]{2,1,0:T(8,128)(2,1)S(1)} %add_convert_fusion.7), channel_id=1, source_target_pairs={{0,8},{2,10},{4,12},{6,14},{8,16},{10,18},{12,20},{14,22},{16,24},... | collective-permute-start | bytes 884744 | tf_op jit(solution)/shard_map/ppermute | solution.py:473
  817.9 11.0 %collective-permute-start.26 = (bf16[1,96,1536]{2,1,0:T(8,128)(2,1)S(1)}, bf16[1,96,1536]{2,1,0:T(8,128)(2,1)S(1)}, u32[]{:S(2)}, u32[]{:S(2)}) collective-permute-start(bf16[1,96,1536]{2,1,0:T(8,128)(2,1)S(1)} %add_convert_fusion.5), channel_id=1, source_target_pairs={{0,8},{2,10},{4,12},{6,14},{8,16},{10,18},{12,20},{14,22},{16,24},... | collective-permute-start | bytes 884744 | tf_op jit(solution)/shard_map/ppermute | solution.py:473
  818.3 13.8 %collective-permute-start.30 = (f32[1,96,384]{2,1,0:T(8,128)S(1)}, f32[1,96,384]{2,1,0:T(8,128)S(1)}, u32[]{:S(2)}, u32[]{:S(2)}) collective-permute-start(f32[1,96,384]{2,1,0:T(8,128)S(1)} %constant_dynamic-slice_fusion.1), channel_id=1, source_target_pairs={{0,8},{2,10},{4,12},{6,14},{8,16},{10,18},{12,20},{14,22},{16,24},... | collective-permute-start | bytes 442376 | tf_op jit(solution)/shard_map/ppermute | solution.py:473
  829.0 11.7 %collective-permute-start.27 = (bf16[1,96,1536]{2,1,0:T(8,128)(2,1)S(1)}, bf16[1,96,1536]{2,1,0:T(8,128)(2,1)S(1)}, u32[]{:S(2)}, u32[]{:S(2)}) collective-permute-start(bf16[1,96,1536]{2,1,0:T(8,128)(2,1)S(1)} %add_convert_fusion.4), channel_id=1, source_target_pairs={{0,8},{2,10},{4,12},{6,14},{8,16},{10,18},{12,20},{14,22},{16,24},... | collective-permute-start | bytes 884744 | tf_op jit(solution)/shard_map/ppermute | solution.py:473
  832.1 8.5 collective-permute-start.31
  840.7 7.0 collective-permute-start.32
  847.8 4.6 collective-permute-start.33
  (56 other events, 429.2 us)
Sparse Core Ops, SparseCore 0:
  12.1 91.3 all-gather.4
  106.3 51.5 all-gather.6
  160.2 87.2 all-gather.8
  249.6 51.4 all-gather.10
  332.4 72.8 reduce-scatter.3
  446.5 109.5 reduce-scatter.5
  678.5 63.9 reduce-scatter.7

commit v3 on v1

--- a/solution.py
+++ b/solution.py
@@ -336,18 +336,63 @@
 
 
 VMEM_LIMIT = 48 * 1024 * 1024
-
-
-def mixer_forward(zx, bcdt, taps, chan, bct, bcb, dtv):
-    rows, width2 = zx.shape
+LIGHT = pl.CostEstimate(flops=1000, bytes_accessed=1000, transcendentals=0)
+
+
+def product_t(a, b, out_dtype, columns=512):
+    rows, depth = a.shape
+    count = b.shape[0]
+
+    def body(a_ref, b_ref, o_ref):
+        o_ref[...] = mm_t(a_ref[...], b_ref[...]).astype(out_dtype)
+
+    return pl.pallas_call(
+        body,
+        grid=(count // columns,),
+        in_specs=[
+            pl.BlockSpec((rows, depth), lambda j: (0, 0)),
+            pl.BlockSpec((columns, depth), lambda j: (j, 0)),
+        ],
+        out_specs=pl.BlockSpec((rows, columns), lambda j: (0, j)),
+        out_shape=jax.ShapeDtypeStruct((rows, count), out_dtype),
+        compiler_params=pltpu.CompilerParams(vmem_limit_bytes=VMEM_LIMIT),
+        cost_estimate=LIGHT,
+    )(a, b)
+
+
+def t_product(a, b, out_dtype, first, count, columns=512):
+    depth, rows = a.shape
+    offset = first // columns
+
+    def body(a_ref, b_ref, o_ref):
+        o_ref[...] = t_mm(a_ref[...], b_ref[...]).astype(out_dtype)
+
+    return pl.pallas_call(
+        body,
+        grid=(count // columns,),
+        in_specs=[
+            pl.BlockSpec((depth, rows), lambda j: (0, 0)),
+            pl.BlockSpec((depth, columns), lambda j: (0, offset + j)),
+        ],
+        out_specs=pl.BlockSpec((rows, columns), lambda j: (0, j)),
+        out_shape=jax.ShapeDtypeStruct((rows, count), out_dtype),
+        compiler_params=pltpu.CompilerParams(vmem_limit_bytes=VMEM_LIMIT),
+        cost_estimate=LIGHT,
+    )(a, b)
+
+
+def mixer_forward(zx, taps, chan, bct, bcb, dtv):
+    rows = zx.shape[0]
+    width2 = zx.shape[1] - 384
     width = width2 // 2
+    side = width2 // 384
     chunks = rows // Q
     return pl.pallas_call(
         functools.partial(fwd_kernel, head_count=width // HEADDIM),
         grid=(chunks,),
         in_specs=[
             pl.BlockSpec((Q, width2), lambda c: (c, 0)),
-            pl.BlockSpec((Q, 384), lambda c: (c, 0)),
+            pl.BlockSpec((Q, 384), lambda c: (c, side)),
             whole((4, width)), whole((8, width)), whole((4, 256)), whole((1, 256)),
             whole((8, LANES)), whole((LANES, width)),
         ],
@@ -371,15 +416,15 @@
         compiler_params=pltpu.CompilerParams(
             dimension_semantics=("arbitrary",), vmem_limit_bytes=VMEM_LIMIT
         ),
-        cost_estimate=pl.CostEstimate(
-            flops=2 * rows * width * 3 * LANES, bytes_accessed=rows * width * 12, transcendentals=0
-        ),
-    )(zx, bcdt, taps, chan, bct, bcb, dtv, spread_matrix(width))
-
-
-def mixer_backward(sg, zx, mixed, sin, bcdt, coef, taps, chan, bct, bcb, dtv):
-    rows, width2 = zx.shape
+        cost_estimate=LIGHT,
+    )(zx, zx, taps, chan, bct, bcb, dtv, spread_matrix(width))
+
+
+def mixer_backward(sg, zx, mixed, sin, coef, taps, chan, bct, bcb, dtv):
+    rows = zx.shape[0]
+    width2 = zx.shape[1] - 384
     width = width2 // 2
+    side = width2 // 384
     chunks = rows // Q
     last = chunks - 1
     return pl.pallas_call(
@@ -391,8 +436,8 @@
             pl.BlockSpec((16, width), lambda c: (jnp.maximum((last - c) * (Q // 16) - 1, 0), 1)),
             pl.BlockSpec((Q, width), lambda c: (last - c, 0)),
             pl.BlockSpec((1, LANES, width), lambda c: (last - c, 0, 0)),
-            pl.BlockSpec((Q, 384), lambda c: (last - c, 0)),
-            pl.BlockSpec((8, 384), lambda c: (jnp.maximum((last - c) * (Q // 8) - 1, 0), 0)),
+            pl.BlockSpec((Q, 384), lambda c: (last - c, side)),
+            pl.BlockSpec((8, 384), lambda c: (jnp.maximum((last - c) * (Q // 8) - 1, 0), side)),
             pl.BlockSpec((Q, LANES), lambda c: (last - c, 0)),
             whole((4, width)), whole((8, width)), whole((4, 256)), whole((1, 256)),
             whole((8, LANES)), whole((LANES, width)), whole((width, LANES)),
@@ -418,10 +463,8 @@
         compiler_params=pltpu.CompilerParams(
             dimension_semantics=("arbitrary",), vmem_limit_bytes=VMEM_LIMIT
         ),
-        cost_estimate=pl.CostEstimate(
-            flops=2 * rows * width * 10 * LANES, bytes_accessed=rows * width * 20, transcendentals=0
-        ),
-    )(sg, zx, zx, mixed, sin, bcdt, bcdt, coef, taps, chan, bct, bcb, dtv,
+        cost_estimate=LIGHT,
+    )(sg, zx, zx, mixed, sin, zx, zx, coef, taps, chan, bct, bcb, dtv,
       spread_matrix(width), gather_matrix(width))
 
 
@@ -435,13 +478,49 @@
     )
 
 
-def sum_devices(v):
-    span = 1
+def dp_factors():
     size = lax.axis_size("dp")
-    while span < size:
-        v = v + lax.ppermute(v, "dp", [(i, i ^ span) for i in range(size)])
-        span *= 2
-    return v
+    known = {16: (2, 2, 4), 64: (2, 4, 2, 4)}
+    return known.get(size, (size,))
+
+
+def after(v, other):
+    return lax.optimization_barrier((v, other))[0]
+
+
+def row_blocks(v):
+    size = lax.axis_size("dp")
+    return v.reshape((size, v.shape[0] // size) + v.shape[1:])
+
+
+def fold(blocks, level, start=None, finish=None, marks=()):
+    factors = dp_factors()
+    factor = factors[level]
+    stride = 1
+    for f in factors[:level]:
+        stride *= f
+    size = lax.axis_size("dp")
+    place = (lax.axis_index("dp") // stride) % factor
+    hops = []
+    for i in range(size):
+        here = (i // stride) % factor
+        hops.append((i, i + ((here + 1) % factor - here) * stride))
+    parts = blocks.reshape((blocks.shape[0] // factor, factor) + blocks.shape[1:])
+
+    def pick(step):
+        return lax.dynamic_index_in_dim(parts, (place + step) % factor, 1, keepdims=False)
+
+    moving = pick(factor - 1)
+    if start is not None:
+        moving = after(moving, start)
+    for step in range(factor - 1):
+        if step < len(marks):
+            moving = after(moving, marks[step])
+        arrived = lax.ppermute(moving, "dp", hops)
+        if finish is not None:
+            arrived = after(arrived, finish)
+        moving = (arrived.astype(f32) + pick(2 * factor - 2 - step).astype(f32)).astype(blocks.dtype)
+    return moving, arrived
 
 
 def head_lanes(v):
@@ -505,23 +584,26 @@
         params.append((conv_x[l], chan, conv_bc[l], conv_bc_bias[l][None, :], dtv))
 
     current = hidden.astype(f32)
-    cot = gather_pair(cotangent)
     saved = []
     for l in range(layers):
         w_in = in_weights[l]
         rms = lax.rsqrt(jnp.mean(current * current, axis=1, keepdims=True) + epsilon)
-        normed = gather_pair((current * rms * pre_gain[l][None, :]).astype(bf16))
-        zx = mm(normed, w_in[:, : 2 * width])
-        bcdt = mm(normed, w_in[:, 2 * width :])
-        scaled, mixed, states, squares = mixer_forward(zx, bcdt, *params[l])
+        own_normed = (current * rms * pre_gain[l][None, :]).astype(bf16)
+        if l == 0:
+            arrived = pair_swap(jnp.concatenate([own_normed, cotangent], axis=0))
+            normed = both_rows(own_normed, arrived[:own_count], first)
+            cot = both_rows(cotangent, arrived[own_count:], first)
+        else:
+            normed = gather_pair(own_normed)
+        zx = mm(normed, w_in)
+        scaled, mixed, states, squares = mixer_forward(zx, *params[l])
         squares = jnp.sum(squares, axis=1).reshape(8, -1)
         squares = (squares + pair_swap(squares)).reshape(rows, 1)
         inv = lax.rsqrt(squares / INNER + epsilon)
         shaped = (scaled * inv).astype(bf16)
         other = mm_t(other_half(shaped), out_weights[l])
-        arrived = pair_swap(other.astype(bf16))
         own = mm_t(own_half(shaped), out_weights[l])
-        lifted = own + arrived.astype(f32)
+        outgoing = other.astype(bf16)
         if l == layers - 1:
             own_dot = jnp.sum(own_half(cot).astype(f32) * own, axis=1, keepdims=True)
             other_dot = jnp.sum(other_half(cot).astype(f32) * other, axis=1, keepdims=True)
@@ -530,15 +612,22 @@
                 jnp.concatenate([own_dot, other_dot], axis=0),
                 jnp.concatenate([other_dot, own_dot], axis=0),
             ).reshape(8, -1)
-            last_dot = (dots + pair_swap(dots)).reshape(rows, 1)
-        saved.append((current, rms, normed, zx, bcdt, shaped, mixed, states, inv, lifted))
-        current = current + lifted
-    hidden_out = current
+            dots = dots + pair_swap(dots)
+            last_dot = dots.reshape(rows, 1)
+            arrived = pair_swap(after(outgoing, dots))
+            last_own, last_arrived = own, arrived
+        else:
+            arrived = pair_swap(outgoing)
+        lifted = own + arrived.astype(f32)
+        saved.append((current, rms, normed, zx, shaped, mixed, states, inv, lifted))
+        if l < layers - 1:
+            current = current + lifted
     grad_rows = cotangent.astype(f32)
     outputs = [None] * layers
+    out_parts = [None] * layers
     packed = [None] * layers
     for l in reversed(range(layers)):
-        current, rms, normed, zx, bcdt, shaped, mixed, states, inv, lifted = saved[l]
+        current, rms, normed, zx, shaped, mixed, states, inv, lifted = saved[l]
         w_in = in_weights[l]
         if l == layers - 1:
             out_grad = cot
@@ -554,36 +643,87 @@
         shaped_grad = mm(out_grad, out_weights[l])
         grad_out = t_mm(out_grad, shaped).astype(bf16)
         low, gchan, gbc, gdt = mixer_backward(
-            shaped_grad, zx, mixed, states, bcdt, coef, *params[l]
+            shaped_grad, zx, mixed, states, coef, *params[l]
         )
-        arrived = pair_swap(mm_t(other_half(low), w_in).astype(bf16))
-        normed_grad = mm_t(own_half(low), w_in) + arrived.astype(f32)
-        grad_in = t_mm(normed, low[:, : 2 * width]).astype(bf16)
-        grad_side = t_mm(normed, low[:, 2 * width :])
-        grad_out_own = lax.psum_scatter(grad_out, "dp", scatter_dimension=0, tiled=True)
-        grad_in_own = lax.psum_scatter(grad_in, "dp", scatter_dimension=0, tiled=True)
-        grad_side = lax.psum_scatter(grad_side, "dp", scatter_dimension=0, tiled=True)
+        if l == layers - 1:
+            low, last_arrived = lax.optimization_barrier((low, last_arrived))
+            hidden_out = saved[l][0] + last_own + last_arrived.astype(f32)
+        if l == 0:
+            low, done_in = lax.optimization_barrier((low, done_in))
+        other = product_t(other_half(low), w_in, bf16)
+        arrived = pair_swap(other)
+        low = after(low, other)
+        if l > 0:
+            grad_in = t_product(normed, low, bf16, 0, 2 * width)
+            done_in = lax.psum_scatter(grad_in, "dp", scatter_dimension=0, tiled=True)
+            low = after(low, grad_in)
+            own = product_t(own_half(low), w_in, f32)
+            done_out = lax.psum_scatter(grad_out, "dp", scatter_dimension=0, tiled=True)
+            arrived, own, done_out = lax.optimization_barrier((arrived, own, done_out))
+            out_parts[l] = done_out
+            low_last, normed_last = low, normed
+        else:
+            in_state = []
+            for i in range(2):
+                part = t_product(normed, low, bf16, i * width, width)
+                in_state.append(fold(row_blocks(part), 0)[0])
+                low = after(low, part)
+            own = product_t(own_half(after(low, in_state[0])), w_in, f32)
+            low = after(low, own)
+        normed_grad = own + arrived.astype(f32)
         unit = current * rms
         weighted = normed_grad * pre_gain[l][None, :]
-        grad_pre = jnp.sum(normed_grad * unit, axis=0)
+        grad_pre = jnp.sum(other.astype(f32) * other_half(normed).astype(f32), axis=0)
+        grad_pre = grad_pre + jnp.sum(own * own_half(normed).astype(f32), axis=0)
+        grad_pre = grad_pre / pre_gain[l]
         grad_rows = grad_rows + rms * (
             weighted - unit * jnp.mean(weighted * unit, axis=1, keepdims=True)
         )
         gchan = gchan.at[7].set(grad_pre)
         packed[l] = jnp.concatenate([gchan, gbc, gdt], axis=1)
-        grad_in_own = grad_in_own.astype(f32)
-        grad_bc = grad_side[:, :256]
-        outputs[l] = (
-            grad_in_own.reshape(-1, 2, width),
-            grad_bc + pair_swap(grad_bc),
-            grad_side[:, 256 : 256 + heads],
-            grad_out_own.astype(f32).T,
-        )
+        if l > 0:
+            low_last = after(low_last, grad_rows)
+            side_last = t_mm(normed_last, low_last[:, 2 * width : 2 * width + 256 + heads])
+        else:
+            side = t_mm(normed, low[:, 2 * width : 2 * width + 256 + heads])
+    done_out = lax.psum_scatter(grad_out, "dp", scatter_dimension=0, tiled=True)
+    done_out = after(done_out, (own, in_state[1]))
     small = jnp.stack(packed)
+    spare = small.reshape(depth, -1)
+    side_width = 256 + heads
+    side = jnp.concatenate([side, side_last, spare], axis=1)
+    side = jnp.pad(side, ((0, 0), (0, -side.shape[1] % LANES)))
+    side = after(side, done_out)
+    side_own = lax.psum_scatter(side, "dp", scatter_dimension=0, tiled=True)
+    shares = side_own[:, 2 * side_width : 2 * side_width + spare.shape[1]].reshape(-1)
+    shares = lax.all_gather(shares, ("dp", "tensor"), axis=0, tiled=False)
+    shares = shares.reshape(-1, lax.axis_size("tensor"), shares.shape[-1])
+    mine = lax.dynamic_index_in_dim(shares, tensor_index, 1, keepdims=False).reshape(small.shape)
+    both = jnp.sum(shares, axis=1).reshape(small.shape)
     row = lax.broadcasted_iota(jnp.int32, small.shape, 1)
     col = lax.broadcasted_iota(jnp.int32, small.shape, 2)
     shared = ((row == 7) & (col < width)) | ((col >= width) & (col < width + 256))
-    small = sum_devices(small + jnp.where(shared, pair_swap(small), 0.0))
+    small = jnp.where(shared, both, mine)
+    queue = in_state
+    for level in range(1, len(dp_factors())):
+        last_level = level == len(dp_factors()) - 1
+        last_arrival = None
+        for n in range(len(queue)):
+            queue[n], last_arrival = fold(
+                queue[n], level, start=None if last_level else last_arrival
+            )
+    done = [q.reshape(q.shape[1:]) for q in queue]
+    out_parts[0] = done_out
+    in_parts = [jnp.concatenate(done, axis=1), done_in]
+    side_parts = [side_own[:, :side_width], side_own[:, side_width : 2 * side_width]]
+    for l in range(layers):
+        grad_bc = side_parts[l][:, :256]
+        outputs[l] = (
+            in_parts[l].astype(f32).reshape(-1, 2, width),
+            grad_bc + pair_swap(grad_bc),
+            side_parts[l][:, 256:],
+            out_parts[l].astype(f32).T,
+        )
     grad_w_zx, grad_w_bc, grad_w_dt, grad_w_out = (
         jnp.stack([o[i] for o in outputs]) for i in range(4)
     )

time: 1070 us -> 873 us (0.82)
  waiting for transfers between devices: 594 us -> 262 us
  matrix products: 197 us -> 99.6 us
  local copies, waits for them, and re-layouts: 38.9 us -> 108 us
  Pallas kernels: 160 us -> 228 us
  blocking collectives: 0 us -> 66.2 us
  other arithmetic: 41.6 us -> 69 us
    reduce_scatter x6 -> x3, waiting for transfers between devices: 292 us -> 0.02 us  [the longest x2 0.02 us: local(): done_out = lax.psum_scatter(grad_out, 'dp', scatter_dimension=0, tiled=True)]
    pallas_call x0 -> x7, Pallas kernels: none -> 68 us  [the longest x4 38 us: product_t(): pl.pallas_call(body, grid=(count // columns,), in_specs=[pl.BlockSpec((ro...]
    all_gather x0 -> x1, blocking collectives: none -> 66.2 us  [local(): shares = lax.all_gather(shares, ('dp', 'tensor'), axis=0, tiled=False)]
    ppermute x4 -> x10, waiting for transfers between devices: 13.4 us -> 73.2 us  [fold(): arrived = lax.ppermute(moving, 'dp', hops)]
    ppermute x15 -> x13, waiting for transfers between devices: 239 us -> 179 us  [pair_swap(): return lax.ppermute(v, 'tensor', ((0, 1), (1, 0)))]
    dot_general x6 -> x4, matrix products: 68 us -> 20.5 us  [t_mm(): lax.dot_general(a, b, (((0,), (0,)), ((), ())), preferred_element_type=f32)]
    dot_general x8 -> x4, matrix products: 64.8 us -> 24.5 us  [mm_t(): lax.dot_general(a, b, (((1,), (1,)), ((), ())), preferred_element_type=f32)]
    all_gather x2, waiting for transfers between devices: 49 us -> 9.6 us  [local(): in_weights.append(lax.all_gather(shard, 'dp', axis=0, tiled=True))]
  transfers between devices with their start and end apart: 29 -> 31, of which waited for: 19 -> 17; matrix products, arithmetic and copies ran while one was open for 21% -> 27% of each run, Pallas kernels for 10% -> 26%
where the time goes in v3:
time: 873 us; the launch traced here: 869 us
  waiting for transfers between devices  262 us (30%)
  Pallas kernels  228 us (26%)
  local copies, waits for them, and re-layouts  108 us (12%)
  matrix products  99.6 us (11%)
  other arithmetic  69 us (8%)
  blocking collectives  66.2 us (8%)
  starting transfers between devices  20 us (2%)
  between operations  15.6 us (2%)
    ppermute x13, waiting for transfers between devices, pair_swap(): return lax.ppermute(v, 'tensor', ((0, 1), (1, 0)))  179 us
    pallas_call x2, Pallas kernels, mixer_backward(): pl.pallas_call(functools.partial(bwd_kernel, head_count=width // HEADDIM)...  103 us
    ppermute x10, waiting for transfers between devices, fold(): arrived = lax.ppermute(moving, 'dp', hops)  73.2 us
    all_gather x1, blocking collectives, local(): shares = lax.all_gather(shares, ('dp', 'tensor'), axis=0, tiled=False)  66.2 us
    pallas_call x2, Pallas kernels, mixer_forward(): pl.pallas_call(functools.partial(fwd_kernel, head_count=width // HEADDIM)...  57.1 us
    dot_general x4, matrix products, mm(): lax.dot_general(a, b, (((1,), (0,)), ((), ())), precision=precision, pref...  54.6 us
    unnamed x206, local copies, waits for them, and re-layouts  42.2 us
    pallas_call x4, Pallas kernels, product_t(): pl.pallas_call(body, grid=(count // columns,), in_specs=[pl.BlockSpec((ro...  38 us
  transfers between devices with their start and end apart: 31, of which 17 were waited for; matrix products, arithmetic and copies ran while one was open for 27% of the time, Pallas kernels for 26%

profile of v3, /device:TPU:0, one launch (start us, length us, event | category | flops | bytes accessed | tf_op | source)
XLA Modules:
  0.0 868.6 jit_solution(16644812227995647166)
XLA Ops:
  8.9 2.1 fusion.49
  18.4 2.9 collective-permute-start
  26.2 63.5 %collective-permute-done = bf16[1024,1536]{1,0:T(8,128)(2,1)} collective-permute-done((bf16[1024,1536]{1,0:T(8,128)(2,1)}, bf16[1024,1536]{1,0:T(8,128)(2,1)}, u32[]{:S(2)}, u32[]{:S(2)}) %collective-permute-start) | collective-permute-done | bytes 3145760 | tf_op jit(solution)/shard_map/ppermute | solution.py:472
  89.7 3.3 fusion.48
  94.0 9.6 %all-gather.6.cloned.1.call-done.b_ref = bf16[1536,3456]{1,0:T(8,128)(2,1)} async-done(((bf16[96,3456]{1,0:T(8,128)(2,1)}), bf16[1536,3456]{1,0:T(8,128)(2,1)}) %all-gather.6.cloned.1.call-update) | async-done | bytes 10616848 | tf_op jit(solution)/shard_map/all_gather | solution.py:575
  103.6 17.1 %fusion.58.zx_ref.bcdt_ref.xprev_ref.bcprev_ref = f32[1024,3456]{1,0:T(8,128)} fusion(bf16[1024,1536]{1,0:T(8,128)(2,1)S(1)} %fusion.5.a_ref, bf16[1536,3456]{1,0:T(8,128)(2,1)} %all-gather.6.cloned.1.call-done.b_ref), kind=kOutput, calls=%fused_computation.171 | convolution fusion | flops 10871635968 | bytes 27918336 | tf_op jit(solution)/shard_map/dot_general | solution.py:26
  120.6 28.5 %shard_map.262 = (f32[1024,1536]{1,0:T(8,128)}, bf16[1024,1536]{1,0:T(8,128)(2,1)S(1)}, bf16[8,128,1536]{2,1,0:T(8,128)(2,1)}, f32[1024,128]{1,0:T(8,128)S(1)}) custom-call(f32[1024,3456]{1,0:T(8,128)} %fusion.58.zx_ref.bcdt_ref.xprev_ref.bcprev_ref, f32[1024,3456]{1,0:T(8,128)} %fusion.58.zx_ref.bcdt_ref.xprev_ref.bcprev_ref, f32[4,1536]{1,0:T(4,128)S(1)} %copy-done.20, ...), custom_call_target="tpu_custom_call" | custom-call | flops 1000 | bytes 1000 | tf_op jit(solution)/shard_map/pallas_call | solution.py:390
  154.5 2.2 collective-permute-done.1
  157.4 4.8 multiply_convert_fusion.1
  162.3 6.6 convolution_convert_fusion.2
  170.4 34.5 %collective-permute-done.2 = bf16[512,1536]{1,0:T(8,128)(2,1)} collective-permute-done((bf16[512,1536]{1,0:T(8,128)(2,1)}, bf16[512,1536]{1,0:T(8,128)(2,1)}, u32[]{:S(2)}, u32[]{:S(2)}) %collective-permute-start.2) | collective-permute-done | bytes 1572896 | tf_op jit(solution)/shard_map/ppermute | solution.py:472
  204.9 8.2 multiply_reduce_fusion.8
  224.6 25.1 %collective-permute-done.3 = bf16[512,1536]{1,0:T(8,128)(2,1)} collective-permute-done((bf16[512,1536]{1,0:T(8,128)(2,1)}, bf16[512,1536]{1,0:T(8,128)(2,1)}, u32[]{:S(2)}, u32[]{:S(2)}) %collective-permute-start.3) | collective-permute-done | bytes 1572896 | tf_op jit(solution)/shard_map/ppermute | solution.py:472
  249.7 4.5 maximum_select_fusion.a_ref
  254.3 18.4 %fusion.59.zx_ref.bcdt_ref.xprev_ref.bcprev_ref = f32[1024,3456]{1,0:T(8,128)} fusion(bf16[1024,1536]{1,0:T(8,128)(2,1)} %maximum_select_fusion.a_ref, bf16[1536,3456]{1,0:T(8,128)(2,1)} %all-gather.10.cloned.1.call-done.b_ref), kind=kOutput, calls=%fused_computation.172 | convolution fusion | flops 10871635968 | bytes 27918336 | tf_op jit(solution)/shard_map/dot_general | solution.py:26
  272.6 28.6 %shard_map.263 = (f32[1024,1536]{1,0:T(8,128)}, bf16[1024,1536]{1,0:T(8,128)(2,1)S(1)}, bf16[8,128,1536]{2,1,0:T(8,128)(2,1)}, f32[1024,128]{1,0:T(8,128)S(1)}) custom-call(f32[1024,3456]{1,0:T(8,128)} %fusion.59.zx_ref.bcdt_ref.xprev_ref.bcprev_ref, f32[1024,3456]{1,0:T(8,128)} %fusion.59.zx_ref.bcdt_ref.xprev_ref.bcprev_ref, f32[4,1536]{1,0:T(4,128)S(1)} %copy-done.22, ...), custom_call_target="tpu_custom_call" | custom-call | flops 1000 | bytes 1000 | tf_op jit(solution)/shard_map/pallas_call | solution.py:390
  307.0 3.3 fusion.6
  314.6 7.0 convolution_convert_fusion.1
  321.9 5.2 fusion.15
  328.7 4.5 multiply_reduce_fusion.7
  334.5 2.4 collective-permute-done.5
  337.3 6.9 fusion.60.sg_ref
  348.7 1.9 copy-done.12
  352.9 51.1 %shard_map.264 = (bf16[1024,3456]{1,0:T(8,128)(2,1)}, f32[8,1536]{1,0:T(8,128)S(1)}, f32[8,256]{1,0:T(8,128)S(1)}, f32[8,128]{1,0:T(8,128)S(1)}) custom-call(f32[1024,1536]{1,0:T(8,128)} %fusion.60.sg_ref, f32[1024,3456]{1,0:T(8,128)} %fusion.59.zx_ref.bcdt_ref.xprev_ref.bcprev_ref, f32[1024,3456]{1,0:T(8,128)} %fusion.59.zx_ref.bcdt_ref.xprev_ref.bcprev_ref, ...), custom_call_target="tpu_custom_call" | custom-call | flops 1000 | bytes 1000 | tf_op jit(solution)/shard_map/pallas_call | solution.py:430
  405.8 2.2 constant_dynamic-slice_fusion.6.a_ref
  408.0 8.5 shard_map.265
  417.7 13.8 %shard_map.266 = bf16[1536,3072]{1,0:T(8,128)(2,1)} custom-call(bf16[1024,1536]{1,0:T(8,128)(2,1)S(1)} %copy-done, bf16[1024,3456]{1,0:T(8,128)(2,1)} %get-tuple-element.217.b_ref), custom_call_target="tpu_custom_call" | custom-call | flops 1000 | bytes 1000 | tf_op jit(solution)/shard_map/pallas_call | solution.py:370
  433.5 4.4 constant_dynamic-slice_fusion.5.a_ref
  437.9 10.5 %shard_map.267 = f32[512,1536]{1,0:T(8,128)S(1)} custom-call(bf16[512,3456]{1,0:T(8,128)(2,1)} %constant_dynamic-slice_fusion.5.a_ref, bf16[1536,3456]{1,0:T(8,128)(2,1)} %all-gather.10.cloned.1.call-done.b_ref), custom_call_target="tpu_custom_call" | custom-call | flops 1000 | bytes 1000 | tf_op jit(solution)/shard_map/pallas_call | solution.py:349
  450.1 13.7 %collective-permute-done.7 = bf16[512,1536]{1,0:T(8,128)(2,1)} collective-permute-done((bf16[512,1536]{1,0:T(8,128)(2,1)}, bf16[512,1536]{1,0:T(8,128)(2,1)}, u32[]{:S(2)}, u32[]{:S(2)}) %collective-permute-start.7) | collective-permute-done | bytes 1572896 | tf_op jit(solution)/shard_map/ppermute | solution.py:472
  463.9 6.8 multiply_reduce_fusion
  471.8 6.8 multiply_reduce_fusion.4
  480.2 30.1 %collective-permute-done.8 = bf16[512,1536]{1,0:T(8,128)(2,1)S(1)} collective-permute-done((bf16[512,1536]{1,0:T(8,128)(2,1)S(1)}, bf16[512,1536]{1,0:T(8,128)(2,1)S(1)}, u32[]{:S(2)}, u32[]{:S(2)}) %collective-permute-start.8) | collective-permute-done | bytes 1572896 | tf_op jit(solution)/shard_map/ppermute | solution.py:472
  511.5 6.8 convolution_convert_fusion
  529.2 12.2 %fusion.33.sg_ref = f32[1024,1536]{1,0:T(8,128)} fusion(bf16[1536,1536]{1,0:T(8,128)(2,1)} %all-gather.8.cloned.1.call-done, bf16[512,1536]{1,0:T(8,128)(2,1)} %copy-done.92, bf16[512,1536]{1,0:T(8,128)(2,1)} %copy-done.58, pred[]{:T(512)S(6)} %eq.155), kind=kOutput, calls=%fused_computation.84 | convolution fusion | flops 4845993984 | bytes 14155777 | tf_op jit(solution)/shard_map/dot_general | solution.py:26
  541.4 51.5 %shard_map.268 = (bf16[1024,3456]{1,0:T(8,128)(2,1)}, f32[8,1536]{1,0:T(8,128)S(1)}, f32[8,256]{1,0:T(8,128)S(1)}, f32[8,128]{1,0:T(8,128)S(1)}) custom-call(f32[1024,1536]{1,0:T(8,128)} %fusion.33.sg_ref, f32[1024,3456]{1,0:T(8,128)} %fusion.58.zx_ref.bcdt_ref.xprev_ref.bcprev_ref, f32[1024,3456]{1,0:T(8,128)} %fusion.58.zx_ref.bcdt_ref.xprev_ref.bcprev_ref, ...), custom_call_target="tpu_custom_call" | custom-call | flops 1000 | bytes 1000 | tf_op jit(solution)/shard_map/pallas_call | solution.py:430
  594.1 4.0 constant_dynamic-slice_fusion.4.a_ref
  598.1 2.0 copy-done.5
  600.1 9.4 %shard_map.269 = bf16[512,1536]{1,0:T(8,128)(2,1)} custom-call(bf16[512,3456]{1,0:T(8,128)(2,1)S(1)} %copy-done.5, bf16[1536,3456]{1,0:T(8,128)(2,1)} %all-gather.6.cloned.1.call-done.b_ref), custom_call_target="tpu_custom_call" | custom-call | flops 1000 | bytes 1000 | tf_op jit(solution)/shard_map/pallas_call | solution.py:349
  609.5 8.0 shard_map.270
  617.5 3.2 dynamic-slice_bitcast_fusion.1
  620.7 8.1 shard_map.271
  628.9 3.2 dynamic-slice_bitcast_fusion
  632.7 4.3 fusion.24
  638.5 2.9 stack_reshape.5
  641.4 1.9 copy.80
  643.4 3.0 fusion.1
  648.9 4.2 constant_dynamic-slice_fusion.3.a_ref
  653.2 9.6 %shard_map.272 = f32[512,1536]{1,0:T(8,128)S(1)} custom-call(bf16[512,3456]{1,0:T(8,128)(2,1)} %constant_dynamic-slice_fusion.3.a_ref, bf16[1536,3456]{1,0:T(8,128)(2,1)} %all-gather.6.cloned.1.call-done.b_ref), custom_call_target="tpu_custom_call" | custom-call | flops 1000 | bytes 1000 | tf_op jit(solution)/shard_map/pallas_call | solution.py:349
  664.5 3.8 fusion
  668.3 5.4 collective-permute-done.11
  673.6 4.8 multiply_reduce_fusion.2
  682.1 2.4 fusion.26
  684.4 2.4 select_maximum_fusion
  686.8 5.5 copy.83
  695.0 5.2 fusion.11
  703.2 17.8 %collective-permute-done.17 = bf16[4,96,1536]{2,1,0:T(8,128)(2,1)S(1)} collective-permute-done((bf16[4,96,1536]{2,1,0:T(8,128)(2,1)S(1)}, bf16[4,96,1536]{2,1,0:T(8,128)(2,1)S(1)}, u32[]{:S(2)}, u32[]{:S(2)}) %collective-permute-start.17) | collective-permute-done | bytes 1179680 | tf_op jit(solution)/shard_map/ppermute | solution.py:519
  722.2 17.4 %collective-permute-done.18 = bf16[1,96,1536]{2,1,0:T(8,128)(2,1)S(1)} collective-permute-done((bf16[1,96,1536]{2,1,0:T(8,128)(2,1)S(1)}, bf16[1,96,1536]{2,1,0:T(8,128)(2,1)S(1)}, u32[]{:S(2)}, u32[]{:S(2)}) %collective-permute-start.18) | collective-permute-done | bytes 294944 | tf_op jit(solution)/shard_map/ppermute | solution.py:519
  739.8 12.3 %collective-permute-done.15 = bf16[1,96,1536]{2,1,0:T(8,128)(2,1)S(1)} collective-permute-done((bf16[1,96,1536]{2,1,0:T(8,128)(2,1)S(1)}, bf16[1,96,1536]{2,1,0:T(8,128)(2,1)S(1)}, u32[]{:S(2)}, u32[]{:S(2)}) %collective-permute-start.15) | collective-permute-done | bytes 294944 | tf_op jit(solution)/shard_map/ppermute | solution.py:519
  752.2 6.2 collective-permute-done.19
  758.6 9.0 %collective-permute-done.16 = bf16[1,96,1536]{2,1,0:T(8,128)(2,1)S(1)} collective-permute-done((bf16[1,96,1536]{2,1,0:T(8,128)(2,1)S(1)}, bf16[1,96,1536]{2,1,0:T(8,128)(2,1)S(1)}, u32[]{:S(2)}, u32[]{:S(2)}) %collective-permute-start.16) | collective-permute-done | bytes 294944 | tf_op jit(solution)/shard_map/ppermute | solution.py:519
  767.7 10.4 %collective-permute-done.20 = bf16[1,96,1536]{2,1,0:T(8,128)(2,1)S(1)} collective-permute-done((bf16[1,96,1536]{2,1,0:T(8,128)(2,1)S(1)}, bf16[1,96,1536]{2,1,0:T(8,128)(2,1)S(1)}, u32[]{:S(2)}, u32[]{:S(2)}) %collective-permute-start.20) | collective-permute-done | bytes 294944 | tf_op jit(solution)/shard_map/ppermute | solution.py:519
  778.3 3.2 copy.81
  782.6 66.2 %all-gather = f32[32,1,1920]{2,1,0:T(1,128)S(1)} all-gather(f32[1,1,1920]{2,1,0:T(1,128)S(1)} %reshape.708), channel_id=1, replica_groups=mesh['dp'=16,'tensor'=2] {'dp','tensor'}, dimensions={0}, use_global_device_ids=true | all-gather | bytes 253440 | tf_op jit(solution)/shard_map/all_gather | solution.py:699
  (364 shorter events, 107.2 us)
Async XLA Ops:
  7.2 96.4 %all-gather.6.cloned.1.call-start = ((), (), s32[]{:S(2)}) async-start(), calls=%async_computation.4 | async-start | bytes 11280384 | tf_op jit(solution)/shard_map/all_gather | solution.py:575
  12.0 150.2 %all-gather.8.cloned.1.call-start = ((), (), s32[]{:S(2)}) async-start(), calls=%async_computation.5 | async-start | bytes 5013504 | tf_op jit(solution)/shard_map/all_gather | solution.py:576
  13.0 241.3 %all-gather.10.cloned.1.call-start = ((), (), s32[]{:S(2)}) async-start(), calls=%async_computation.6 | async-start | bytes 11280384 | tf_op jit(solution)/shard_map/all_gather | solution.py:575
  14.1 307.8 %all-gather.12.cloned.1.call-start = ((), (), s32[]{:S(2)}) async-start(), calls=%async_computation.7 | async-start | bytes 5013504 | tf_op jit(solution)/shard_map/all_gather | solution.py:576
  16.3 9.2 %copy-start.84 = (f32[2,4,256]{2,1,0:T(4,128)S(1)}, f32[2,4,256]{2,1,0:T(4,128)}, u32[]{:S(2)}) copy-start(f32[2,4,256]{2,1,0:T(4,128)} %param.46) | copy-start | bytes 24580
  18.4 71.4 %collective-permute-start = (bf16[1024,1536]{1,0:T(8,128)(2,1)}, bf16[1024,1536]{1,0:T(8,128)(2,1)}, u32[]{:S(2)}, u32[]{:S(2)}) collective-permute-start(bf16[1024,1536]{1,0:T(8,128)(2,1)} %pad_maximum_fusion.1), channel_id=1, source_target_pairs={{0,1},{1,0},{2,3},{3,2},{4,5},{5,4},{6,7},{7,6},{8,9},{9,8},{10,11... | collective-permute-start | bytes 9437192 | tf_op jit(solution)/shard_map/ppermute | solution.py:472
  24.8 68.2 %copy-start.15 = (f32[8,1536]{1,0:T(8,128)}, f32[8,1536]{1,0:T(8,128)S(1)}, u32[]{:S(2)}) copy-start(f32[8,1536]{1,0:T(8,128)S(1)} %scatter.44.chan_ref) | copy-start | bytes 147460
  24.8 68.2 %copy-start.66 = (s32[1536]{0:T(1024)}, s32[1536]{0:T(1024)S(1)}, u32[]{:S(2)}) copy-start(s32[1536]{0:T(1024)S(1)} %get-tuple-element.346) | copy-start | bytes 18436
  25.4 95.2 %copy-start.28 = (f32[4,256]{1,0:T(4,128)}, f32[4,256]{1,0:T(4,128)S(1)}, u32[]{:S(2)}) copy-start(f32[4,256]{1,0:T(4,128)S(1)} %get-tuple-element.335.bct_ref) | copy-start | bytes 12292
  26.2 66.8 %copy-start.43 = (bf16[512,1536]{1,0:T(8,128)(2,1)S(1)}, bf16[512,1536]{1,0:T(8,128)(2,1)}, u32[]{:S(2)}) copy-start(bf16[512,1536]{1,0:T(8,128)(2,1)} %copy-done.42) | copy-start | bytes 4718596
  103.6 17.1 %copy-start.16 = (f32[8,1536]{1,0:T(8,128)S(1)}, f32[8,1536]{1,0:T(8,128)}, u32[]{:S(2)}) copy-start(f32[8,1536]{1,0:T(8,128)} %copy-done.15) | copy-start | bytes 147460
  103.6 17.1 %copy-start.20 = (f32[4,1536]{1,0:T(4,128)S(1)}, f32[4,1536]{1,0:T(4,128)}, u32[]{:S(2)}) copy-start(f32[4,1536]{1,0:T(4,128)} %get-tuple-element.325.taps_ref) | copy-start | bytes 73732
  153.0 9.3 %copy-start.71 = (f32[1024]{0:T(1024)}, f32[1024]{0:T(1024)S(1)}, u32[]{:S(2)}) copy-start(f32[1024]{0:T(1024)S(1)} %reduce_sum.136) | copy-start | bytes 12292
  153.0 3.8 collective-permute-start.1
  168.9 36.0 %collective-permute-start.2 = (bf16[512,1536]{1,0:T(8,128)(2,1)}, bf16[512,1536]{1,0:T(8,128)(2,1)}, u32[]{:S(2)}, u32[]{:S(2)}) collective-permute-start(bf16[512,1536]{1,0:T(8,128)(2,1)} %convolution_convert_fusion.2), channel_id=1, source_target_pairs={{0,1},{1,0},{2,3},{3,2},{4,5},{5,4},{6,7},{7,6},{8,9},{9,8},{10,11... | collective-permute-start | bytes 4718600 | tf_op jit(solution)/shard_map/ppermute | solution.py:472
  170.3 293.5 %reduce-scatter.7.cloned.1.call-start = ((), (), s32[]{:S(2)}) async-start(), calls=%async_computation.8 | async-start | bytes 5013504 | tf_op jit(solution)/shard_map/reduce_scatter | solution.py:661
  170.4 42.7 %copy-start.64 = (f32[1536]{0:T(1024)S(1)}, f32[1536]{0:T(1024)}, u32[]{:S(2)}) copy-start(f32[1536]{0:T(1024)} %get-tuple-element.297) | copy-start | bytes 18436
  214.6 35.1 %collective-permute-start.3 = (bf16[512,1536]{1,0:T(8,128)(2,1)}, bf16[512,1536]{1,0:T(8,128)(2,1)}, u32[]{:S(2)}, u32[]{:S(2)}) collective-permute-start(bf16[512,1536]{1,0:T(8,128)(2,1)} %multiply_convert_fusion.2), channel_id=1, source_target_pairs={{0,1},{1,0},{2,3},{3,2},{4,5},{5,4},{6,7},{7,6},{8,9},{9,8},{10,11... | collective-permute-start | bytes 4718600 | tf_op jit(solution)/shard_map/ppermute | solution.py:472
  254.3 18.4 %copy-start.18 = (f32[8,1536]{1,0:T(8,128)S(1)}, f32[8,1536]{1,0:T(8,128)}, u32[]{:S(2)}) copy-start(f32[8,1536]{1,0:T(8,128)} %scatter.51.chan_ref) | copy-start | bytes 147460
  254.3 18.4 %copy-start.22 = (f32[4,1536]{1,0:T(4,128)S(1)}, f32[4,1536]{1,0:T(4,128)}, u32[]{:S(2)}) copy-start(f32[4,1536]{1,0:T(4,128)} %get-tuple-element.324.taps_ref) | copy-start | bytes 73732
  254.3 18.4 %copy-start.30 = (f32[1,256]{1,0:T(1,128)S(1)}, f32[1,256]{1,0:T(1,128)}, u32[]{:S(2)}) copy-start(f32[1,256]{1,0:T(1,128)} %get-tuple-element.336.bcb_ref) | copy-start | bytes 3076
  305.5 4.9 collective-permute-start.4
  321.7 272.4 %reduce-scatter.9.cloned.1.call-start = ((), (), s32[]{:S(2)}) async-start(), calls=%async_computation.9 | async-start | bytes 10027008 | tf_op jit(solution)/shard_map/reduce_scatter | solution.py:658
  333.2 3.8 collective-permute-start.5
  337.0 68.8 %collective-permute-start.6 = (bf16[512,1536]{1,0:T(8,128)(2,1)}, bf16[512,1536]{1,0:T(8,128)(2,1)}, u32[]{:S(2)}, u32[]{:S(2)}) collective-permute-start(bf16[512,1536]{1,0:T(8,128)(2,1)} %get-tuple-element.201), channel_id=1, source_target_pairs={{0,1},{1,0},{2,3},{3,2},{4,5},{5,4},{6,7},{7,6},{8,9},{9,8},{10,11... | collective-permute-start | bytes 4718600 | tf_op jit(solution)/shard_map/ppermute | solution.py:472
  408.0 9.7 %copy-start = (bf16[1024,1536]{1,0:T(8,128)(2,1)S(1)}, bf16[1024,1536]{1,0:T(8,128)(2,1)}, u32[]{:S(2)}) copy-start(bf16[1024,1536]{1,0:T(8,128)(2,1)} %maximum_select_fusion.a_ref) | copy-start | bytes 9437188
  431.6 236.7 %reduce-scatter.11.cloned.1.call-start = ((), (), s32[]{:S(2)}) async-start(), calls=%async_computation.10 | async-start | bytes 5013504 | tf_op jit(solution)/shard_map/reduce_scatter | solution.py:689
  431.6 32.2 %collective-permute-start.7 = (bf16[512,1536]{1,0:T(8,128)(2,1)}, bf16[512,1536]{1,0:T(8,128)(2,1)}, u32[]{:S(2)}, u32[]{:S(2)}) collective-permute-start(bf16[512,1536]{1,0:T(8,128)(2,1)} %copy-done.6), channel_id=1, source_target_pairs={{0,1},{1,0},{2,3},{3,2},{4,5},{5,4},{6,7},{7,6},{8,9},{9,8},{10,11... | collective-permute-start | bytes 4718600 | tf_op jit(solution)/shard_map/ppermute | solution.py:472
  437.9 26.0 %copy-start.65 = (f32[1536]{0:T(1024)S(1)}, f32[1536]{0:T(1024)}, u32[]{:S(2)}) copy-start(f32[1536]{0:T(1024)} %get-tuple-element.297) | copy-start | bytes 18436
  471.8 39.7 %copy-start.52 = (bf16[1024,1536]{1,0:T(8,128)(2,1)S(1)}, bf16[1024,1536]{1,0:T(8,128)(2,1)}, u32[]{:S(2)}) copy-start(bf16[1024,1536]{1,0:T(8,128)(2,1)} %multiply_convert_fusion.1) | copy-start | bytes 9437188
  478.6 31.7 %copy-start.58 = (bf16[512,1536]{1,0:T(8,128)(2,1)}, bf16[512,1536]{1,0:T(8,128)(2,1)S(1)}, u32[]{:S(2)}) copy-start(bf16[512,1536]{1,0:T(8,128)(2,1)S(1)} %get-tuple-element.300) | copy-start | bytes 4718596
  478.6 31.7 %collective-permute-start.8 = (bf16[512,1536]{1,0:T(8,128)(2,1)S(1)}, bf16[512,1536]{1,0:T(8,128)(2,1)S(1)}, u32[]{:S(2)}, u32[]{:S(2)}) collective-permute-start(bf16[512,1536]{1,0:T(8,128)(2,1)S(1)} %get-tuple-element.300), channel_id=1, source_target_pairs={{0,1},{1,0},{2,3},{3,2},{4,5},{5,4},{6,7},{7,6},{8,9},{9,8},{10,11... | collective-permute-start | bytes 4718600 | tf_op jit(solution)/shard_map/ppermute | solution.py:472
  518.3 263.2 %reduce-scatter.13.cloned.1.call-start = ((), (), s32[]{:S(2)}) async-start(), calls=%async_computation.11 | async-start | bytes 4177920
  519.7 3.9 collective-permute-start.9
  529.1 12.2 %copy-start.8 = (bf16[1536,128]{1,0:T(8,128)(2,1)S(1)}, bf16[1536,128]{1,0:T(8,128)(2,1)}, u32[]{:S(2)}) copy-start(bf16[1536,128]{1,0:T(8,128)(2,1)} %fusion.28.gather_ref) | copy-start | bytes 1179652
  529.1 12.2 %copy-start.10 = (bf16[1024,1536]{1,0:T(8,128)(2,1)S(1)}, bf16[1024,1536]{1,0:T(8,128)(2,1)}, u32[]{:S(2)}) copy-start(bf16[1024,1536]{1,0:T(8,128)(2,1)} %copy-done.9) | copy-start | bytes 9437188
  529.1 12.2 %copy-start.17 = (f32[8,1536]{1,0:T(8,128)S(1)}, f32[8,1536]{1,0:T(8,128)}, u32[]{:S(2)}) copy-start(f32[8,1536]{1,0:T(8,128)} %copy-done.15) | copy-start | bytes 147460
  529.1 12.2 %copy-start.21 = (f32[4,1536]{1,0:T(4,128)S(1)}, f32[4,1536]{1,0:T(4,128)}, u32[]{:S(2)}) copy-start(f32[4,1536]{1,0:T(4,128)} %get-tuple-element.325.taps_ref) | copy-start | bytes 73732
  529.1 12.2 %copy-start.29 = (f32[4,256]{1,0:T(4,128)S(1)}, f32[4,256]{1,0:T(4,128)}, u32[]{:S(2)}) copy-start(f32[4,256]{1,0:T(4,128)} %copy-done.28) | copy-start | bytes 12292
  620.7 22.6 %collective-permute-start.10 = (bf16[8,96,1536]{2,1,0:T(8,128)(2,1)}, bf16[8,96,1536]{2,1,0:T(8,128)(2,1)}, u32[]{:S(2)}, u32[]{:S(2)}) collective-permute-start(bf16[8,96,1536]{2,1,0:T(8,128)(2,1)} %dynamic-slice_bitcast_fusion.1), channel_id=1, source_target_pairs={{0,2},{2,0},{4,6},{6,4},{8,10},{10,8},{12,14},{14,12},{16,18},{18,... | collective-permute-start | bytes 7077896 | tf_op jit(solution)/shard_map/ppermute | solution.py:519
  632.1 32.3 %collective-permute-start.12 = (bf16[8,96,1536]{2,1,0:T(8,128)(2,1)}, bf16[8,96,1536]{2,1,0:T(8,128)(2,1)}, u32[]{:S(2)}, u32[]{:S(2)}) collective-permute-start(bf16[8,96,1536]{2,1,0:T(8,128)(2,1)} %dynamic-slice_bitcast_fusion), channel_id=1, source_target_pairs={{0,2},{2,0},{4,6},{6,4},{8,10},{10,8},{12,14},{14,12},{16,18},{18,... | collective-permute-start | bytes 7077896 | tf_op jit(solution)/shard_map/ppermute | solution.py:519
  637.0 36.6 %collective-permute-start.11 = (bf16[512,1536]{1,0:T(8,128)(2,1)}, bf16[512,1536]{1,0:T(8,128)(2,1)}, u32[]{:S(2)}, u32[]{:S(2)}) collective-permute-start(bf16[512,1536]{1,0:T(8,128)(2,1)} %shard_map.269), channel_id=1, source_target_pairs={{0,1},{1,0},{2,3},{3,2},{4,5},{5,4},{6,7},{7,6},{8,9},{9,8},{10,11... | collective-permute-start | bytes 4718600 | tf_op jit(solution)/shard_map/ppermute | solution.py:472
  648.9 15.5 %slice-start = ((s8[4718592]{0:T(1024)(128)(4,1)}), s8[4194304]{0:T(1024)(128)(4,1)S(1)}, s32[]{:S(2)}) async-start(s8[4718592]{0:T(1024)(128)(4,1)} %bitcast.151), calls=%async_computation.12 | async-start | bytes 8388608
  653.1 11.3 %slice-start.1 = ((s8[4718592]{0:T(1024)(128)(4,1)}), s8[524288]{0:T(1024)(128)(4,1)S(1)}, s32[]{:S(2)}) async-start(s8[4718592]{0:T(1024)(128)(4,1)} %bitcast.151), calls=%async_computation.13 | async-start | bytes 1048576
  653.2 40.7 %collective-permute-start.13 = (bf16[4,96,1536]{2,1,0:T(8,128)(2,1)}, bf16[4,96,1536]{2,1,0:T(8,128)(2,1)}, u32[]{:S(2)}, u32[]{:S(2)}) collective-permute-start(bf16[4,96,1536]{2,1,0:T(8,128)(2,1)} %dynamic-slice_bitcast_fusion.3), channel_id=1, source_target_pairs={{0,4},{2,6},{4,0},{6,2},{8,12},{10,14},{12,8},{14,10},{16,20},{18,... | collective-permute-start | bytes 3538952 | tf_op jit(solution)/shard_map/ppermute | solution.py:519
  664.4 9.2 %copy-start.63 = (f32[1536]{0:T(1024)S(1)}, f32[1536]{0:T(1024)}, u32[]{:S(2)}) copy-start(f32[1536]{0:T(1024)} %copy-done.62) | copy-start | bytes 18436
  664.4 9.2 %copy-start.75 = (f32[512]{0:T(512)S(1)}, f32[512]{0:T(512)}, u32[]{:S(2)}) copy-start(f32[512]{0:T(512)} %copy-done.74) | copy-start | bytes 6148
  668.2 10.2 %copy-start.70 = (f32[2,1536]{1,0:T(2,128)S(1)}, f32[2,1536]{1,0:T(2,128)}, u32[]{:S(2)}) copy-start(f32[2,1536]{1,0:T(2,128)} %param.40) | copy-start | bytes 36868
  668.2 10.2 %copy-start.27 = (f32[8,1536]{1,0:T(8,128)S(1)}, f32[8,1536]{1,0:T(8,128)}, u32[]{:S(2)}) copy-start(f32[8,1536]{1,0:T(8,128)} %copy-done.26) | copy-start | bytes 147460
  668.2 10.4 %copy-start.25 = (f32[8,1536]{1,0:T(8,128)S(1)}, f32[8,1536]{1,0:T(8,128)}, u32[]{:S(2)}) copy-start(f32[8,1536]{1,0:T(8,128)} %copy-done.24) | copy-start | bytes 147460
  668.2 10.6 %copy-start.33 = (f32[8,256]{1,0:T(8,128)S(1)}, f32[8,256]{1,0:T(8,128)}, u32[]{:S(2)}) copy-start(f32[8,256]{1,0:T(8,128)} %copy-done.32) | copy-start | bytes 24580
  668.2 10.6 %copy-start.35 = (f32[8,128]{1,0:T(8,128)S(1)}, f32[8,128]{1,0:T(8,128)}, u32[]{:S(2)}) copy-start(f32[8,128]{1,0:T(8,128)} %copy-done.34) | copy-start | bytes 12292
  668.2 10.6 %copy-start.37 = (f32[8,128]{1,0:T(8,128)S(1)}, f32[8,128]{1,0:T(8,128)}, u32[]{:S(2)}) copy-start(f32[8,128]{1,0:T(8,128)} %copy-done.36) | copy-start | bytes 12292
  693.9 27.1 %collective-permute-start.17 = (bf16[4,96,1536]{2,1,0:T(8,128)(2,1)S(1)}, bf16[4,96,1536]{2,1,0:T(8,128)(2,1)S(1)}, u32[]{:S(2)}, u32[]{:S(2)}) collective-permute-start(bf16[4,96,1536]{2,1,0:T(8,128)(2,1)S(1)} %dynamic-slice_bitcast_fusion.2), channel_id=1, source_target_pairs={{0,4},{2,6},{4,0},{6,2},{8,12},{10,14},{12,8},{14,10},{16,20},{18,... | collective-permute-start | bytes 3538952 | tf_op jit(solution)/shard_map/ppermute | solution.py:519
  700.2 20.8 %copy-start.48 = (bf16[8,96,1536]{2,1,0:T(8,128)(2,1)S(1)}, bf16[8,96,1536]{2,1,0:T(8,128)(2,1)}, u32[]{:S(2)}) copy-start(bf16[8,96,1536]{2,1,0:T(8,128)(2,1)} %fusion) | copy-start | bytes 7077892
  703.1 18.6 %collective-permute-start.14 = (bf16[1,96,1536]{2,1,0:T(8,128)(2,1)S(1)}, bf16[1,96,1536]{2,1,0:T(8,128)(2,1)S(1)}, u32[]{:S(2)}, u32[]{:S(2)}) collective-permute-start(bf16[1,96,1536]{2,1,0:T(8,128)(2,1)S(1)} %constant_dynamic-slice_fusion.1), channel_id=1, source_target_pairs={{0,8},{2,10},{4,12},{6,14},{8,16},{10,18},{12,20},{14,22},{16,24},... | collective-permute-start | bytes 884744 | tf_op jit(solution)/shard_map/ppermute | solution.py:519
  721.4 56.8 %copy-start.56 = (bf16[1,96,2,1536]{3,1,2,0:T(8,128)(2,1)S(1)}, bf16[1,96,2,1536]{3,1,2,0:T(8,128)(2,1)}, u32[]{:S(2)}) copy-start(bf16[1,96,2,1536]{3,1,2,0:T(8,128)(2,1)} %copy.80) | copy-start | bytes 1769476
  721.4 18.2 %collective-permute-start.18 = (bf16[1,96,1536]{2,1,0:T(8,128)(2,1)S(1)}, bf16[1,96,1536]{2,1,0:T(8,128)(2,1)S(1)}, u32[]{:S(2)}, u32[]{:S(2)}) collective-permute-start(bf16[1,96,1536]{2,1,0:T(8,128)(2,1)S(1)} %constant_dynamic-slice_fusion), channel_id=1, source_target_pairs={{0,8},{2,10},{4,12},{6,14},{8,16},{10,18},{12,20},{14,22},{16,24},... | collective-permute-start | bytes 884744 | tf_op jit(solution)/shard_map/ppermute | solution.py:519
  721.8 30.3 %collective-permute-start.15 = (bf16[1,96,1536]{2,1,0:T(8,128)(2,1)S(1)}, bf16[1,96,1536]{2,1,0:T(8,128)(2,1)S(1)}, u32[]{:S(2)}, u32[]{:S(2)}) collective-permute-start(bf16[1,96,1536]{2,1,0:T(8,128)(2,1)S(1)} %add_convert_fusion.5), channel_id=1, source_target_pairs={{0,8},{2,10},{4,12},{6,14},{8,16},{10,18},{12,20},{14,22},{16,24},... | collective-permute-start | bytes 884744 | tf_op jit(solution)/shard_map/ppermute | solution.py:519
  739.7 18.8 %collective-permute-start.19 = (bf16[1,96,1536]{2,1,0:T(8,128)(2,1)S(1)}, bf16[1,96,1536]{2,1,0:T(8,128)(2,1)S(1)}, u32[]{:S(2)}, u32[]{:S(2)}) collective-permute-start(bf16[1,96,1536]{2,1,0:T(8,128)(2,1)S(1)} %add_convert_fusion.2), channel_id=1, source_target_pairs={{0,8},{2,10},{4,12},{6,14},{8,16},{10,18},{12,20},{14,22},{16,24},... | collective-permute-start | bytes 884744 | tf_op jit(solution)/shard_map/ppermute | solution.py:519
  752.2 15.5 %collective-permute-start.16 = (bf16[1,96,1536]{2,1,0:T(8,128)(2,1)S(1)}, bf16[1,96,1536]{2,1,0:T(8,128)(2,1)S(1)}, u32[]{:S(2)}, u32[]{:S(2)}) collective-permute-start(bf16[1,96,1536]{2,1,0:T(8,128)(2,1)S(1)} %add_convert_fusion.4), channel_id=1, source_target_pairs={{0,8},{2,10},{4,12},{6,14},{8,16},{10,18},{12,20},{14,22},{16,24},... | collective-permute-start | bytes 884744 | tf_op jit(solution)/shard_map/ppermute | solution.py:519
  758.6 19.5 %collective-permute-start.20 = (bf16[1,96,1536]{2,1,0:T(8,128)(2,1)S(1)}, bf16[1,96,1536]{2,1,0:T(8,128)(2,1)S(1)}, u32[]{:S(2)}, u32[]{:S(2)}) collective-permute-start(bf16[1,96,1536]{2,1,0:T(8,128)(2,1)S(1)} %add_convert_fusion.1), channel_id=1, source_target_pairs={{0,8},{2,10},{4,12},{6,14},{8,16},{10,18},{12,20},{14,22},{16,24},... | collective-permute-start | bytes 884744 | tf_op jit(solution)/shard_map/ppermute | solution.py:519
  854.2 5.8 collective-permute-start.22
  855.0 5.6 collective-permute-start.21
  (62 other events, 216.4 us)
Sparse Core Ops, SparseCore 0:
  12.1 91.3 all-gather.5
  106.4 51.5 all-gather.7
  160.3 87.2 all-gather.9
  249.7 51.5 all-gather.11
  321.8 72.6 reduce-scatter.6
  431.7 109.0 reduce-scatter.8
  544.7 75.3 reduce-scatter.10
  692.4 85.8 reduce-scatter.12

commit v4 on v3

--- a/solution.py
+++ b/solution.py
@@ -339,25 +339,28 @@
 LIGHT = pl.CostEstimate(flops=1000, bytes_accessed=1000, transcendentals=0)
 
 
-def product_t(a, b, out_dtype, columns=512):
-    rows, depth = a.shape
-    count = b.shape[0]
-
-    def body(a_ref, b_ref, o_ref):
+def product_t(a, b, out_dtype, half, columns=512):
+    rows = a.shape[0] // 2
+    count, depth = b.shape
+
+    def body(half_ref, a_ref, b_ref, o_ref):
         o_ref[...] = mm_t(a_ref[...], b_ref[...]).astype(out_dtype)
 
     return pl.pallas_call(
         body,
-        grid=(count // columns,),
-        in_specs=[
-            pl.BlockSpec((rows, depth), lambda j: (0, 0)),
-            pl.BlockSpec((columns, depth), lambda j: (j, 0)),
-        ],
-        out_specs=pl.BlockSpec((rows, columns), lambda j: (0, j)),
+        grid_spec=pltpu.PrefetchScalarGridSpec(
+            num_scalar_prefetch=1,
+            grid=(count // columns,),
+            in_specs=[
+                pl.BlockSpec((rows, depth), lambda j, h: (h[0], 0)),
+                pl.BlockSpec((columns, depth), lambda j, h: (j, 0)),
+            ],
+            out_specs=pl.BlockSpec((rows, columns), lambda j, h: (0, j)),
+        ),
         out_shape=jax.ShapeDtypeStruct((rows, count), out_dtype),
         compiler_params=pltpu.CompilerParams(vmem_limit_bytes=VMEM_LIMIT),
         cost_estimate=LIGHT,
-    )(a, b)
+    )(half.reshape(1), a, b)
 
 
 def t_product(a, b, out_dtype, first, count, columns=512):
@@ -521,6 +524,65 @@
             arrived = after(arrived, finish)
         moving = (arrived.astype(f32) + pick(2 * factor - 2 - step).astype(f32)).astype(blocks.dtype)
     return moving, arrived
+
+
+def sum_devices(v, spans):
+    size = lax.axis_size("dp")
+    for span in spans:
+        v = v + lax.ppermute(v, "dp", [(i, i ^ span) for i in range(size)])
+    return v
+
+
+def ring_gather(shard):
+    size = lax.axis_size("dp")
+    chips = size // 2
+    order = {8: (0, 2, 4, 6, 7, 5, 3, 1)}.get(chips, tuple(range(chips)))
+    index = lax.axis_index("dp")
+    core = index % 2
+    place = jnp.asarray([order.index(c) for c in range(chips)], jnp.int32)[index // 2]
+    chip_at = jnp.asarray(order, jnp.int32)
+    onward, back = [], []
+    for k in range(chips):
+        here, there = order[k], order[(k + 1) % chips]
+        for c in range(2):
+            onward.append((here * 2 + c, there * 2 + c))
+            back.append((there * 2 + c, here * 2 + c))
+    cores = [(i, i ^ 1) for i in range(size)]
+    whole_array = jnp.zeros((size,) + shard.shape, shard.dtype)
+    half = chips // 2
+    cut = (shard.shape[1] // 256) * LANES
+
+    def swap(piece):
+        return lax.ppermute(piece, "dp", cores)
+
+    def put(target, piece, other, position):
+        chip = chip_at[position % chips]
+        target = lax.dynamic_update_slice(target, piece[None], (chip * 2 + core, 0, 0))
+        return lax.dynamic_update_slice(target, other[None], (chip * 2 + 1 - core, 0, 0))
+
+    ahead = behind = shard
+    others = [swap(shard)]
+    places = [(shard, place)]
+    for step in range(1, half):
+        ahead = lax.ppermute(ahead, "dp", onward)
+        behind = lax.ppermute(behind, "dp", back)
+        ahead, behind, others = lax.optimization_barrier((ahead, behind, others))
+        places += [(ahead, place - step + chips), (behind, place + step)]
+        others = others + [swap(ahead), swap(behind)]
+    reached = behind
+    piece = jnp.concatenate(
+        [
+            lax.ppermute(ahead[:, :cut], "dp", onward),
+            lax.ppermute(behind[:, cut:], "dp", back),
+        ],
+        axis=1,
+    )
+    piece, others = lax.optimization_barrier((piece, others))
+    places.append((piece, place + half))
+    others = others + [swap(piece)]
+    for (got, position), other in zip(places, others):
+        whole_array = put(whole_array, got, other, position)
+    return whole_array.reshape((-1,) + shard.shape[1:]), reached
 
 
 def head_lanes(v):
@@ -572,8 +634,15 @@
             ],
             axis=1,
         )
-        in_weights.append(lax.all_gather(shard, "dp", axis=0, tiled=True))
-        out_weights.append(lax.all_gather(w_out[l].T, "dp", axis=0, tiled=True))
+        out_shard = w_out[l].T
+        if l == 0:
+            gathered, reached = ring_gather(shard)
+            in_weights.append(gathered)
+            out_shard = after(out_shard, reached)
+        else:
+            shard = after(shard, reached)
+            in_weights.append(lax.all_gather(shard, "dp", axis=0, tiled=True))
+        out_weights.append(lax.all_gather(out_shard, "dp", axis=0, tiled=True))
     params = []
     for l in range(layers):
         chan = jnp.zeros((8, width), f32)
@@ -650,14 +719,14 @@
             hidden_out = saved[l][0] + last_own + last_arrived.astype(f32)
         if l == 0:
             low, done_in = lax.optimization_barrier((low, done_in))
-        other = product_t(other_half(low), w_in, bf16)
+        other = product_t(low, w_in, bf16, 1 - tensor_index)
         arrived = pair_swap(other)
         low = after(low, other)
         if l > 0:
             grad_in = t_product(normed, low, bf16, 0, 2 * width)
             done_in = lax.psum_scatter(grad_in, "dp", scatter_dimension=0, tiled=True)
             low = after(low, grad_in)
-            own = product_t(own_half(low), w_in, f32)
+            own = product_t(low, w_in, f32, tensor_index)
             done_out = lax.psum_scatter(grad_out, "dp", scatter_dimension=0, tiled=True)
             arrived, own, done_out = lax.optimization_barrier((arrived, own, done_out))
             out_parts[l] = done_out
@@ -668,8 +737,13 @@
                 part = t_product(normed, low, bf16, i * width, width)
                 in_state.append(fold(row_blocks(part), 0)[0])
                 low = after(low, part)
-            own = product_t(own_half(after(low, in_state[0])), w_in, f32)
-            low = after(low, own)
+                if i == 0:
+                    side = t_mm(normed, low[:, 2 * width :])
+                    low = after(low, side)
+            own = product_t(after(low, in_state), w_in, f32, tensor_index)
+            for level in range(1, len(dp_factors()) - 1):
+                in_state = [fold(q, level)[0] for q in in_state]
+            arrived = after(arrived, in_state)
         normed_grad = own + arrived.astype(f32)
         unit = current * rms
         weighted = normed_grad * pre_gain[l][None, :]
@@ -683,35 +757,26 @@
         packed[l] = jnp.concatenate([gchan, gbc, gdt], axis=1)
         if l > 0:
             low_last = after(low_last, grad_rows)
-            side_last = t_mm(normed_last, low_last[:, 2 * width : 2 * width + 256 + heads])
-        else:
-            side = t_mm(normed, low[:, 2 * width : 2 * width + 256 + heads])
+            side_last = t_mm(normed_last, low_last[:, 2 * width :])
     done_out = lax.psum_scatter(grad_out, "dp", scatter_dimension=0, tiled=True)
-    done_out = after(done_out, (own, in_state[1]))
+    side_width = 384
+    side = jnp.concatenate([side, side_last], axis=1)
+    side_own = lax.psum_scatter(side, "dp", scatter_dimension=0, tiled=True)
     small = jnp.stack(packed)
-    spare = small.reshape(depth, -1)
-    side_width = 256 + heads
-    side = jnp.concatenate([side, side_last, spare], axis=1)
-    side = jnp.pad(side, ((0, 0), (0, -side.shape[1] % LANES)))
-    side = after(side, done_out)
-    side_own = lax.psum_scatter(side, "dp", scatter_dimension=0, tiled=True)
-    shares = side_own[:, 2 * side_width : 2 * side_width + spare.shape[1]].reshape(-1)
-    shares = lax.all_gather(shares, ("dp", "tensor"), axis=0, tiled=False)
-    shares = shares.reshape(-1, lax.axis_size("tensor"), shares.shape[-1])
-    mine = lax.dynamic_index_in_dim(shares, tensor_index, 1, keepdims=False).reshape(small.shape)
-    both = jnp.sum(shares, axis=1).reshape(small.shape)
     row = lax.broadcasted_iota(jnp.int32, small.shape, 1)
     col = lax.broadcasted_iota(jnp.int32, small.shape, 2)
     shared = ((row == 7) & (col < width)) | ((col >= width) & (col < width + 256))
-    small = jnp.where(shared, both, mine)
+    small = small + jnp.where(shared, pair_swap(small), 0.0)
+    spans = [1]
+    while spans[-1] * 2 < lax.axis_size("dp"):
+        spans.append(spans[-1] * 2)
+    small = sum_devices(small, spans[:1] + spans[:1:-1])
     queue = in_state
-    for level in range(1, len(dp_factors())):
-        last_level = level == len(dp_factors()) - 1
-        last_arrival = None
-        for n in range(len(queue)):
-            queue[n], last_arrival = fold(
-                queue[n], level, start=None if last_level else last_arrival
-            )
+    level = len(dp_factors()) - 1
+    for n in range(len(queue)):
+        marks = (small, small, side_own) if n == len(queue) - 1 else ()
+        queue[n], _ = fold(queue[n], level, marks=marks)
+    small = sum_devices(after(small, queue[0]), spans[1:2])
     done = [q.reshape(q.shape[1:]) for q in queue]
     out_parts[0] = done_out
     in_parts = [jnp.concatenate(done, axis=1), done_in]
@@ -721,7 +786,7 @@
         outputs[l] = (
             in_parts[l].astype(f32).reshape(-1, 2, width),
             grad_bc + pair_swap(grad_bc),
-            side_parts[l][:, 256:],
+            side_parts[l][:, 256 : 256 + heads],
             out_parts[l].astype(f32).T,
         )
     grad_w_zx, grad_w_bc, grad_w_dt, grad_w_out = (

time: 873 us -> 830 us (0.951)
  blocking collectives: 66.2 us -> 0 us
  starting transfers between devices: 20 us -> 53.3 us
  waiting for transfers between devices: 262 us -> 236 us
  between operations: 15.6 us -> 27.9 us
    ppermute x0 -> x20, waiting for transfers between devices: none -> 68.9 us  [the longest x3 30.5 us: ring_gather(): ahead = lax.ppermute(ahead, 'dp', onward)]
    all_gather x1 -> x0, blocking collectives: 66.2 us -> none  [local(): shares = lax.all_gather(shares, ('dp', 'tensor'), axis=0, tiled=False)]
    ppermute x13 -> x14, waiting for transfers between devices: 179 us -> 123 us  [pair_swap(): return lax.ppermute(v, 'tensor', ((0, 1), (1, 0)))]
    ppermute x10, waiting for transfers between devices: 73.2 us -> 44.6 us  [fold(): arrived = lax.ppermute(moving, 'dp', hops)]
    dynamic_update_slice x0 -> x15, local copies, waits for them, and re-layouts: none -> 22.7 us  [the longest x8 11.9 us: put(): lax.dynamic_update_slice(target, other[None], (chip * 2 + 1 - core, 0, 0))]
    ppermute x10, starting transfers between devices: 1.5 us -> 19.4 us  [fold(): arrived = lax.ppermute(moving, 'dp', hops)]
    ppermute x0 -> x20, starting transfers between devices: none -> 14.8 us  [the longest x3 5.2 us: ring_gather(): behind = lax.ppermute(behind, 'dp', back)]
    dynamic_slice x5 -> x2, local copies, waits for them, and re-layouts: 15 us -> 1.24 us  [the longest x1 0.66 us: put(): chip = chip_at[position % chips]]
  transfers between devices with their start and end apart: 31 -> 51, of which waited for: 17 -> 26; matrix products, arithmetic and copies ran while one was open for 27% -> 30% of each run, Pallas kernels for 26% -> 28%
where the time goes in v4:
time: 830 us; the launch traced here: 822 us
  waiting for transfers between devices  236 us (28%)
  Pallas kernels  229 us (28%)
  local copies, waits for them, and re-layouts  107 us (13%)
  matrix products  102 us (12%)
  other arithmetic  67.1 us (8%)
  starting transfers between devices  53.3 us (6%)
  between operations  27.9 us (3%)
    ppermute x14, waiting for transfers between devices, pair_swap(): return lax.ppermute(v, 'tensor', ((0, 1), (1, 0)))  123 us
    pallas_call x2, Pallas kernels, mixer_backward(): pl.pallas_call(functools.partial(bwd_kernel, head_count=width // HEADDIM)...  103 us
    pallas_call x2, Pallas kernels, mixer_forward(): pl.pallas_call(functools.partial(fwd_kernel, head_count=width // HEADDIM)...  57.6 us
    dot_general x4, matrix products, mm(): lax.dot_general(a, b, (((1,), (0,)), ((), ())), precision=precision, pref...  53.7 us
    ppermute x10, waiting for transfers between devices, fold(): arrived = lax.ppermute(moving, 'dp', hops)  44.6 us
    pallas_call x4, Pallas kernels, product_t(): pl.pallas_call(body, grid_spec=pltpu.PrefetchScalarGridSpec(num_scalar_pr...  38.4 us
    unnamed x240, local copies, waits for them, and re-layouts  38 us
    pallas_call x3, Pallas kernels, t_product(): pl.pallas_call(body, grid=(count // columns,), in_specs=[pl.BlockSpec((de...  30.6 us
  transfers between devices with their start and end apart: 51, of which 26 were waited for; matrix products, arithmetic and copies ran while one was open for 30% of the time, Pallas kernels for 28%

profile of v4, /device:TPU:0, one launch (start us, length us, event | category | flops | bytes accessed | tf_op | source)
XLA Modules:
  0.0 822.5 jit_solution(3416269674050455619)
XLA Ops:
  9.0 3.0 fusion.48
  12.9 3.0 collective-permute-start.2
  16.1 14.8 %collective-permute-done.2 = bf16[96,3456]{1,0:T(8,128)(2,1)S(1)} collective-permute-done((bf16[96,3456]{1,0:T(8,128)(2,1)S(1)}, bf16[96,3456]{1,0:T(8,128)(2,1)S(1)}, u32[]{:S(2)}, u32[]{:S(2)}) %collective-permute-start.2) | collective-permute-done | bytes 663584 | tf_op jit(solution)/shard_map/ppermute | solution.py:568
  34.6 15.1 %collective-permute-done.4 = bf16[96,3456]{1,0:T(8,128)(2,1)S(1)} collective-permute-done((bf16[96,3456]{1,0:T(8,128)(2,1)S(1)}, bf16[96,3456]{1,0:T(8,128)(2,1)S(1)}, u32[]{:S(2)}, u32[]{:S(2)}) %collective-permute-start.4) | collective-permute-done | bytes 663584 | tf_op jit(solution)/shard_map/ppermute | solution.py:567
  53.5 14.1 %collective-permute-done.8 = bf16[96,3456]{1,0:T(8,128)(2,1)} collective-permute-done((bf16[96,3456]{1,0:T(8,128)(2,1)S(1)}, bf16[96,3456]{1,0:T(8,128)(2,1)}, u32[]{:S(2)}, u32[]{:S(2)}) %collective-permute-start.8) | collective-permute-done | bytes 663584 | tf_op jit(solution)/shard_map/ppermute | solution.py:567
  71.6 3.3 pad_maximum_fusion.2
  88.6 4.7 broadcast_in_dim.41
  106.6 12.4 %collective-permute-done.12 = bf16[96,1664]{1,0:T(8,128)(2,1)S(1)} collective-permute-done((bf16[96,1664]{1,0:T(8,128)(2,1)}, bf16[96,1664]{1,0:T(8,128)(2,1)S(1)}, u32[]{:S(2)}, u32[]{:S(2)}) %collective-permute-start.12) | collective-permute-done | bytes 319520 | tf_op jit(solution)/shard_map/ppermute | solution.py:575
  144.8 3.2 fusion.47
  150.0 17.4 %fusion.57.zx_ref.bcdt_ref.xprev_ref.bcprev_ref = f32[1024,3456]{1,0:T(8,128)} fusion(bf16[1024,1536]{1,0:T(8,128)(2,1)S(1)} %fusion.5.a_ref, bf16[1536,3456]{1,0:T(8,128)(2,1)} %bitcast.27.b_ref), kind=kOutput, calls=%fused_computation.183 | convolution fusion | flops 10871635968 | bytes 27918336 | tf_op jit(solution)/shard_map/dot_general | solution.py:26
  167.4 29.1 %shard_map.280 = (f32[1024,1536]{1,0:T(8,128)}, bf16[1024,1536]{1,0:T(8,128)(2,1)S(1)}, bf16[8,128,1536]{2,1,0:T(8,128)(2,1)}, f32[1024,128]{1,0:T(8,128)S(1)}) custom-call(f32[1024,3456]{1,0:T(8,128)} %fusion.57.zx_ref.bcdt_ref.xprev_ref.bcprev_ref, f32[1024,3456]{1,0:T(8,128)} %fusion.57.zx_ref.bcdt_ref.xprev_ref.bcprev_ref, ...), custom_call_target="tpu_custom_call" | custom-call | flops 1000 | bytes 1000 | tf_op jit(solution)/shard_map/pallas_call | solution.py:393
  202.8 3.2 multiply_convert_fusion.1
  206.0 7.2 convolution_convert_fusion.2
  214.7 32.6 %collective-permute-done.18 = bf16[512,1536]{1,0:T(8,128)(2,1)} collective-permute-done((bf16[512,1536]{1,0:T(8,128)(2,1)}, bf16[512,1536]{1,0:T(8,128)(2,1)}, u32[]{:S(2)}, u32[]{:S(2)}) %collective-permute-start.18) | collective-permute-done | bytes 1572896 | tf_op jit(solution)/shard_map/ppermute | solution.py:475
  247.3 8.2 multiply_reduce_fusion.8
  264.9 26.1 %collective-permute-done.19 = bf16[512,1536]{1,0:T(8,128)(2,1)} collective-permute-done((bf16[512,1536]{1,0:T(8,128)(2,1)}, bf16[512,1536]{1,0:T(8,128)(2,1)}, u32[]{:S(2)}, u32[]{:S(2)}) %collective-permute-start.19) | collective-permute-done | bytes 1572896 | tf_op jit(solution)/shard_map/ppermute | solution.py:475
  291.0 3.3 maximum_select_fusion.a_ref
  294.4 18.2 %fusion.58.zx_ref.bcdt_ref.xprev_ref.bcprev_ref = f32[1024,3456]{1,0:T(8,128)} fusion(bf16[1024,1536]{1,0:T(8,128)(2,1)S(1)} %maximum_select_fusion.a_ref, bf16[1536,3456]{1,0:T(8,128)(2,1)} %all-gather.6.cloned.1.call-done.b_ref), kind=kOutput, calls=%fused_computation.184 | convolution fusion | flops 10871635968 | bytes 27918336 | tf_op jit(solution)/shard_map/dot_general | solution.py:26
  312.6 28.5 %shard_map.281 = (f32[1024,1536]{1,0:T(8,128)}, bf16[1024,1536]{1,0:T(8,128)(2,1)S(1)}, bf16[8,128,1536]{2,1,0:T(8,128)(2,1)}, f32[1024,128]{1,0:T(8,128)S(1)}) custom-call(f32[1024,3456]{1,0:T(8,128)} %fusion.58.zx_ref.bcdt_ref.xprev_ref.bcprev_ref, f32[1024,3456]{1,0:T(8,128)} %fusion.58.zx_ref.bcdt_ref.xprev_ref.bcprev_ref, f32[4,1536]{1,0:T(4,128)S(1)} %copy-done.24, ...), custom_call_target="tpu_custom_call" | custom-call | flops 1000 | bytes 1000 | tf_op jit(solution)/shard_map/pallas_call | solution.py:393
  346.5 3.6 fusion.6
  353.5 7.0 convolution_convert_fusion.1
  360.8 5.2 fusion.15
  366.8 4.5 multiply_reduce_fusion.7
  375.6 7.0 fusion.59.sg_ref
  390.5 51.1 %shard_map.282 = (bf16[1024,3456]{1,0:T(8,128)(2,1)}, f32[8,1536]{1,0:T(8,128)S(1)}, f32[8,256]{1,0:T(8,128)S(1)}, f32[8,128]{1,0:T(8,128)S(1)}) custom-call(f32[1024,1536]{1,0:T(8,128)} %fusion.59.sg_ref, f32[1024,3456]{1,0:T(8,128)} %fusion.58.zx_ref.bcdt_ref.xprev_ref.bcprev_ref, f32[1024,3456]{1,0:T(8,128)} %fusion.58.zx_ref.bcdt_ref.xprev_ref.bcprev_ref, ...), custom_call_target="tpu_custom_call" | custom-call | flops 1000 | bytes 1000 | tf_op jit(solution)/shard_map/pallas_call | solution.py:433
  441.5 9.5 %shard_map.283 = bf16[512,1536]{1,0:T(8,128)(2,1)S(1)} custom-call(s32[1]{0:T(128)} %bitcast.57.half_ref, bf16[1024,3456]{1,0:T(8,128)(2,1)} %get-tuple-element.279.a_ref.b_ref, bf16[1536,3456]{1,0:T(8,128)(2,1)} %all-gather.6.cloned.1.call-done.b_ref), custom_call_target="tpu_custom_call" | custom-call | flops 1000 | bytes 1000 | tf_op jit(solution)/shard_map/pallas_call | solution.py:349
  452.2 13.8 %shard_map.284 = bf16[1536,3072]{1,0:T(8,128)(2,1)} custom-call(bf16[1024,1536]{1,0:T(8,128)(2,1)S(1)} %maximum_select_fusion.a_ref, bf16[1024,3456]{1,0:T(8,128)(2,1)} %get-tuple-element.279.a_ref.b_ref), custom_call_target="tpu_custom_call" | custom-call | flops 1000 | bytes 1000 | tf_op jit(solution)/shard_map/pallas_call | solution.py:373
  467.8 9.6 %shard_map.285 = f32[512,1536]{1,0:T(8,128)S(1)} custom-call(s32[1]{0:T(128)} %bitcast.58.half_ref, bf16[1024,3456]{1,0:T(8,128)(2,1)} %get-tuple-element.279.a_ref.b_ref, bf16[1536,3456]{1,0:T(8,128)(2,1)} %all-gather.6.cloned.1.call-done.b_ref), custom_call_target="tpu_custom_call" | custom-call | flops 1000 | bytes 1000 | tf_op jit(solution)/shard_map/pallas_call | solution.py:349
  479.0 18.5 %collective-permute-done.23 = bf16[512,1536]{1,0:T(8,128)(2,1)} collective-permute-done((bf16[512,1536]{1,0:T(8,128)(2,1)}, bf16[512,1536]{1,0:T(8,128)(2,1)}, u32[]{:S(2)}, u32[]{:S(2)}) %collective-permute-start.23) | collective-permute-done | bytes 1572896 | tf_op jit(solution)/shard_map/ppermute | solution.py:475
  497.6 5.9 multiply_reduce_fusion
  504.7 6.7 multiply_reduce_fusion.4
  512.9 29.4 %collective-permute-done.24 = bf16[512,1536]{1,0:T(8,128)(2,1)S(1)} collective-permute-done((bf16[512,1536]{1,0:T(8,128)(2,1)S(1)}, bf16[512,1536]{1,0:T(8,128)(2,1)S(1)}, u32[]{:S(2)}, u32[]{:S(2)}) %collective-permute-start.24) | collective-permute-done | bytes 1572896 | tf_op jit(solution)/shard_map/ppermute | solution.py:475
  543.5 6.8 convolution_convert_fusion
  555.1 11.1 %fusion.33.sg_ref = f32[1024,1536]{1,0:T(8,128)} fusion(bf16[1536,1536]{1,0:T(8,128)(2,1)} %all-gather.4.cloned.1.call-done, bf16[512,1536]{1,0:T(8,128)(2,1)} %copy-done.110, bf16[512,1536]{1,0:T(8,128)(2,1)S(1)} %copy-done.62, pred[]{:T(512)S(6)} %eq.164), kind=kOutput, calls=%fused_computation.99 | convolution fusion | flops 4845993984 | bytes 14155777 | tf_op jit(solution)/shard_map/dot_general | solution.py:26
  566.3 51.5 %shard_map.286 = (bf16[1024,3456]{1,0:T(8,128)(2,1)}, f32[8,1536]{1,0:T(8,128)S(1)}, f32[8,256]{1,0:T(8,128)S(1)}, f32[8,128]{1,0:T(8,128)S(1)}) custom-call(f32[1024,1536]{1,0:T(8,128)} %fusion.33.sg_ref, f32[1024,3456]{1,0:T(8,128)} %fusion.57.zx_ref.bcdt_ref.xprev_ref.bcprev_ref, f32[1024,3456]{1,0:T(8,128)} %fusion.57.zx_ref.bcdt_ref.xprev_ref.bcprev_ref, ...), custom_call_target="tpu_custom_call" | custom-call | flops 1000 | bytes 1000 | tf_op jit(solution)/shard_map/pallas_call | solution.py:433
  617.8 9.6 %shard_map.287 = bf16[512,1536]{1,0:T(8,128)(2,1)S(1)} custom-call(s32[1]{0:T(128)} %bitcast.57.half_ref, bf16[1024,3456]{1,0:T(8,128)(2,1)} %get-tuple-element.268.a_ref.b_ref, bf16[1536,3456]{1,0:T(8,128)(2,1)} %bitcast.27.b_ref), custom_call_target="tpu_custom_call" | custom-call | flops 1000 | bytes 1000 | tf_op jit(solution)/shard_map/pallas_call | solution.py:349
  627.4 8.5 %shard_map.288 = bf16[1536,1536]{1,0:T(8,128)(2,1)} custom-call(bf16[1024,1536]{1,0:T(8,128)(2,1)S(1)} %copy-done.1, bf16[1024,3456]{1,0:T(8,128)(2,1)} %get-tuple-element.268.a_ref.b_ref), custom_call_target="tpu_custom_call" | custom-call | flops 1000 | bytes 1000 | tf_op jit(solution)/shard_map/pallas_call | solution.py:373
  636.0 3.2 dynamic-slice_bitcast_fusion.1
  639.2 4.0 fusion.26
  643.1 8.2 shard_map.289
  651.4 3.2 dynamic-slice_bitcast_fusion
  655.2 5.1 fusion.24
  660.3 3.1 fusion.1
  664.7 9.3 %collective-permute-start.29 = (bf16[4,96,1536]{2,1,0:T(8,128)(2,1)}, bf16[4,96,1536]{2,1,0:T(8,128)(2,1)}, u32[]{:S(2)}, u32[]{:S(2)}) collective-permute-start(bf16[4,96,1536]{2,1,0:T(8,128)(2,1)} %dynamic-slice_bitcast_fusion.3), channel_id=1, source_target_pairs={{0,4},{2,6},{4,0},{6,2},{8,12},{10,14},{12,8},{14,10},{16,20},{18,... | collective-permute-start | bytes 3538952 | tf_op jit(solution)/shard_map/ppermute | solution.py:522
  674.0 2.3 fusion
  683.0 2.9 stack_reshape.5
  687.8 4.9 pad_maximum_fusion
  692.7 6.1 copy.66
  698.8 9.7 %shard_map.290 = f32[512,1536]{1,0:T(8,128)S(1)} custom-call(s32[1]{0:T(128)} %bitcast.58.half_ref, bf16[1024,3456]{1,0:T(8,128)(2,1)} %get-tuple-element.268.a_ref.b_ref, bf16[1536,3456]{1,0:T(8,128)(2,1)} %bitcast.27.b_ref), custom_call_target="tpu_custom_call" | custom-call | flops 1000 | bytes 1000 | tf_op jit(solution)/shard_map/pallas_call | solution.py:349
  708.6 2.8 fusion.14
  714.3 11.5 %collective-permute-done.30 = bf16[4,96,1536]{2,1,0:T(8,128)(2,1)} collective-permute-done((bf16[4,96,1536]{2,1,0:T(8,128)(2,1)}, bf16[4,96,1536]{2,1,0:T(8,128)(2,1)}, u32[]{:S(2)}, u32[]{:S(2)}) %collective-permute-start.30) | collective-permute-done | bytes 1179680 | tf_op jit(solution)/shard_map/ppermute | solution.py:522
  725.8 2.6 fusion.13
  728.4 2.9 multiply_reduce_fusion.2
  733.4 3.6 collective-permute-done.31
  740.3 2.4 collective-permute-start.33
  742.7 12.6 %collective-permute-done.36 = bf16[1,96,1536]{2,1,0:T(8,128)(2,1)S(1)} collective-permute-done((bf16[1,96,1536]{2,1,0:T(8,128)(2,1)S(1)}, bf16[1,96,1536]{2,1,0:T(8,128)(2,1)S(1)}, u32[]{:S(2)}, u32[]{:S(2)}) %collective-permute-start.36) | collective-permute-done | bytes 294944 | tf_op jit(solution)/shard_map/ppermute | solution.py:522
  756.3 4.5 collective-permute-start.37
  760.8 5.5 fusion.11
  766.2 2.4 collective-permute-done.33
  769.4 4.7 collective-permute-done.34
  776.9 13.7 %collective-permute-done.39 = bf16[1,96,1536]{2,1,0:T(8,128)(2,1)S(1)} collective-permute-done((bf16[1,96,1536]{2,1,0:T(8,128)(2,1)S(1)}, bf16[1,96,1536]{2,1,0:T(8,128)(2,1)S(1)}, u32[]{:S(2)}, u32[]{:S(2)}) %collective-permute-start.39) | collective-permute-done | bytes 294944 | tf_op jit(solution)/shard_map/ppermute | solution.py:522
  796.0 4.0 collective-permute-done.40
  809.0 2.9 collective-permute-done.41
  812.2 3.2 copy.64
  (450 shorter events, 146.9 us)
Async XLA Ops:
  7.2 45.5 %copy-start.77 = (bf16[2,1536,96]{1,2,0:T(8,128)(2,1)S(1)}, bf16[2,1536,96]{1,2,0:T(8,128)(2,1)}, u32[]{:S(2)}) copy-start(bf16[2,1536,96]{1,2,0:T(8,128)(2,1)} %param.54) | copy-start | bytes 1769476
  7.2 198.8 %all-gather.4.cloned.1.call-start = ((), (), s32[]{:S(2)}) async-start(), calls=%async_computation.4 | async-start | bytes 5013504 | tf_op jit(solution)/shard_map/all_gather | solution.py:645
  8.9 60.5 %copy-start.85 = (f32[2,1536]{1,0:T(2,128)S(1)}, f32[2,1536]{1,0:T(2,128)}, u32[]{:S(2)}) copy-start(f32[2,1536]{1,0:T(2,128)} %param.42) | copy-start | bytes 36868
  8.9 61.1 %copy-start.38 = (bf16[512,1536]{1,0:T(8,128)(2,1)S(1)}, bf16[512,1536]{1,0:T(8,128)(2,1)}, u32[]{:S(2)}) copy-start(bf16[512,1536]{1,0:T(8,128)(2,1)} %param.41) | copy-start | bytes 4718596
  12.9 18.0 %collective-permute-start.2 = (bf16[96,3456]{1,0:T(8,128)(2,1)S(1)}, bf16[96,3456]{1,0:T(8,128)(2,1)S(1)}, u32[]{:S(2)}, u32[]{:S(2)}) collective-permute-start(bf16[96,3456]{1,0:T(8,128)(2,1)S(1)} %fusion.31), channel_id=1, source_target_pairs={{8,0},{10,2},{16,8},{18,10},{24,16},{26,18},{28,24},{30,26},{20,28... | collective-permute-start | bytes 1990664 | tf_op jit(solution)/shard_map/ppermute | solution.py:568
  15.9 16.4 %collective-permute-start.1 = (bf16[96,3456]{1,0:T(8,128)(2,1)S(1)}, bf16[96,3456]{1,0:T(8,128)(2,1)S(1)}, u32[]{:S(2)}, u32[]{:S(2)}) collective-permute-start(bf16[96,3456]{1,0:T(8,128)(2,1)S(1)} %fusion.31), channel_id=1, source_target_pairs={{0,8},{2,10},{8,16},{10,18},{16,24},{18,26},{24,28},{26,30},{28,20... | collective-permute-start | bytes 1990664 | tf_op jit(solution)/shard_map/ppermute | solution.py:567
  16.1 16.3 %collective-permute-start.3 = (bf16[96,3456]{1,0:T(8,128)(2,1)S(1)}, bf16[96,3456]{1,0:T(8,128)(2,1)S(1)}, u32[]{:S(2)}, u32[]{:S(2)}) collective-permute-start(bf16[96,3456]{1,0:T(8,128)(2,1)S(1)} %fusion.31), channel_id=1, source_target_pairs={{0,2},{2,0},{4,6},{6,4},{8,10},{10,8},{12,14},{14,12},{16,18},{18,... | collective-permute-start | bytes 1990664 | tf_op jit(solution)/shard_map/ppermute | solution.py:556
  32.3 2.3 collective-permute-start.6
  32.4 17.3 %collective-permute-start.4 = (bf16[96,3456]{1,0:T(8,128)(2,1)S(1)}, bf16[96,3456]{1,0:T(8,128)(2,1)S(1)}, u32[]{:S(2)}, u32[]{:S(2)}) collective-permute-start(bf16[96,3456]{1,0:T(8,128)(2,1)S(1)} %collective-permute-done.1), channel_id=1, source_target_pairs={{0,8},{2,10},{8,16},{10,18},{16,24},{18,26},{24,28},{26,30},{28,20... | collective-permute-start | bytes 1990664 | tf_op jit(solution)/shard_map/ppermute | solution.py:567
  32.8 16.9 %collective-permute-start.7 = (bf16[96,3456]{1,0:T(8,128)(2,1)S(1)}, bf16[96,3456]{1,0:T(8,128)(2,1)S(1)}, u32[]{:S(2)}, u32[]{:S(2)}) collective-permute-start(bf16[96,3456]{1,0:T(8,128)(2,1)S(1)} %collective-permute-done.2), channel_id=1, source_target_pairs={{0,2},{2,0},{4,6},{6,4},{8,10},{10,8},{12,14},{14,12},{16,18},{18,... | collective-permute-start | bytes 1990664 | tf_op jit(solution)/shard_map/ppermute | solution.py:556
  33.0 17.2 %collective-permute-start.5 = (bf16[96,3456]{1,0:T(8,128)(2,1)S(1)}, bf16[96,3456]{1,0:T(8,128)(2,1)S(1)}, u32[]{:S(2)}, u32[]{:S(2)}) collective-permute-start(bf16[96,3456]{1,0:T(8,128)(2,1)S(1)} %collective-permute-done.2), channel_id=1, source_target_pairs={{8,0},{10,2},{16,8},{18,10},{24,16},{26,18},{28,24},{30,26},{20,28... | collective-permute-start | bytes 1990664 | tf_op jit(solution)/shard_map/ppermute | solution.py:568
  50.2 3.3 collective-permute-start.10
  50.5 17.1 %collective-permute-start.8 = (bf16[96,3456]{1,0:T(8,128)(2,1)S(1)}, bf16[96,3456]{1,0:T(8,128)(2,1)}, u32[]{:S(2)}, u32[]{:S(2)}) collective-permute-start(bf16[96,3456]{1,0:T(8,128)(2,1)S(1)} %collective-permute-done.4), channel_id=1, source_target_pairs={{0,8},{2,10},{8,16},{10,18},{16,24},{18,26},{24,28},{26,30},{28,20... | collective-permute-start | bytes 1990664 | tf_op jit(solution)/shard_map/ppermute | solution.py:567
  51.9 15.7 %collective-permute-start.11 = (bf16[96,3456]{1,0:T(8,128)(2,1)S(1)}, bf16[96,3456]{1,0:T(8,128)(2,1)S(1)}, u32[]{:S(2)}, u32[]{:S(2)}) collective-permute-start(bf16[96,3456]{1,0:T(8,128)(2,1)S(1)} %collective-permute-done.5), channel_id=1, source_target_pairs={{0,2},{2,0},{4,6},{6,4},{8,10},{10,8},{12,14},{14,12},{16,18},{18,... | collective-permute-start | bytes 1990664 | tf_op jit(solution)/shard_map/ppermute | solution.py:556
  52.1 17.3 %collective-permute-start.9 = (bf16[96,3456]{1,0:T(8,128)(2,1)S(1)}, bf16[96,3456]{1,0:T(8,128)(2,1)}, u32[]{:S(2)}, u32[]{:S(2)}) collective-permute-start(bf16[96,3456]{1,0:T(8,128)(2,1)S(1)} %collective-permute-done.5), channel_id=1, source_target_pairs={{8,0},{10,2},{16,8},{18,10},{24,16},{26,18},{28,24},{30,26},{20,28... | collective-permute-start | bytes 1990664 | tf_op jit(solution)/shard_map/ppermute | solution.py:568
  69.4 225.0 %all-gather.6.cloned.1.call-start = ((), (), s32[]{:S(2)}) async-start(), calls=%async_computation.5 | async-start | bytes 11280384 | tf_op jit(solution)/shard_map/all_gather | solution.py:644
  74.9 69.9 %collective-permute-start = (bf16[1024,1536]{1,0:T(8,128)(2,1)}, bf16[1024,1536]{1,0:T(8,128)(2,1)}, u32[]{:S(2)}, u32[]{:S(2)}) collective-permute-start(bf16[1024,1536]{1,0:T(8,128)(2,1)} %pad_maximum_fusion.2), channel_id=1, source_target_pairs={{0,1},{1,0},{2,3},{3,2},{4,5},{5,4},{6,7},{7,6},{8,9},{9,8},{10,11... | collective-permute-start | bytes 9437192 | tf_op jit(solution)/shard_map/ppermute | solution.py:475
  86.6 80.7 %copy-start.30 = (f32[4,256]{1,0:T(4,128)}, f32[4,256]{1,0:T(4,128)S(1)}, u32[]{:S(2)}) copy-start(f32[4,256]{1,0:T(4,128)S(1)} %get-tuple-element.376.bct_ref) | copy-start | bytes 12292
  88.4 78.9 %copy-start.22 = (f32[4,1536]{1,0:T(4,128)}, f32[4,1536]{1,0:T(4,128)S(1)}, u32[]{:S(2)}) copy-start(f32[4,1536]{1,0:T(4,128)S(1)} %get-tuple-element.366.taps_ref) | copy-start | bytes 73732
  96.1 24.7 %collective-permute-start.13 = (bf16[96,1792]{1,0:T(8,128)(2,1)S(1)}, bf16[96,1792]{1,0:T(8,128)(2,1)S(1)}, u32[]{:S(2)}, u32[]{:S(2)}) collective-permute-start(bf16[96,1792]{1,0:T(8,128)(2,1)S(1)} %slice.327), channel_id=1, source_target_pairs={{8,0},{10,2},{16,8},{18,10},{24,16},{26,18},{28,24},{30,26},{20,28... | collective-permute-start | bytes 1032200 | tf_op jit(solution)/shard_map/ppermute | solution.py:576
  104.0 15.0 %collective-permute-start.12 = (bf16[96,1664]{1,0:T(8,128)(2,1)}, bf16[96,1664]{1,0:T(8,128)(2,1)S(1)}, u32[]{:S(2)}, u32[]{:S(2)}) collective-permute-start(bf16[96,1664]{1,0:T(8,128)(2,1)} %slice.326), channel_id=1, source_target_pairs={{0,8},{2,10},{8,16},{10,18},{16,24},{18,26},{24,28},{26,30},{28,20... | collective-permute-start | bytes 958472 | tf_op jit(solution)/shard_map/ppermute | solution.py:575
  105.4 62.0 %copy-start.28 = (f32[8,128]{1,0:T(8,128)}, f32[8,128]{1,0:T(8,128)S(1)}, u32[]{:S(2)}) copy-start(f32[8,128]{1,0:T(8,128)S(1)} %scatter.46.dtv_ref) | copy-start | bytes 12292
  105.7 61.7 %copy-start.17 = (f32[8,1536]{1,0:T(8,128)}, f32[8,1536]{1,0:T(8,128)S(1)}, u32[]{:S(2)}) copy-start(f32[8,1536]{1,0:T(8,128)S(1)} %scatter.44.chan_ref) | copy-start | bytes 147460
  105.7 15.1 %collective-permute-start.14 = (bf16[96,3456]{1,0:T(8,128)(2,1)}, bf16[96,3456]{1,0:T(8,128)(2,1)}, u32[]{:S(2)}, u32[]{:S(2)}) collective-permute-start(bf16[96,3456]{1,0:T(8,128)(2,1)} %collective-permute-done.8), channel_id=1, source_target_pairs={{0,2},{2,0},{4,6},{6,4},{8,10},{10,8},{12,14},{14,12},{16,18},{18,... | collective-permute-start | bytes 1990664 | tf_op jit(solution)/shard_map/ppermute | solution.py:556
  105.8 15.1 %collective-permute-start.15 = (bf16[96,3456]{1,0:T(8,128)(2,1)}, bf16[96,3456]{1,0:T(8,128)(2,1)}, u32[]{:S(2)}, u32[]{:S(2)}) collective-permute-start(bf16[96,3456]{1,0:T(8,128)(2,1)} %collective-permute-done.9), channel_id=1, source_target_pairs={{0,2},{2,0},{4,6},{6,4},{8,10},{10,8},{12,14},{14,12},{16,18},{18,... | collective-permute-start | bytes 1990664 | tf_op jit(solution)/shard_map/ppermute | solution.py:556
  106.3 61.1 %copy-start.32 = (f32[1,256]{1,0:T(1,128)}, f32[1,256]{1,0:T(1,128)S(1)}, u32[]{:S(2)}) copy-start(f32[1,256]{1,0:T(1,128)S(1)} %get-tuple-element.378.bcb_ref) | copy-start | bytes 3076
  106.3 254.4 %all-gather.8.cloned.1.call-start = ((), (), s32[]{:S(2)}) async-start(), calls=%async_computation.6 | async-start | bytes 5013504 | tf_op jit(solution)/shard_map/all_gather | solution.py:645
  120.9 28.1 %collective-permute-start.16 = (bf16[96,3456]{1,0:T(8,128)(2,1)S(1)}, bf16[96,3456]{1,0:T(8,128)(2,1)S(1)}, u32[]{:S(2)}, u32[]{:S(2)}) collective-permute-start(bf16[96,3456]{1,0:T(8,128)(2,1)S(1)} %pad_maximum_fusion.4), channel_id=1, source_target_pairs={{0,2},{2,0},{4,6},{6,4},{8,10},{10,8},{12,14},{14,12},{16,18},{18,... | collective-permute-start | bytes 1990664 | tf_op jit(solution)/shard_map/ppermute | solution.py:556
  198.5 3.7 collective-permute-start.17
  213.2 34.1 %collective-permute-start.18 = (bf16[512,1536]{1,0:T(8,128)(2,1)}, bf16[512,1536]{1,0:T(8,128)(2,1)}, u32[]{:S(2)}, u32[]{:S(2)}) collective-permute-start(bf16[512,1536]{1,0:T(8,128)(2,1)} %convolution_convert_fusion.2), channel_id=1, source_target_pairs={{0,1},{1,0},{2,3},{3,2},{4,5},{5,4},{6,7},{7,6},{8,9},{9,8},{10,11... | collective-permute-start | bytes 4718600 | tf_op jit(solution)/shard_map/ppermute | solution.py:475
  214.6 282.9 %reduce-scatter.7.cloned.1.call-start = ((), (), s32[]{:S(2)}) async-start(), calls=%async_computation.7 | async-start | bytes 5013504 | tf_op jit(solution)/shard_map/reduce_scatter | solution.py:730
  214.7 40.8 %copy-start.80 = (f32[1536]{0:T(1024)S(1)}, f32[1536]{0:T(1024)}, u32[]{:S(2)}) copy-start(f32[1536]{0:T(1024)} %get-tuple-element.336) | copy-start | bytes 18436
  257.3 33.7 %collective-permute-start.19 = (bf16[512,1536]{1,0:T(8,128)(2,1)}, bf16[512,1536]{1,0:T(8,128)(2,1)}, u32[]{:S(2)}, u32[]{:S(2)}) collective-permute-start(bf16[512,1536]{1,0:T(8,128)(2,1)} %multiply_convert_fusion.2), channel_id=1, source_target_pairs={{0,1},{1,0},{2,3},{3,2},{4,5},{5,4},{6,7},{7,6},{8,9},{9,8},{10,11... | collective-permute-start | bytes 4718600 | tf_op jit(solution)/shard_map/ppermute | solution.py:475
  294.3 203.2 %copy-start.2 = (bf16[1024,1536]{1,0:T(8,128)(2,1)}, bf16[1024,1536]{1,0:T(8,128)(2,1)S(1)}, u32[]{:S(2)}) copy-start(bf16[1024,1536]{1,0:T(8,128)(2,1)S(1)} %maximum_select_fusion.a_ref) | copy-start | bytes 9437188
  344.9 5.2 collective-permute-start.20
  360.5 257.3 %reduce-scatter.9.cloned.1.call-start = ((), (), s32[]{:S(2)}) async-start(), calls=%async_computation.8 | async-start | bytes 10027008 | tf_op jit(solution)/shard_map/reduce_scatter | solution.py:727
  371.3 3.8 collective-permute-start.21
  375.1 66.4 %collective-permute-start.22 = (bf16[512,1536]{1,0:T(8,128)(2,1)}, bf16[512,1536]{1,0:T(8,128)(2,1)}, u32[]{:S(2)}, u32[]{:S(2)}) collective-permute-start(bf16[512,1536]{1,0:T(8,128)(2,1)} %get-tuple-element.253), channel_id=1, source_target_pairs={{0,1},{1,0},{2,3},{3,2},{4,5},{5,4},{6,7},{7,6},{8,9},{9,8},{10,11... | collective-permute-start | bytes 4718600 | tf_op jit(solution)/shard_map/ppermute | solution.py:475
  466.0 213.4 %reduce-scatter.11.cloned.1.call-start = ((), (), s32[]{:S(2)}) async-start(), calls=%async_computation.9 | async-start | bytes 5013504 | tf_op jit(solution)/shard_map/reduce_scatter | solution.py:761
  466.1 31.4 %collective-permute-start.23 = (bf16[512,1536]{1,0:T(8,128)(2,1)}, bf16[512,1536]{1,0:T(8,128)(2,1)}, u32[]{:S(2)}, u32[]{:S(2)}) collective-permute-start(bf16[512,1536]{1,0:T(8,128)(2,1)} %copy-done.9), channel_id=1, source_target_pairs={{0,1},{1,0},{2,3},{3,2},{4,5},{5,4},{6,7},{7,6},{8,9},{9,8},{10,11... | collective-permute-start | bytes 4718600 | tf_op jit(solution)/shard_map/ppermute | solution.py:475
  504.7 38.8 %copy-start.54 = (bf16[1024,1536]{1,0:T(8,128)(2,1)S(1)}, bf16[1024,1536]{1,0:T(8,128)(2,1)}, u32[]{:S(2)}) copy-start(bf16[1024,1536]{1,0:T(8,128)(2,1)} %copy-done.53) | copy-start | bytes 9437188
  511.4 31.0 %collective-permute-start.24 = (bf16[512,1536]{1,0:T(8,128)(2,1)S(1)}, bf16[512,1536]{1,0:T(8,128)(2,1)S(1)}, u32[]{:S(2)}, u32[]{:S(2)}) collective-permute-start(bf16[512,1536]{1,0:T(8,128)(2,1)S(1)} %get-tuple-element.339), channel_id=1, source_target_pairs={{0,1},{1,0},{2,3},{3,2},{4,5},{5,4},{6,7},{7,6},{8,9},{9,8},{10,11... | collective-permute-start | bytes 4718600 | tf_op jit(solution)/shard_map/ppermute | solution.py:475
  550.3 249.7 %reduce-scatter.13.cloned.1.call-start = ((), (), s32[]{:S(2)}) async-start(), calls=%async_computation.10 | async-start | bytes 5013504
  551.1 3.6 collective-permute-start.25
  639.2 21.1 %collective-permute-start.26 = (bf16[8,96,1536]{2,1,0:T(8,128)(2,1)}, bf16[8,96,1536]{2,1,0:T(8,128)(2,1)}, u32[]{:S(2)}, u32[]{:S(2)}) collective-permute-start(bf16[8,96,1536]{2,1,0:T(8,128)(2,1)} %dynamic-slice_bitcast_fusion.1), channel_id=1, source_target_pairs={{0,2},{2,0},{4,6},{6,4},{8,10},{10,8},{12,14},{14,12},{16,18},{18,... | collective-permute-start | bytes 7077896 | tf_op jit(solution)/shard_map/ppermute | solution.py:522
  654.6 19.4 %collective-permute-start.27 = (bf16[8,96,1536]{2,1,0:T(8,128)(2,1)}, bf16[8,96,1536]{2,1,0:T(8,128)(2,1)}, u32[]{:S(2)}, u32[]{:S(2)}) collective-permute-start(bf16[8,96,1536]{2,1,0:T(8,128)(2,1)} %dynamic-slice_bitcast_fusion), channel_id=1, source_target_pairs={{0,2},{2,0},{4,6},{6,4},{8,10},{10,8},{12,14},{14,12},{16,18},{18,... | collective-permute-start | bytes 7077896 | tf_op jit(solution)/shard_map/ppermute | solution.py:522
  664.7 43.9 %collective-permute-start.29 = (bf16[4,96,1536]{2,1,0:T(8,128)(2,1)}, bf16[4,96,1536]{2,1,0:T(8,128)(2,1)}, u32[]{:S(2)}, u32[]{:S(2)}) collective-permute-start(bf16[4,96,1536]{2,1,0:T(8,128)(2,1)} %dynamic-slice_bitcast_fusion.3), channel_id=1, source_target_pairs={{0,4},{2,6},{4,0},{6,2},{8,12},{10,14},{12,8},{14,10},{16,20},{18,... | collective-permute-start | bytes 3538952 | tf_op jit(solution)/shard_map/ppermute | solution.py:522
  678.9 46.9 %collective-permute-start.30 = (bf16[4,96,1536]{2,1,0:T(8,128)(2,1)}, bf16[4,96,1536]{2,1,0:T(8,128)(2,1)}, u32[]{:S(2)}, u32[]{:S(2)}) collective-permute-start(bf16[4,96,1536]{2,1,0:T(8,128)(2,1)} %dynamic-slice_bitcast_fusion.2), channel_id=1, source_target_pairs={{0,4},{2,6},{4,0},{6,2},{8,12},{10,14},{12,8},{14,10},{16,20},{18,... | collective-permute-start | bytes 3538952 | tf_op jit(solution)/shard_map/ppermute | solution.py:522
  681.6 46.8 %collective-permute-start.28 = (bf16[512,1536]{1,0:T(8,128)(2,1)}, bf16[512,1536]{1,0:T(8,128)(2,1)}, u32[]{:S(2)}, u32[]{:S(2)}) collective-permute-start(bf16[512,1536]{1,0:T(8,128)(2,1)} %copy-done.7), channel_id=1, source_target_pairs={{0,1},{1,0},{2,3},{3,2},{4,5},{5,4},{6,7},{7,6},{8,9},{9,8},{10,11... | collective-permute-start | bytes 4718600 | tf_op jit(solution)/shard_map/ppermute | solution.py:475
  712.2 25.0 %collective-permute-start.35 = (bf16[1,96,1536]{2,1,0:T(8,128)(2,1)}, bf16[1,96,1536]{2,1,0:T(8,128)(2,1)}, u32[]{:S(2)}, u32[]{:S(2)}) collective-permute-start(bf16[1,96,1536]{2,1,0:T(8,128)(2,1)} %constant_dynamic-slice_fusion.1), channel_id=1, source_target_pairs={{0,8},{2,10},{4,12},{6,14},{8,16},{10,18},{12,20},{14,22},{16,24},... | collective-permute-start | bytes 884744 | tf_op jit(solution)/shard_map/ppermute | solution.py:522
  731.8 5.2 collective-permute-start.31
  737.1 3.1 collective-permute-start.32
  738.4 16.9 %collective-permute-start.36 = (bf16[1,96,1536]{2,1,0:T(8,128)(2,1)S(1)}, bf16[1,96,1536]{2,1,0:T(8,128)(2,1)S(1)}, u32[]{:S(2)}, u32[]{:S(2)}) collective-permute-start(bf16[1,96,1536]{2,1,0:T(8,128)(2,1)S(1)} %add_convert_fusion.5), channel_id=1, source_target_pairs={{0,8},{2,10},{4,12},{6,14},{8,16},{10,18},{12,20},{14,22},{16,24},... | collective-permute-start | bytes 884744 | tf_op jit(solution)/shard_map/ppermute | solution.py:522
  740.3 28.3 %collective-permute-start.33 = (f32[2,8,1920]{2,1,0:T(8,128)S(1)}, f32[2,8,1920]{2,1,0:T(8,128)S(1)}, u32[]{:S(2)}, u32[]{:S(2)}) collective-permute-start(f32[2,8,1920]{2,1,0:T(8,128)S(1)} %fusion.76), channel_id=1, source_target_pairs={{0,16},{2,18},{4,20},{6,22},{8,24},{10,26},{12,28},{14,30},{16,0},... | collective-permute-start | bytes 368648 | tf_op jit(solution)/shard_map/ppermute | solution.py:532
  756.3 18.1 %collective-permute-start.37 = (bf16[1,96,1536]{2,1,0:T(8,128)(2,1)S(1)}, bf16[1,96,1536]{2,1,0:T(8,128)(2,1)S(1)}, u32[]{:S(2)}, u32[]{:S(2)}) collective-permute-start(bf16[1,96,1536]{2,1,0:T(8,128)(2,1)S(1)} %add_convert_fusion.4), channel_id=1, source_target_pairs={{0,8},{2,10},{4,12},{6,14},{8,16},{10,18},{12,20},{14,22},{16,24},... | collective-permute-start | bytes 884744 | tf_op jit(solution)/shard_map/ppermute | solution.py:522
  766.2 33.8 %copy-start.49 = (bf16[4,96,1536]{2,1,0:T(8,128)(2,1)S(1)}, bf16[4,96,1536]{2,1,0:T(8,128)(2,1)}, u32[]{:S(2)}) copy-start(bf16[4,96,1536]{2,1,0:T(8,128)(2,1)} %fusion.13) | copy-start | bytes 3538948
  768.6 5.4 collective-permute-start.34
  774.1 16.5 %collective-permute-start.39 = (bf16[1,96,1536]{2,1,0:T(8,128)(2,1)S(1)}, bf16[1,96,1536]{2,1,0:T(8,128)(2,1)S(1)}, u32[]{:S(2)}, u32[]{:S(2)}) collective-permute-start(bf16[1,96,1536]{2,1,0:T(8,128)(2,1)S(1)} %constant_dynamic-slice_fusion), channel_id=1, source_target_pairs={{0,8},{2,10},{4,12},{6,14},{8,16},{10,18},{12,20},{14,22},{16,24},... | collective-permute-start | bytes 884744 | tf_op jit(solution)/shard_map/ppermute | solution.py:522
  775.5 36.5 %copy-start.58 = (bf16[1,96,2,1536]{3,1,2,0:T(8,128)(2,1)S(1)}, bf16[1,96,2,1536]{3,1,2,0:T(8,128)(2,1)}, u32[]{:S(2)}) copy-start(bf16[1,96,2,1536]{3,1,2,0:T(8,128)(2,1)} %copy.63) | copy-start | bytes 1769476
  775.5 15.4 %collective-permute-start.38 = (f32[2,8,1920]{2,1,0:T(8,128)S(1)}, f32[2,8,1920]{2,1,0:T(8,128)S(1)}, u32[]{:S(2)}, u32[]{:S(2)}) collective-permute-start(f32[2,8,1920]{2,1,0:T(8,128)S(1)} %add.649), channel_id=1, source_target_pairs={{0,4},{2,6},{4,0},{6,2},{8,12},{10,14},{12,8},{14,10},{16,20},{18,... | collective-permute-start | bytes 368648 | tf_op jit(solution)/shard_map/ppermute | solution.py:532
  790.7 9.3 %collective-permute-start.40 = (bf16[1,96,1536]{2,1,0:T(8,128)(2,1)S(1)}, bf16[1,96,1536]{2,1,0:T(8,128)(2,1)S(1)}, u32[]{:S(2)}, u32[]{:S(2)}) collective-permute-start(bf16[1,96,1536]{2,1,0:T(8,128)(2,1)S(1)} %add_convert_fusion.2), channel_id=1, source_target_pairs={{0,8},{2,10},{4,12},{6,14},{8,16},{10,18},{12,20},{14,22},{16,24},... | collective-permute-start | bytes 884744 | tf_op jit(solution)/shard_map/ppermute | solution.py:522
  801.3 5.0 collective-permute-start.42
  803.1 5.0 collective-permute-start.43
  803.4 8.5 %collective-permute-start.41 = (bf16[1,96,1536]{2,1,0:T(8,128)(2,1)S(1)}, bf16[1,96,1536]{2,1,0:T(8,128)(2,1)S(1)}, u32[]{:S(2)}, u32[]{:S(2)}) collective-permute-start(bf16[1,96,1536]{2,1,0:T(8,128)(2,1)S(1)} %add_convert_fusion.1), channel_id=1, source_target_pairs={{0,8},{2,10},{4,12},{6,14},{8,16},{10,18},{12,20},{14,22},{16,24},... | collective-permute-start | bytes 884744 | tf_op jit(solution)/shard_map/ppermute | solution.py:522
  (101 other events, 947.9 us)
Sparse Core Ops, SparseCore 0:
  69.5 56.8 all-gather.3
  128.7 89.6 all-gather.5
  220.6 51.5 all-gather.7
  360.6 80.2 reduce-scatter.6
  466.2 117.2 reduce-scatter.8
  587.1 75.3 reduce-scatter.10
  698.9 96.3 reduce-scatter.12

commit v5 on v4

--- a/solution.py
+++ b/solution.py
@@ -103,16 +103,18 @@
     step_l = split_lanes(step)
     grow_l = split_lanes(jnp.where(live, jnp.exp2(cum2), 0.0))
     left_l = split_lanes(jnp.where(live, jnp.exp2(last - cum2), 0.0))
-    all_l = split_lanes(jnp.where(live[0:8], jnp.exp2(jnp.broadcast_to(last, (8, LANES))), 0.0))
+    all_l = split_lanes(jnp.where(live[0:16], jnp.exp2(jnp.broadcast_to(last, (16, LANES))), 0.0))
+    stacked = jnp.concatenate([step_l, grow_l, left_l, all_l], axis=0)
     half = iota2((Q, LANES), 1) < HEADDIM
     ssq = jnp.zeros((Q, LANES), f32)
     for g in range(width // GROUP):
         columns = slice(g * GROUP, (g + 1) * GROUP)
         spread = spread_ref[:, columns]
-        step_e = mm(step_l, spread)
-        grow_e = mm(grow_l, spread)
-        left_e = mm(left_l, spread)
-        all_e = mm(all_l, spread)[0:1, :]
+        spreads = mm(stacked, spread)
+        step_e = spreads[0:Q]
+        grow_e = spreads[Q : 2 * Q]
+        left_e = spreads[2 * Q : 3 * Q]
+        all_e = spreads[3 * Q : 3 * Q + 1]
         ext_ref[8 : 8 + Q, columns] = zx_ref[:, width + g * GROUP : width + (g + 1) * GROUP].astype(f32)
         z = taps_sum(ext_ref, taps_ref, chan_ref, columns)
         xc = z * sigmoid(z)
@@ -121,7 +123,7 @@
         vl = (v - vb.astype(f32)).astype(bf16)
         state = state_ref[:, columns]
         state_b = state.astype(bf16)
-        sin_ref[0, :, columns] = state_b
+        sin_ref[0, :, columns] = state
         state_l = (state - state_b.astype(f32)).astype(bf16)
         y = mm(c_both, jnp.concatenate([state_b, state_b], axis=0)) + mm(cb, state_l)
         y = y * grow_e
@@ -148,7 +150,7 @@
         y = y + jnp.concatenate(parts, axis=1)
         state_ref[:, columns] = state * all_e + mm(bt, (v * left_e).astype(bf16))
         mixed = y + chan_ref[2:3, columns] * xc
-        mixed_ref[:, columns] = mixed.astype(bf16)
+        mixed_ref[:, columns] = mixed
         gate = zx_ref[:, columns].astype(f32)
         gated = mixed * (gate * sigmoid(gate))
         squares = gated * gated
@@ -195,13 +197,16 @@
     cb = c_part.astype(bf16)
     bt = b_part.T.astype(bf16)
     ct = c_part.T.astype(bf16)
+    c_both = jnp.concatenate([cb, (c_part - cb.astype(f32)).astype(bf16)], axis=1)
+    b_both = jnp.concatenate([bb, (b_part - bb.astype(f32)).astype(bf16)], axis=1)
     upper = iota2((Q, Q), 0) <= iota2((Q, Q), 1)
     scores = jnp.where(lower, mm(c_part, b_part.T, highest), 0.0)
     scores_t = scores.T
     step_l = split_lanes(step)
     grow_l = split_lanes(jnp.where(live, jnp.exp2(cum2), 0.0))
     left_l = split_lanes(jnp.where(live, jnp.exp2(last - cum2), 0.0))
-    all_l = split_lanes(jnp.where(live[0:8], jnp.exp2(jnp.broadcast_to(last, (8, LANES))), 0.0))
+    all_l = split_lanes(jnp.where(live[0:16], jnp.exp2(jnp.broadcast_to(last, (16, LANES))), 0.0))
+    stacked = jnp.concatenate([step_l, grow_l, left_l, all_l], axis=0)
     half = iota2((Q, LANES), 1) < HEADDIM
     coef = coef_ref[:, 0:1]
     inv = coef_ref[:, 1:2]
@@ -209,9 +214,7 @@
     d_c = jnp.zeros((Q, LANES), f32)
     d_b = jnp.zeros((Q, LANES), f32)
     row_sums = jnp.zeros((Q, LANES), f32)
-    red_step = jnp.zeros((Q, LANES), f32)
-    red_in = jnp.zeros((Q, LANES), f32)
-    red_out = jnp.zeros((Q, LANES), f32)
+    reduced = jnp.zeros((3 * Q, LANES), f32)
     red_all = jnp.zeros((8, LANES), f32)
     ones = jnp.ones((16, Q), bf16)
     pair_rows = iota2((2 * Q, LANES), 0) // Q
@@ -220,10 +223,11 @@
         columns = slice(g * GROUP, (g + 1) * GROUP)
         spread = spread_ref[:, columns]
         gather = gather_ref[columns, :]
-        step_e = mm(step_l, spread)
-        grow_e = mm(grow_l, spread)
-        left_e = mm(left_l, spread)
-        all_e = mm(all_l, spread)[0:1, :]
+        spreads = mm(stacked, spread)
+        step_e = spreads[0:Q]
+        grow_e = spreads[Q : 2 * Q]
+        left_e = spreads[2 * Q : 3 * Q]
+        all_e = spreads[3 * Q : 3 * Q + 1]
         ext_ref[8 : 8 + Q, columns] = zx_ref[:, width + g * GROUP : width + (g + 1) * GROUP].astype(f32)
         z = taps_sum(ext_ref, taps_ref, chan_ref, columns)
         s = sigmoid(z)
@@ -244,16 +248,17 @@
         dyb = dy.astype(bf16)
         v = xc * step_e
         vb = v.astype(bf16)
-        sin = sin_ref[0, :, columns]
+        sin_full = sin_ref[0, :, columns]
+        sin = sin_full.astype(bf16)
         ey = dy * grow_e
         eyb = ey.astype(bf16)
-        inter = ey * mm(cb, sin)
+        inter = ey * mm(c_both, jnp.concatenate([sin, sin], axis=0))
         dstate = dstate_ref[:, columns]
         dstate_b = dstate.astype(bf16)
-        dv_state = mm(bb, dstate_b) * left_e
+        dv_state = mm(b_both, jnp.concatenate([dstate_b, dstate_b], axis=0)) * left_e
         d_c = d_c + mm_t(eyb, sin)
         d_b = d_b + mm_t((v * left_e).astype(bf16), dstate_b)
-        kept = jnp.sum(sin.astype(f32) * dstate, axis=0, keepdims=True) * all_e
+        kept = jnp.sum(sin_full * dstate, axis=0, keepdims=True) * all_e
         dstate_ref[:, columns] = dstate * all_e + mm(ct, eyb)
         parts = []
         for pair in range(GROUP // LANES):
@@ -281,9 +286,10 @@
             colsum_ref[head : head + 1, :] = sums[0:1, 0:Q]
             colsum_ref[head + 1 : head + 2, :] = sums[0:1, Q : 2 * Q]
         dv = jnp.concatenate(parts, axis=1) + dv_state
-        red_step = red_step + mm((dv * xc).astype(bf16), gather)
-        red_in = red_in + mm(inter.astype(bf16), gather)
-        red_out = red_out + mm((v * dv_state).astype(bf16), gather)
+        terms = jnp.concatenate([dv * xc, inter, v * dv_state], axis=0)
+        terms_b = terms.astype(bf16)
+        terms_l = (terms - terms_b.astype(f32)).astype(bf16)
+        reduced = reduced + mm(terms_b, gather) + mm(terms_l, gather)
         red_all = red_all + mm(jnp.broadcast_to(kept, (8, GROUP)), gather.astype(f32), highest)
         dz = (dv * step_e + chan_ref[2:3, columns] * dy) * x_dsilu
         dz_ref[0:Q, columns] = dz
@@ -295,6 +301,9 @@
             )
         gchan_ref[4:5, columns] += jnp.sum(dz, axis=0, keepdims=True)
         low_ref[:, width + g * GROUP : width + (g + 1) * GROUP] = dx.astype(bf16)
+    red_step = reduced[0:Q]
+    red_in = reduced[Q : 2 * Q]
+    red_out = reduced[2 * Q : 3 * Q]
     through = row_sums - colsum_ref[...].T + red_in
     d_decay = mm(upper.astype(f32), through, highest) + mm(
         jnp.where(upper, 0.0, 1.0), red_out, highest
@@ -407,8 +416,8 @@
         ],
         out_shape=[
             jax.ShapeDtypeStruct((rows, width), f32),
-            jax.ShapeDtypeStruct((rows, width), bf16),
-            jax.ShapeDtypeStruct((chunks, LANES, width), bf16),
+            jax.ShapeDtypeStruct((rows, width), f32),
+            jax.ShapeDtypeStruct((chunks, LANES, width), f32),
             jax.ShapeDtypeStruct((rows, LANES), f32),
         ],
         scratch_shapes=[
@@ -496,7 +505,7 @@
     return v.reshape((size, v.shape[0] // size) + v.shape[1:])
 
 
-def fold(blocks, level, start=None, finish=None, marks=()):
+def fold(blocks, level, gate=None):
     factors = dp_factors()
     factor = factors[level]
     stride = 1
@@ -514,16 +523,14 @@
         return lax.dynamic_index_in_dim(parts, (place + step) % factor, 1, keepdims=False)
 
     moving = pick(factor - 1)
-    if start is not None:
-        moving = after(moving, start)
+    seen = []
     for step in range(factor - 1):
-        if step < len(marks):
-            moving = after(moving, marks[step])
+        if gate is not None and step == factor - 2:
+            moving = after(moving, gate(seen))
         arrived = lax.ppermute(moving, "dp", hops)
-        if finish is not None:
-            arrived = after(arrived, finish)
+        seen.append(arrived)
         moving = (arrived.astype(f32) + pick(2 * factor - 2 - step).astype(f32)).astype(blocks.dtype)
-    return moving, arrived
+    return moving
 
 
 def sum_devices(v, spans):
@@ -531,58 +538,6 @@
     for span in spans:
         v = v + lax.ppermute(v, "dp", [(i, i ^ span) for i in range(size)])
     return v
-
-
-def ring_gather(shard):
-    size = lax.axis_size("dp")
-    chips = size // 2
-    order = {8: (0, 2, 4, 6, 7, 5, 3, 1)}.get(chips, tuple(range(chips)))
-    index = lax.axis_index("dp")
-    core = index % 2
-    place = jnp.asarray([order.index(c) for c in range(chips)], jnp.int32)[index // 2]
-    chip_at = jnp.asarray(order, jnp.int32)
-    onward, back = [], []
-    for k in range(chips):
-        here, there = order[k], order[(k + 1) % chips]
-        for c in range(2):
-            onward.append((here * 2 + c, there * 2 + c))
-            back.append((there * 2 + c, here * 2 + c))
-    cores = [(i, i ^ 1) for i in range(size)]
-    whole_array = jnp.zeros((size,) + shard.shape, shard.dtype)
-    half = chips // 2
-    cut = (shard.shape[1] // 256) * LANES
-
-    def swap(piece):
-        return lax.ppermute(piece, "dp", cores)
-
-    def put(target, piece, other, position):
-        chip = chip_at[position % chips]
-        target = lax.dynamic_update_slice(target, piece[None], (chip * 2 + core, 0, 0))
-        return lax.dynamic_update_slice(target, other[None], (chip * 2 + 1 - core, 0, 0))
-
-    ahead = behind = shard
-    others = [swap(shard)]
-    places = [(shard, place)]
-    for step in range(1, half):
-        ahead = lax.ppermute(ahead, "dp", onward)
-        behind = lax.ppermute(behind, "dp", back)
-        ahead, behind, others = lax.optimization_barrier((ahead, behind, others))
-        places += [(ahead, place - step + chips), (behind, place + step)]
-        others = others + [swap(ahead), swap(behind)]
-    reached = behind
-    piece = jnp.concatenate(
-        [
-            lax.ppermute(ahead[:, :cut], "dp", onward),
-            lax.ppermute(behind[:, cut:], "dp", back),
-        ],
-        axis=1,
-    )
-    piece, others = lax.optimization_barrier((piece, others))
-    places.append((piece, place + half))
-    others = others + [swap(piece)]
-    for (got, position), other in zip(places, others):
-        whole_array = put(whole_array, got, other, position)
-    return whole_array.reshape((-1,) + shard.shape[1:]), reached
 
 
 def head_lanes(v):
@@ -635,13 +590,7 @@
             axis=1,
         )
         out_shard = w_out[l].T
-        if l == 0:
-            gathered, reached = ring_gather(shard)
-            in_weights.append(gathered)
-            out_shard = after(out_shard, reached)
-        else:
-            shard = after(shard, reached)
-            in_weights.append(lax.all_gather(shard, "dp", axis=0, tiled=True))
+        in_weights.append(lax.all_gather(shard, "dp", axis=0, tiled=True))
         out_weights.append(lax.all_gather(out_shard, "dp", axis=0, tiled=True))
     params = []
     for l in range(layers):
@@ -703,7 +652,7 @@
             row_dot = last_dot
         else:
             own_grad = grad_rows.astype(bf16)
-            out_grad = gather_pair(own_grad)
+            out_grad, side_last = lax.optimization_barrier((gather_pair(own_grad), side_last))
             own_dot = jnp.sum(own_grad.astype(f32) * lifted, axis=1).reshape(8, -1)
             row_dot = both_rows(own_dot.reshape(-1, 1), pair_swap(own_dot).reshape(-1, 1), first)
         coef = jnp.pad(
@@ -732,17 +681,17 @@
             out_parts[l] = done_out
             low_last, normed_last = low, normed
         else:
+            side = t_mm(normed, low[:, 2 * width :])
+            side = lax.dynamic_update_slice(side_last, side, (0, 0))
+            low = after(low, side)
             in_state = []
             for i in range(2):
                 part = t_product(normed, low, bf16, i * width, width)
-                in_state.append(fold(row_blocks(part), 0)[0])
+                in_state.append(fold(row_blocks(part), 0))
                 low = after(low, part)
-                if i == 0:
-                    side = t_mm(normed, low[:, 2 * width :])
-                    low = after(low, side)
             own = product_t(after(low, in_state), w_in, f32, tensor_index)
             for level in range(1, len(dp_factors()) - 1):
-                in_state = [fold(q, level)[0] for q in in_state]
+                in_state = [fold(q, level) for q in in_state]
             arrived = after(arrived, in_state)
         normed_grad = own + arrived.astype(f32)
         unit = current * rms
@@ -758,9 +707,9 @@
         if l > 0:
             low_last = after(low_last, grad_rows)
             side_last = t_mm(normed_last, low_last[:, 2 * width :])
+            side_last = jnp.pad(side_last, ((0, 0), (side_last.shape[1], 0)))
     done_out = lax.psum_scatter(grad_out, "dp", scatter_dimension=0, tiled=True)
     side_width = 384
-    side = jnp.concatenate([side, side_last], axis=1)
     side_own = lax.psum_scatter(side, "dp", scatter_dimension=0, tiled=True)
     small = jnp.stack(packed)
     row = lax.broadcasted_iota(jnp.int32, small.shape, 1)
@@ -770,13 +719,18 @@
     spans = [1]
     while spans[-1] * 2 < lax.axis_size("dp"):
         spans.append(spans[-1] * 2)
-    small = sum_devices(small, spans[:1] + spans[:1:-1])
     queue = in_state
     level = len(dp_factors()) - 1
-    for n in range(len(queue)):
-        marks = (small, small, side_own) if n == len(queue) - 1 else ()
-        queue[n], _ = fold(queue[n], level, marks=marks)
-    small = sum_devices(after(small, queue[0]), spans[1:2])
+    partial_sums = []
+
+    def gate(seen):
+        early = after(small, seen[0]) if seen else small
+        partial_sums.append(sum_devices(early, spans[:1] + spans[:1:-1]))
+        return partial_sums[0], side_own
+
+    queue[0] = fold(queue[0], level)
+    queue[1] = fold(queue[1], level, gate)
+    small = sum_devices(after(partial_sums[0], queue[0]), spans[1:2])
     done = [q.reshape(q.shape[1:]) for q in queue]
     out_parts[0] = done_out
     in_parts = [jnp.concatenate(done, axis=1), done_in]

time: 830 us -> 794 us (0.957)
  waiting for transfers between devices: 236 us -> 275 us
  local copies, waits for them, and re-layouts: 107 us -> 68.9 us
  starting transfers between devices: 53.3 us -> 30.4 us
  between operations: 27.9 us -> 15.6 us
  Pallas kernels: 229 us -> 239 us
    ppermute x16 -> x0, waiting for transfers between devices: 61.8 us -> none  [the longest x3 30.5 us: ring_gather(): ahead = lax.ppermute(ahead, 'dp', onward)]
    ppermute x14, waiting for transfers between devices: 123 us -> 183 us  [pair_swap(): return lax.ppermute(v, 'tensor', ((0, 1), (1, 0)))]
    ppermute x4, waiting for transfers between devices: 7.07 us -> 33.7 us  [sum_devices(): v = v + lax.ppermute(v, 'dp', [(i, i ^ span) for i in range(size)])]
    dynamic_update_slice x15 -> x0, local copies, waits for them, and re-layouts: 22.7 us -> none  [the longest x8 11.9 us: put(): lax.dynamic_update_slice(target, other[None], (chip * 2 + 1 - core, 0, 0))]
    unnamed x240 -> x181, local copies, waits for them, and re-layouts: 38 us -> 23.4 us
    all_gather x1 -> x2, waiting for transfers between devices: 0.02 us -> 11.6 us  [local(): in_weights.append(lax.all_gather(shard, 'dp', axis=0, tiled=True))]
    ppermute x10, starting transfers between devices: 19.4 us -> 8.6 us  [fold(): arrived = lax.ppermute(moving, 'dp', hops)]
    ppermute x16 -> x0, starting transfers between devices: 10.3 us -> none  [the longest x3 5.2 us: ring_gather(): behind = lax.ppermute(behind, 'dp', back)]
  transfers between devices with their start and end apart: 51 -> 36, of which waited for: 26 -> 20; matrix products, arithmetic and copies ran while one was open for 30% -> 26% of each run, Pallas kernels for 28% -> 30%
where the time goes in v5:
time: 794 us; the launch traced here: 790 us
  waiting for transfers between devices  275 us (35%)
  Pallas kernels  239 us (30%)
  matrix products  96 us (12%)
  local copies, waits for them, and re-layouts  68.9 us (9%)
  other arithmetic  65.5 us (8%)
  starting transfers between devices  30.4 us (4%)
  between operations  15.6 us (2%)
    ppermute x14, waiting for transfers between devices, pair_swap(): return lax.ppermute(v, 'tensor', ((0, 1), (1, 0)))  183 us
    pallas_call x2, Pallas kernels, mixer_backward(): pl.pallas_call(functools.partial(bwd_kernel, head_count=width // HEADDIM)...  112 us
    pallas_call x2, Pallas kernels, mixer_forward(): pl.pallas_call(functools.partial(fwd_kernel, head_count=width // HEADDIM)...  57.1 us
    dot_general x4, matrix products, mm(): lax.dot_general(a, b, (((1,), (0,)), ((), ())), precision=precision, pref...  50.6 us
    ppermute x10, waiting for transfers between devices, fold(): arrived = lax.ppermute(moving, 'dp', hops)  45 us
    pallas_call x4, Pallas kernels, product_t(): pl.pallas_call(body, grid_spec=pltpu.PrefetchScalarGridSpec(num_scalar_pr...  40 us
    ppermute x4, waiting for transfers between devices, sum_devices(): v = v + lax.ppermute(v, 'dp', [(i, i ^ span) for i in range(size)])  33.7 us
    pallas_call x3, Pallas kernels, t_product(): pl.pallas_call(body, grid=(count // columns,), in_specs=[pl.BlockSpec((de...  30 us
  transfers between devices with their start and end apart: 36, of which 20 were waited for; matrix products, arithmetic and copies ran while one was open for 26% of the time, Pallas kernels for 30%

profile of v5, /device:TPU:0, one launch (start us, length us, event | category | flops | bytes accessed | tf_op | source)
XLA Modules:
  0.0 789.9 jit_solution(4250537512945814578)
XLA Ops:
  8.9 2.1 fusion.44
  16.4 1.9 pad_maximum_fusion.1
  18.4 2.9 collective-permute-start
  26.2 63.4 %collective-permute-done = bf16[1024,1536]{1,0:T(8,128)(2,1)S(1)} collective-permute-done((bf16[1024,1536]{1,0:T(8,128)(2,1)}, bf16[1024,1536]{1,0:T(8,128)(2,1)S(1)}, u32[]{:S(2)}, u32[]{:S(2)}) %collective-permute-start) | collective-permute-done | bytes 3145760 | tf_op jit(solution)/shard_map/ppermute | solution.py:484
  92.0 11.6 %all-gather.5.cloned.1.call-done.b_ref = bf16[1536,3456]{1,0:T(8,128)(2,1)} async-done(((bf16[96,3456]{1,0:T(8,128)(2,1)}), bf16[1536,3456]{1,0:T(8,128)(2,1)}) %all-gather.5.cloned.1.call-update) | async-done | bytes 10616848 | tf_op jit(solution)/shard_map/all_gather | solution.py:593
  103.6 17.1 %fusion.52.zx_ref.bcdt_ref.xprev_ref.bcprev_ref = f32[1024,3456]{1,0:T(8,128)} fusion(bf16[1024,1536]{1,0:T(8,128)(2,1)S(1)} %fusion.5.a_ref, bf16[1536,3456]{1,0:T(8,128)(2,1)} %all-gather.5.cloned.1.call-done.b_ref), kind=kOutput, calls=%fused_computation.160 | convolution fusion | flops 10871635968 | bytes 27918336 | tf_op jit(solution)/shard_map/dot_general | solution.py:26
  120.6 28.6 %shard_map.262 = (f32[1024,1536]{1,0:T(8,128)}, f32[1024,1536]{1,0:T(8,128)}, f32[8,128,1536]{2,1,0:T(8,128)}, f32[1024,128]{1,0:T(8,128)S(1)}) custom-call(f32[1024,3456]{1,0:T(8,128)} %fusion.52.zx_ref.bcdt_ref.xprev_ref.bcprev_ref, f32[1024,3456]{1,0:T(8,128)} %fusion.52.zx_ref.bcdt_ref.xprev_ref.bcprev_ref, f32[4,1536]{1,0:T(4,128)S(1)} %copy-done.15, ...), custom_call_target="tpu_custom_call" | custom-call | flops 1000 | bytes 1000 | tf_op jit(solution)/shard_map/pallas_call | solution.py:402
  151.0 2.1 collective-permute-done.1
  153.7 3.3 multiply_convert_fusion.1
  158.0 6.1 convolution_convert_fusion.2
  165.6 35.3 %collective-permute-done.2 = bf16[512,1536]{1,0:T(8,128)(2,1)} collective-permute-done((bf16[512,1536]{1,0:T(8,128)(2,1)}, bf16[512,1536]{1,0:T(8,128)(2,1)}, u32[]{:S(2)}, u32[]{:S(2)}) %collective-permute-start.2) | collective-permute-done | bytes 1572896 | tf_op jit(solution)/shard_map/ppermute | solution.py:484
  200.9 8.2 %multiply_reduce_fusion.8 = (f32[512]{0:T(512)S(1)}, f32[512,1536]{1,0:T(8,128)S(1)}, f32[512,1536]{1,0:T(8,128)}) fusion(bf16[512,1536]{1,0:T(8,128)(2,1)} %collective-permute-done.2, bf16[512,1536]{1,0:T(8,128)(2,1)} %param.39, bf16[1536,1536]{1,0:T(8,128)(2,1)} %all-gather.7.cloned.1.call-done, bf16[1024,1536]{1,0:T(8,128)(2,1)} %copy-done.48, ...), kind=kOutput, calls=%fused_computation.41 | convolution fusion | flops 2420637184 | bytes 15730692 | tf_op jit(solution)/shard_map/dot_general | solution.py:32
  218.1 28.6 %collective-permute-done.3 = bf16[512,1536]{1,0:T(8,128)(2,1)} collective-permute-done((bf16[512,1536]{1,0:T(8,128)(2,1)}, bf16[512,1536]{1,0:T(8,128)(2,1)}, u32[]{:S(2)}, u32[]{:S(2)}) %collective-permute-start.3) | collective-permute-done | bytes 1572896 | tf_op jit(solution)/shard_map/ppermute | solution.py:484
  246.7 3.2 maximum_select_fusion.a_ref
  250.0 17.1 %fusion.53.zx_ref.bcdt_ref.xprev_ref.bcprev_ref = f32[1024,3456]{1,0:T(8,128)} fusion(bf16[1024,1536]{1,0:T(8,128)(2,1)S(1)} %maximum_select_fusion.a_ref, bf16[1536,3456]{1,0:T(8,128)(2,1)} %all-gather.9.cloned.1.call-done.b_ref), kind=kOutput, calls=%fused_computation.161 | convolution fusion | flops 10871635968 | bytes 27918336 | tf_op jit(solution)/shard_map/dot_general | solution.py:26
  267.0 28.5 %shard_map.263 = (f32[1024,1536]{1,0:T(8,128)}, f32[1024,1536]{1,0:T(8,128)}, f32[8,128,1536]{2,1,0:T(8,128)}, f32[1024,128]{1,0:T(8,128)S(1)}) custom-call(f32[1024,3456]{1,0:T(8,128)} %fusion.53.zx_ref.bcdt_ref.xprev_ref.bcprev_ref, f32[1024,3456]{1,0:T(8,128)} %fusion.53.zx_ref.bcdt_ref.xprev_ref.bcprev_ref, f32[4,1536]{1,0:T(4,128)S(1)} %copy-done.17, ...), custom_call_target="tpu_custom_call" | custom-call | flops 1000 | bytes 1000 | tf_op jit(solution)/shard_map/pallas_call | solution.py:402
  296.4 1.8 reduce_sum.129
  299.7 3.4 fusion.6
  303.1 1.9 fusion.74
  307.4 7.1 convolution_convert_fusion.1
  315.1 5.1 fusion.15
  321.6 4.5 multiply_reduce_fusion.7
  327.6 2.2 collective-permute-done.5
  330.3 7.0 fusion.54.sg_ref
  344.0 55.8 %shard_map.264 = (bf16[1024,3456]{1,0:T(8,128)(2,1)}, f32[8,1536]{1,0:T(8,128)S(1)}, f32[8,256]{1,0:T(8,128)S(1)}, f32[8,128]{1,0:T(8,128)S(1)}) custom-call(f32[1024,1536]{1,0:T(8,128)} %fusion.54.sg_ref, f32[1024,3456]{1,0:T(8,128)} %fusion.53.zx_ref.bcdt_ref.xprev_ref.bcprev_ref, f32[1024,3456]{1,0:T(8,128)} %fusion.53.zx_ref.bcdt_ref.xprev_ref.bcprev_ref, ...), custom_call_target="tpu_custom_call" | custom-call | flops 1000 | bytes 1000 | tf_op jit(solution)/shard_map/pallas_call | solution.py:442
  401.6 9.4 %shard_map.265 = bf16[512,1536]{1,0:T(8,128)(2,1)S(1)} custom-call(s32[1]{0:T(128)} %bitcast.31.half_ref, bf16[1024,3456]{1,0:T(8,128)(2,1)} %get-tuple-element.211.a_ref.b_ref, bf16[1536,3456]{1,0:T(8,128)(2,1)} %all-gather.9.cloned.1.call-done.b_ref), custom_call_target="tpu_custom_call" | custom-call | flops 1000 | bytes 1000 | tf_op jit(solution)/shard_map/pallas_call | solution.py:358
  412.2 13.7 %shard_map.266 = bf16[1536,3072]{1,0:T(8,128)(2,1)} custom-call(bf16[1024,1536]{1,0:T(8,128)(2,1)S(1)} %maximum_select_fusion.a_ref, bf16[1024,3456]{1,0:T(8,128)(2,1)} %get-tuple-element.211.a_ref.b_ref), custom_call_target="tpu_custom_call" | custom-call | flops 1000 | bytes 1000 | tf_op jit(solution)/shard_map/pallas_call | solution.py:382
  427.7 9.9 %shard_map.267 = f32[512,1536]{1,0:T(8,128)S(1)} custom-call(s32[1]{0:T(128)} %bitcast.32.half_ref, bf16[1024,3456]{1,0:T(8,128)(2,1)} %get-tuple-element.211.a_ref.b_ref, bf16[1536,3456]{1,0:T(8,128)(2,1)} %all-gather.9.cloned.1.call-done.b_ref), custom_call_target="tpu_custom_call" | custom-call | flops 1000 | bytes 1000 | tf_op jit(solution)/shard_map/pallas_call | solution.py:358
  439.3 19.9 %collective-permute-done.7 = bf16[512,1536]{1,0:T(8,128)(2,1)} collective-permute-done((bf16[512,1536]{1,0:T(8,128)(2,1)}, bf16[512,1536]{1,0:T(8,128)(2,1)}, u32[]{:S(2)}, u32[]{:S(2)}) %collective-permute-start.7) | collective-permute-done | bytes 1572896 | tf_op jit(solution)/shard_map/ppermute | solution.py:484
  459.2 5.9 multiply_reduce_fusion
  466.2 6.6 multiply_reduce_fusion.4
  474.4 3.0 fusion.25
  477.4 2.4 pad.66
  479.8 25.7 %collective-permute-done.8 = bf16[512,1536]{1,0:T(8,128)(2,1)S(1)} collective-permute-done((bf16[512,1536]{1,0:T(8,128)(2,1)S(1)}, bf16[512,1536]{1,0:T(8,128)(2,1)S(1)}, u32[]{:S(2)}, u32[]{:S(2)}) %collective-permute-start.8) | collective-permute-done | bytes 1572896 | tf_op jit(solution)/shard_map/ppermute | solution.py:484
  506.5 6.8 convolution_convert_fusion
  524.2 9.5 %fusion.55.sg_ref = f32[1024,1536]{1,0:T(8,128)} fusion(bf16[1024,1536]{1,0:T(8,128)(2,1)S(1)} %maximum_select_fusion.1, bf16[1536,1536]{1,0:T(8,128)(2,1)} %all-gather.7.cloned.1.call-done), kind=kOutput, calls=%fused_computation.163 | convolution fusion | flops 4831838208 | bytes 14155776 | tf_op jit(solution)/shard_map/dot_general | solution.py:26
  533.7 55.8 %shard_map.268 = (bf16[1024,3456]{1,0:T(8,128)(2,1)}, f32[8,1536]{1,0:T(8,128)S(1)}, f32[8,256]{1,0:T(8,128)S(1)}, f32[8,128]{1,0:T(8,128)S(1)}) custom-call(f32[1024,1536]{1,0:T(8,128)} %fusion.55.sg_ref, f32[1024,3456]{1,0:T(8,128)} %fusion.52.zx_ref.bcdt_ref.xprev_ref.bcprev_ref, f32[1024,3456]{1,0:T(8,128)} %fusion.52.zx_ref.bcdt_ref.xprev_ref.bcprev_ref, ...), custom_call_target="tpu_custom_call" | custom-call | flops 1000 | bytes 1000 | tf_op jit(solution)/shard_map/pallas_call | solution.py:442
  589.5 10.5 %shard_map.269 = bf16[512,1536]{1,0:T(8,128)(2,1)} custom-call(s32[1]{0:T(128)} %bitcast.31.half_ref, bf16[1024,3456]{1,0:T(8,128)(2,1)} %get-tuple-element.222.a_ref.b_ref, bf16[1536,3456]{1,0:T(8,128)(2,1)} %all-gather.5.cloned.1.call-done.b_ref), custom_call_target="tpu_custom_call" | custom-call | flops 1000 | bytes 1000 | tf_op jit(solution)/shard_map/pallas_call | solution.py:358
  600.0 4.5 convolution_dynamic-update-slice_fusion
  604.6 8.3 %shard_map.270 = bf16[1536,1536]{1,0:T(8,128)(2,1)} custom-call(bf16[1024,1536]{1,0:T(8,128)(2,1)S(1)} %copy-done.1, bf16[1024,3456]{1,0:T(8,128)(2,1)} %get-tuple-element.222.a_ref.b_ref), custom_call_target="tpu_custom_call" | custom-call | flops 1000 | bytes 1000 | tf_op jit(solution)/shard_map/pallas_call | solution.py:382
  612.9 3.2 dynamic-slice_bitcast_fusion.1
  616.1 8.0 %shard_map.271 = bf16[1536,1536]{1,0:T(8,128)(2,1)} custom-call(bf16[1024,1536]{1,0:T(8,128)(2,1)S(1)} %copy-done.1, bf16[1024,3456]{1,0:T(8,128)(2,1)} %get-tuple-element.222.a_ref.b_ref), custom_call_target="tpu_custom_call" | custom-call | flops 1000 | bytes 1000 | tf_op jit(solution)/shard_map/pallas_call | solution.py:382
  624.1 3.2 dynamic-slice_bitcast_fusion
  627.8 3.0 fusion.1
  632.4 3.0 fusion
  641.1 2.1 maximum_convert_fusion.1
  643.3 2.9 stack_reshape.5
  646.1 2.0 copy.61
  648.1 10.1 %shard_map.272 = f32[512,1536]{1,0:T(8,128)S(1)} custom-call(s32[1]{0:T(128)} %bitcast.32.half_ref, bf16[1024,3456]{1,0:T(8,128)(2,1)} %get-tuple-element.222.a_ref.b_ref, bf16[1536,3456]{1,0:T(8,128)(2,1)} %all-gather.5.cloned.1.call-done.b_ref), custom_call_target="tpu_custom_call" | custom-call | flops 1000 | bytes 1000 | tf_op jit(solution)/shard_map/pallas_call | solution.py:358
  658.3 3.0 collective-permute-done.13
  663.7 1.9 collective-permute-start.20
  665.6 32.7 %collective-permute-done.14 = bf16[4,96,1536]{2,1,0:T(8,128)(2,1)} collective-permute-done((bf16[4,96,1536]{2,1,0:T(8,128)(2,1)}, bf16[4,96,1536]{2,1,0:T(8,128)(2,1)}, u32[]{:S(2)}, u32[]{:S(2)}) %collective-permute-start.14) | collective-permute-done | bytes 1179680 | tf_op jit(solution)/shard_map/ppermute | solution.py:530
  698.2 2.6 fusion.13
  700.9 3.4 multiply_reduce_fusion.2
  707.1 1.8 collective-permute-start.16
  709.8 6.4 collective-permute-done.16
  719.4 5.9 fusion.11
  725.3 13.8 %collective-permute-done.18 = f32[2,8,1920]{2,1,0:T(8,128)S(1)} collective-permute-done((f32[2,8,1920]{2,1,0:T(8,128)S(1)}, f32[2,8,1920]{2,1,0:T(8,128)S(1)}, u32[]{:S(2)}, u32[]{:S(2)}) %collective-permute-start.18) | collective-permute-done | bytes 122912 | tf_op jit(solution)/shard_map/ppermute | solution.py:539
  739.3 2.0 collective-permute-start.22
  741.5 15.2 %collective-permute-done.19 = f32[2,8,1920]{2,1,0:T(8,128)S(1)} collective-permute-done((f32[2,8,1920]{2,1,0:T(8,128)S(1)}, f32[2,8,1920]{2,1,0:T(8,128)S(1)}, u32[]{:S(2)}, u32[]{:S(2)}) %collective-permute-start.19) | collective-permute-done | bytes 122912 | tf_op jit(solution)/shard_map/ppermute | solution.py:539
  757.0 4.8 collective-permute-done.23
  771.4 2.0 collective-permute-done.26
  776.4 2.9 collective-permute-done.25
  779.6 3.2 copy.64
  (342 shorter events, 94.2 us)
Async XLA Ops:
  7.2 96.4 %all-gather.5.cloned.1.call-start = ((), (), s32[]{:S(2)}) async-start(), calls=%async_computation.4 | async-start | bytes 11280384 | tf_op jit(solution)/shard_map/all_gather | solution.py:593
  12.0 146.0 %all-gather.7.cloned.1.call-start = ((), (), s32[]{:S(2)}) async-start(), calls=%async_computation.5 | async-start | bytes 5013504 | tf_op jit(solution)/shard_map/all_gather | solution.py:594
  13.0 236.9 %all-gather.9.cloned.1.call-start = ((), (), s32[]{:S(2)}) async-start(), calls=%async_computation.6 | async-start | bytes 11280384 | tf_op jit(solution)/shard_map/all_gather | solution.py:593
  14.1 300.9 %all-gather.11.cloned.1.call-start = ((), (), s32[]{:S(2)}) async-start(), calls=%async_computation.7 | async-start | bytes 5013504 | tf_op jit(solution)/shard_map/all_gather | solution.py:594
  16.3 9.1 %copy-start.78 = (f32[2,4,256]{2,1,0:T(4,128)S(1)}, f32[2,4,256]{2,1,0:T(4,128)}, u32[]{:S(2)}) copy-start(f32[2,4,256]{2,1,0:T(4,128)} %param.46) | copy-start | bytes 24580
  18.4 71.2 %collective-permute-start = (bf16[1024,1536]{1,0:T(8,128)(2,1)}, bf16[1024,1536]{1,0:T(8,128)(2,1)S(1)}, u32[]{:S(2)}, u32[]{:S(2)}) collective-permute-start(bf16[1024,1536]{1,0:T(8,128)(2,1)} %pad_maximum_fusion.1), channel_id=1, source_target_pairs={{0,1},{1,0},{2,3},{3,2},{4,5},{5,4},{6,7},{7,6},{8,9},{9,8},{10,11... | collective-permute-start | bytes 9437192 | tf_op jit(solution)/shard_map/ppermute | solution.py:484
  25.4 95.2 %copy-start.21 = (f32[4,256]{1,0:T(4,128)}, f32[4,256]{1,0:T(4,128)S(1)}, u32[]{:S(2)}) copy-start(f32[4,256]{1,0:T(4,128)S(1)} %get-tuple-element.328.bct_ref) | copy-start | bytes 12292
  26.2 64.8 %copy-start.35 = (bf16[512,1536]{1,0:T(8,128)(2,1)S(1)}, bf16[512,1536]{1,0:T(8,128)(2,1)}, u32[]{:S(2)}) copy-start(bf16[512,1536]{1,0:T(8,128)(2,1)} %copy-done.34) | copy-start | bytes 4718596
  92.0 28.6 %copy-start = (bf16[1024,1536]{1,0:T(8,128)(2,1)}, bf16[1024,1536]{1,0:T(8,128)(2,1)S(1)}, u32[]{:S(2)}) copy-start(bf16[1024,1536]{1,0:T(8,128)(2,1)S(1)} %fusion.5.a_ref) | copy-start | bytes 9437188
  103.6 17.1 %copy-start.10 = (f32[8,1536]{1,0:T(8,128)S(1)}, f32[8,1536]{1,0:T(8,128)}, u32[]{:S(2)}) copy-start(f32[8,1536]{1,0:T(8,128)} %copy-done.9) | copy-start | bytes 147460
  103.6 17.1 %copy-start.15 = (f32[4,1536]{1,0:T(4,128)S(1)}, f32[4,1536]{1,0:T(4,128)}, u32[]{:S(2)}) copy-start(f32[4,1536]{1,0:T(4,128)} %get-tuple-element.318.taps_ref) | copy-start | bytes 73732
  149.4 3.7 collective-permute-start.1
  164.1 36.8 %collective-permute-start.2 = (bf16[512,1536]{1,0:T(8,128)(2,1)}, bf16[512,1536]{1,0:T(8,128)(2,1)}, u32[]{:S(2)}, u32[]{:S(2)}) collective-permute-start(bf16[512,1536]{1,0:T(8,128)(2,1)} %convolution_convert_fusion.2), channel_id=1, source_target_pairs={{0,1},{1,0},{2,3},{3,2},{4,5},{5,4},{6,7},{7,6},{8,9},{9,8},{10,11... | collective-permute-start | bytes 4718600 | tf_op jit(solution)/shard_map/ppermute | solution.py:484
  165.6 293.6 %reduce-scatter.5.cloned.1.call-start = ((), (), s32[]{:S(2)}) async-start(), calls=%async_computation.8 | async-start | bytes 5013504 | tf_op jit(solution)/shard_map/reduce_scatter | solution.py:679
  165.6 43.6 %copy-start.57 = (f32[1536]{0:T(1024)S(1)}, f32[1536]{0:T(1024)}, u32[]{:S(2)}) copy-start(f32[1536]{0:T(1024)} %get-tuple-element.288) | copy-start | bytes 18436
  210.7 36.0 %collective-permute-start.3 = (bf16[512,1536]{1,0:T(8,128)(2,1)}, bf16[512,1536]{1,0:T(8,128)(2,1)}, u32[]{:S(2)}, u32[]{:S(2)}) collective-permute-start(bf16[512,1536]{1,0:T(8,128)(2,1)} %multiply_convert_fusion.2), channel_id=1, source_target_pairs={{0,1},{1,0},{2,3},{3,2},{4,5},{5,4},{6,7},{7,6},{8,9},{9,8},{10,11... | collective-permute-start | bytes 4718600 | tf_op jit(solution)/shard_map/ppermute | solution.py:484
  249.9 17.1 %copy-start.13 = (f32[8,1536]{1,0:T(8,128)S(1)}, f32[8,1536]{1,0:T(8,128)}, u32[]{:S(2)}) copy-start(f32[8,1536]{1,0:T(8,128)} %copy-done.12) | copy-start | bytes 147460
  249.9 17.1 %copy-start.17 = (f32[4,1536]{1,0:T(4,128)S(1)}, f32[4,1536]{1,0:T(4,128)}, u32[]{:S(2)}) copy-start(f32[4,1536]{1,0:T(4,128)} %get-tuple-element.317.taps_ref) | copy-start | bytes 73732
  249.9 17.1 %copy-start.23 = (f32[1,256]{1,0:T(1,128)S(1)}, f32[1,256]{1,0:T(1,128)}, u32[]{:S(2)}) copy-start(f32[1,256]{1,0:T(1,128)} %get-tuple-element.329.bcb_ref) | copy-start | bytes 3076
  298.2 4.9 collective-permute-start.4
  314.5 274.9 %reduce-scatter.7.cloned.1.call-start = ((), (), s32[]{:S(2)}) async-start(), calls=%async_computation.9 | async-start | bytes 10027008 | tf_op jit(solution)/shard_map/reduce_scatter | solution.py:676
  326.2 3.7 collective-permute-start.5
  329.9 71.7 %collective-permute-start.6 = (bf16[512,1536]{1,0:T(8,128)(2,1)}, bf16[512,1536]{1,0:T(8,128)(2,1)}, u32[]{:S(2)}, u32[]{:S(2)}) collective-permute-start(bf16[512,1536]{1,0:T(8,128)(2,1)} %get-tuple-element.204), channel_id=1, source_target_pairs={{0,1},{1,0},{2,3},{3,2},{4,5},{5,4},{6,7},{7,6},{8,9},{9,8},{10,11... | collective-permute-start | bytes 4718600 | tf_op jit(solution)/shard_map/ppermute | solution.py:484
  425.9 215.2 %reduce-scatter.11.cloned.1.call-start = ((), (), s32[]{:S(2)}) async-start(), calls=%async_computation.11 | async-start | bytes 5013504 | tf_op jit(solution)/shard_map/reduce_scatter | solution.py:711
  426.0 33.2 %collective-permute-start.7 = (bf16[512,1536]{1,0:T(8,128)(2,1)}, bf16[512,1536]{1,0:T(8,128)(2,1)}, u32[]{:S(2)}, u32[]{:S(2)}) collective-permute-start(bf16[512,1536]{1,0:T(8,128)(2,1)} %copy-done.5), channel_id=1, source_target_pairs={{0,1},{1,0},{2,3},{3,2},{4,5},{5,4},{6,7},{7,6},{8,9},{9,8},{10,11... | collective-permute-start | bytes 4718600 | tf_op jit(solution)/shard_map/ppermute | solution.py:484
  427.7 31.5 %copy-start.58 = (f32[1536]{0:T(1024)S(1)}, f32[1536]{0:T(1024)}, u32[]{:S(2)}) copy-start(f32[1536]{0:T(1024)} %get-tuple-element.288) | copy-start | bytes 18436
  472.8 32.7 %collective-permute-start.8 = (bf16[512,1536]{1,0:T(8,128)(2,1)S(1)}, bf16[512,1536]{1,0:T(8,128)(2,1)S(1)}, u32[]{:S(2)}, u32[]{:S(2)}) collective-permute-start(bf16[512,1536]{1,0:T(8,128)(2,1)S(1)} %get-tuple-element.291), channel_id=1, source_target_pairs={{0,1},{1,0},{2,3},{3,2},{4,5},{5,4},{6,7},{7,6},{8,9},{9,8},{10,11... | collective-permute-start | bytes 4718600 | tf_op jit(solution)/shard_map/ppermute | solution.py:484
  479.8 26.7 %copy-start.49 = (bf16[1024,1536]{1,0:T(8,128)(2,1)S(1)}, bf16[1024,1536]{1,0:T(8,128)(2,1)}, u32[]{:S(2)}) copy-start(bf16[1024,1536]{1,0:T(8,128)(2,1)} %copy-done.48) | copy-start | bytes 9437188
  513.4 253.4 %reduce-scatter.9.cloned.1.call-start = ((), (), s32[]{:S(2)}) async-start(), calls=%async_computation.10 | async-start | bytes 5013504 | tf_op jit(solution)/shard_map/reduce_scatter | solution.py:713
  514.7 3.9 collective-permute-start.9
  524.1 9.5 %copy-start.7 = (bf16[1536,128]{1,0:T(8,128)(2,1)S(1)}, bf16[1536,128]{1,0:T(8,128)(2,1)}, u32[]{:S(2)}) copy-start(bf16[1536,128]{1,0:T(8,128)(2,1)} %fusion.27.gather_ref) | copy-start | bytes 1179652
  524.1 9.5 %copy-start.11 = (f32[8,1536]{1,0:T(8,128)S(1)}, f32[8,1536]{1,0:T(8,128)}, u32[]{:S(2)}) copy-start(f32[8,1536]{1,0:T(8,128)} %copy-done.9) | copy-start | bytes 147460
  524.2 9.5 %copy-start.16 = (f32[4,1536]{1,0:T(4,128)S(1)}, f32[4,1536]{1,0:T(4,128)}, u32[]{:S(2)}) copy-start(f32[4,1536]{1,0:T(4,128)} %get-tuple-element.318.taps_ref) | copy-start | bytes 73732
  524.2 9.5 %copy-start.22 = (f32[4,256]{1,0:T(4,128)S(1)}, f32[4,256]{1,0:T(4,128)}, u32[]{:S(2)}) copy-start(f32[4,256]{1,0:T(4,128)} %copy-done.21) | copy-start | bytes 12292
  589.5 10.5 %copy-start.1 = (bf16[1024,1536]{1,0:T(8,128)(2,1)S(1)}, bf16[1024,1536]{1,0:T(8,128)(2,1)}, u32[]{:S(2)}) copy-start(bf16[1024,1536]{1,0:T(8,128)(2,1)} %copy-done) | copy-start | bytes 9437188
  616.1 11.7 %collective-permute-start.10 = (bf16[8,96,1536]{2,1,0:T(8,128)(2,1)}, bf16[8,96,1536]{2,1,0:T(8,128)(2,1)}, u32[]{:S(2)}, u32[]{:S(2)}) collective-permute-start(bf16[8,96,1536]{2,1,0:T(8,128)(2,1)} %dynamic-slice_bitcast_fusion.1), channel_id=1, source_target_pairs={{0,2},{2,0},{4,6},{6,4},{8,10},{10,8},{12,14},{14,12},{16,18},{18,... | collective-permute-start | bytes 7077896 | tf_op jit(solution)/shard_map/ppermute | solution.py:530
  627.3 5.1 collective-permute-start.11
  632.1 29.2 %collective-permute-start.13 = (bf16[4,96,1536]{2,1,0:T(8,128)(2,1)}, bf16[4,96,1536]{2,1,0:T(8,128)(2,1)}, u32[]{:S(2)}, u32[]{:S(2)}) collective-permute-start(bf16[4,96,1536]{2,1,0:T(8,128)(2,1)} %dynamic-slice_bitcast_fusion.3), channel_id=1, source_target_pairs={{0,4},{2,6},{4,0},{6,2},{8,12},{10,14},{12,8},{14,10},{16,20},{18,... | collective-permute-start | bytes 3538952 | tf_op jit(solution)/shard_map/ppermute | solution.py:530
  638.0 60.2 %collective-permute-start.14 = (bf16[4,96,1536]{2,1,0:T(8,128)(2,1)}, bf16[4,96,1536]{2,1,0:T(8,128)(2,1)}, u32[]{:S(2)}, u32[]{:S(2)}) collective-permute-start(bf16[4,96,1536]{2,1,0:T(8,128)(2,1)} %dynamic-slice_bitcast_fusion.2), channel_id=1, source_target_pairs={{0,4},{2,6},{4,0},{6,2},{8,12},{10,14},{12,8},{14,10},{16,20},{18,... | collective-permute-start | bytes 3538952 | tf_op jit(solution)/shard_map/ppermute | solution.py:530
  639.8 61.1 %collective-permute-start.12 = (bf16[512,1536]{1,0:T(8,128)(2,1)}, bf16[512,1536]{1,0:T(8,128)(2,1)}, u32[]{:S(2)}, u32[]{:S(2)}) collective-permute-start(bf16[512,1536]{1,0:T(8,128)(2,1)} %shard_map.269), channel_id=1, source_target_pairs={{0,1},{1,0},{2,3},{3,2},{4,5},{5,4},{6,7},{7,6},{8,9},{9,8},{10,11... | collective-permute-start | bytes 4718600 | tf_op jit(solution)/shard_map/ppermute | solution.py:484
  648.1 13.2 %copy-start.39 = (bf16[8,96,1536]{2,1,0:T(8,128)(2,1)S(1)}, bf16[8,96,1536]{2,1,0:T(8,128)(2,1)}, u32[]{:S(2)}) copy-start(bf16[8,96,1536]{2,1,0:T(8,128)(2,1)} %copy-done.38) | copy-start | bytes 7077892
  658.2 42.6 %copy-start.2 = (f32[512,1536]{1,0:T(8,128)}, f32[512,1536]{1,0:T(8,128)S(1)}, u32[]{:S(2)}) copy-start(f32[512,1536]{1,0:T(8,128)S(1)} %shard_map.272) | copy-start | bytes 9437188
  658.3 40.0 %copy-start.41 = (bf16[8,96,1536]{2,1,0:T(8,128)(2,1)S(1)}, bf16[8,96,1536]{2,1,0:T(8,128)(2,1)}, u32[]{:S(2)}) copy-start(bf16[8,96,1536]{2,1,0:T(8,128)(2,1)} %copy-done.40) | copy-start | bytes 7077892
  658.3 42.6 %copy-start.32 = (bf16[512,1536]{1,0:T(8,128)(2,1)S(1)}, bf16[512,1536]{1,0:T(8,128)(2,1)}, u32[]{:S(2)}) copy-start(bf16[512,1536]{1,0:T(8,128)(2,1)} %param.39) | copy-start | bytes 4718596
  658.3 42.6 %copy-start.56 = (f32[1536]{0:T(1024)S(1)}, f32[1536]{0:T(1024)}, u32[]{:S(2)}) copy-start(f32[1536]{0:T(1024)} %copy-done.55) | copy-start | bytes 18436
  658.3 42.6 %copy-start.68 = (f32[512]{0:T(512)S(1)}, f32[512]{0:T(512)}, u32[]{:S(2)}) copy-start(f32[512]{0:T(512)} %copy-done.67) | copy-start | bytes 6148
  662.9 41.4 %copy-start.44 = (bf16[4,96,1536]{2,1,0:T(8,128)(2,1)}, bf16[4,96,1536]{2,1,0:T(8,128)(2,1)S(1)}, u32[]{:S(2)}) copy-start(bf16[4,96,1536]{2,1,0:T(8,128)(2,1)S(1)} %fusion.14) | copy-start | bytes 3538948
  663.7 52.5 %collective-permute-start.20 = (bf16[1,96,1536]{2,1,0:T(8,128)(2,1)}, bf16[1,96,1536]{2,1,0:T(8,128)(2,1)}, u32[]{:S(2)}, u32[]{:S(2)}) collective-permute-start(bf16[1,96,1536]{2,1,0:T(8,128)(2,1)} %constant_dynamic-slice_fusion), channel_id=1, source_target_pairs={{0,8},{2,10},{4,12},{6,14},{8,16},{10,18},{12,20},{14,22},{16,24},... | collective-permute-start | bytes 884744 | tf_op jit(solution)/shard_map/ppermute | solution.py:530
  704.3 15.1 %copy-start.33 = (bf16[512,1536]{1,0:T(8,128)(2,1)S(1)}, bf16[512,1536]{1,0:T(8,128)(2,1)}, u32[]{:S(2)}) copy-start(bf16[512,1536]{1,0:T(8,128)(2,1)} %param.39) | copy-start | bytes 4718596
  704.8 4.9 collective-permute-start.15
  707.1 9.1 %collective-permute-start.16 = (bf16[1,96,1536]{2,1,0:T(8,128)(2,1)S(1)}, bf16[1,96,1536]{2,1,0:T(8,128)(2,1)S(1)}, u32[]{:S(2)}, u32[]{:S(2)}) collective-permute-start(bf16[1,96,1536]{2,1,0:T(8,128)(2,1)S(1)} %constant_dynamic-slice_fusion.1), channel_id=1, source_target_pairs={{0,8},{2,10},{4,12},{6,14},{8,16},{10,18},{12,20},{14,22},{16,24},... | collective-permute-start | bytes 884744 | tf_op jit(solution)/shard_map/ppermute | solution.py:530
  716.2 1.4 collective-permute-start.17
  717.3 21.9 %collective-permute-start.21 = (bf16[1,96,1536]{2,1,0:T(8,128)(2,1)S(1)}, bf16[1,96,1536]{2,1,0:T(8,128)(2,1)S(1)}, u32[]{:S(2)}, u32[]{:S(2)}) collective-permute-start(bf16[1,96,1536]{2,1,0:T(8,128)(2,1)S(1)} %add_convert_fusion.5), channel_id=1, source_target_pairs={{0,8},{2,10},{4,12},{6,14},{8,16},{10,18},{12,20},{14,22},{16,24},... | collective-permute-start | bytes 884744 | tf_op jit(solution)/shard_map/ppermute | solution.py:530
  717.6 21.6 %copy-start.45 = (bf16[4,96,1536]{2,1,0:T(8,128)(2,1)S(1)}, bf16[4,96,1536]{2,1,0:T(8,128)(2,1)}, u32[]{:S(2)}) copy-start(bf16[4,96,1536]{2,1,0:T(8,128)(2,1)} %copy-done.44) | copy-start | bytes 3538948
  717.6 23.8 %copy-start.43 = (bf16[4,96,1536]{2,1,0:T(8,128)(2,1)S(1)}, bf16[4,96,1536]{2,1,0:T(8,128)(2,1)}, u32[]{:S(2)}) copy-start(bf16[4,96,1536]{2,1,0:T(8,128)(2,1)} %fusion.13) | copy-start | bytes 3538948
  717.6 21.5 %collective-permute-start.18 = (f32[2,8,1920]{2,1,0:T(8,128)S(1)}, f32[2,8,1920]{2,1,0:T(8,128)S(1)}, u32[]{:S(2)}, u32[]{:S(2)}) collective-permute-start(f32[2,8,1920]{2,1,0:T(8,128)S(1)} %add.419), channel_id=1, source_target_pairs={{0,16},{2,18},{4,20},{6,22},{8,24},{10,26},{12,28},{14,30},{16,0},... | collective-permute-start | bytes 368648 | tf_op jit(solution)/shard_map/ppermute | solution.py:539
  739.1 17.6 %collective-permute-start.19 = (f32[2,8,1920]{2,1,0:T(8,128)S(1)}, f32[2,8,1920]{2,1,0:T(8,128)S(1)}, u32[]{:S(2)}, u32[]{:S(2)}) collective-permute-start(f32[2,8,1920]{2,1,0:T(8,128)S(1)} %add.420), channel_id=1, source_target_pairs={{0,8},{2,10},{4,12},{6,14},{8,0},{10,2},{12,4},{14,6},{16,24},{18,... | collective-permute-start | bytes 368648 | tf_op jit(solution)/shard_map/ppermute | solution.py:539
  739.3 40.1 %copy-start.53 = (bf16[1,96,2,1536]{3,1,2,0:T(8,128)(2,1)S(1)}, bf16[1,96,2,1536]{3,1,2,0:T(8,128)(2,1)}, u32[]{:S(2)}) copy-start(bf16[1,96,2,1536]{3,1,2,0:T(8,128)(2,1)} %copy.61) | copy-start | bytes 1769476
  739.3 17.4 %collective-permute-start.22 = (bf16[1,96,1536]{2,1,0:T(8,128)(2,1)S(1)}, bf16[1,96,1536]{2,1,0:T(8,128)(2,1)S(1)}, u32[]{:S(2)}, u32[]{:S(2)}) collective-permute-start(bf16[1,96,1536]{2,1,0:T(8,128)(2,1)S(1)} %add_convert_fusion.4), channel_id=1, source_target_pairs={{0,8},{2,10},{4,12},{6,14},{8,16},{10,18},{12,20},{14,22},{16,24},... | collective-permute-start | bytes 884744 | tf_op jit(solution)/shard_map/ppermute | solution.py:530
  741.4 15.5 %collective-permute-start.24 = (bf16[1,96,1536]{2,1,0:T(8,128)(2,1)S(1)}, bf16[1,96,1536]{2,1,0:T(8,128)(2,1)S(1)}, u32[]{:S(2)}, u32[]{:S(2)}) collective-permute-start(bf16[1,96,1536]{2,1,0:T(8,128)(2,1)S(1)} %add_convert_fusion.2), channel_id=1, source_target_pairs={{0,8},{2,10},{4,12},{6,14},{8,16},{10,18},{12,20},{14,22},{16,24},... | collective-permute-start | bytes 884744 | tf_op jit(solution)/shard_map/ppermute | solution.py:530
  756.8 4.9 collective-permute-start.23
  768.7 4.7 collective-permute-start.26
  770.1 4.6 collective-permute-start.27
  770.8 8.5 %collective-permute-start.25 = (bf16[1,96,1536]{2,1,0:T(8,128)(2,1)S(1)}, bf16[1,96,1536]{2,1,0:T(8,128)(2,1)S(1)}, u32[]{:S(2)}, u32[]{:S(2)}) collective-permute-start(bf16[1,96,1536]{2,1,0:T(8,128)(2,1)S(1)} %add_convert_fusion.1), channel_id=1, source_target_pairs={{0,8},{2,10},{4,12},{6,14},{8,16},{10,18},{12,20},{14,22},{16,24},... | collective-permute-start | bytes 884744 | tf_op jit(solution)/shard_map/ppermute | solution.py:530
  (58 other events, 224.5 us)
Sparse Core Ops, SparseCore 0:
  12.1 91.3 all-gather.4
  106.4 51.5 all-gather.6
  160.3 87.2 all-gather.8
  249.7 51.5 all-gather.10
  314.7 73.5 reduce-scatter.4
  426.0 110.6 reduce-scatter.6
  540.6 75.2 reduce-scatter.10
  643.4 97.3 reduce-scatter.8
